TPU v7x, 32 devices: a whole 2x2x4 slice. The times are simulated.
32 devices in a mesh: dp: 8 (over z, y), tensor: 4 (over x, core).
Axes of the slice: x: 2, y: 2, z: 4, core: 2. Of those that a mesh axis runs over, the one named last changes fastest.
Arguments:
- tokens: bfloat16 [24576, 2048], P(('dp', 'tensor')), may hold values from -6 to 6
- cotangent: bfloat16 [24576, 2048], P(('dp', 'tensor'))
- doc_lengths: int32 [8, 4], P('dp'), may hold values from 1 to 1536, 3072 in all within a row
- mix_in: float32 [3, 2048, 2048], P(None, 'dp', 'tensor')
- mix_out: float32 [2048, 2048], P('tensor', 'dp')
- ffn_in: float32 [2, 2048, 5632], P(None, 'dp', 'tensor')
- ffn_out: float32 [5632, 2048], P('tensor', 'dp')
- gains: float32 [2, 2048], replicated, may hold values from 0.5 to 1.5
- mix_in_m: float32 [3, 2048, 2048], P(None, 'dp', 'tensor'), may hold values from -20 to 20
- mix_out_m: float32 [2048, 2048], P('tensor', 'dp'), may hold values from -40 to 40
- ffn_in_m: float32 [2, 2048, 5632], P(None, 'dp', 'tensor'), may hold values from -56 to 56
- ffn_out_m: float32 [5632, 2048], P('tensor', 'dp'), may hold values from -64 to 64
- gains_m: float32 [2, 2048], replicated, may hold values from -112 to 112
- mix_in_v: float32 [3, 2048, 2048], P(None, 'dp', 'tensor'), may hold values from 0.98304 to 3.93216
- mix_out_v: float32 [2048, 2048], P('tensor', 'dp'), may hold values from 3.93216 to 15.72864
- ffn_in_v: float32 [2, 2048, 5632], P(None, 'dp', 'tensor'), may hold values from 6.144 to 24.576
- ffn_out_v: float32 [5632, 2048], P('tensor', 'dp'), may hold values from 8.84736 to 35.38944
- gains_v: float32 [2, 2048], replicated, may hold values from 24.576 to 98.304
Outputs:
- mixed: bfloat16 [24576, 2048], P(('dp', 'tensor'))
- input_grad: float32 [24576, 2048], P(('dp', 'tensor'))
- mix_in_next: float32 [3, 2048, 2048], P(None, 'dp', 'tensor')
- mix_out_next: float32 [2048, 2048], P('tensor', 'dp')
- ffn_in_next: float32 [2, 2048, 5632], P(None, 'dp', 'tensor')
- ffn_out_next: float32 [5632, 2048], P('tensor', 'dp')
- gains_next: float32 [2, 2048], replicated
- mix_in_m_next: float32 [3, 2048, 2048], P(None, 'dp', 'tensor')
- mix_out_m_next: float32 [2048, 2048], P('tensor', 'dp')
- ffn_in_m_next: float32 [2, 2048, 5632], P(None, 'dp', 'tensor')
- ffn_out_m_next: float32 [5632, 2048], P('tensor', 'dp')
- gains_m_next: float32 [2, 2048], replicated
- mix_in_v_next: float32 [3, 2048, 2048], P(None, 'dp', 'tensor')
- mix_out_v_next: float32 [2048, 2048], P('tensor', 'dp')
- ffn_in_v_next: float32 [2, 2048, 5632], P(None, 'dp', 'tensor')
- ffn_out_v_next: float32 [5632, 2048], P('tensor', 'dp')
- gains_v_next: float32 [2, 2048], replicated
- mix_in_copy: bfloat16 [3, 2048, 2048], P(None, 'dp', 'tensor')
- mix_out_copy: bfloat16 [2048, 2048], P('tensor', 'dp')
- ffn_in_copy: bfloat16 [2, 2048, 5632], P(None, 'dp', 'tensor')
- ffn_out_copy: bfloat16 [5632, 2048], P('tensor', 'dp')
- layer_norms: float32 [2, 9], replicated
Inputs may be any that keep to these rules, and one draw needn't show every extreme that they name: `doc_lengths`: each row holds the lengths of one group's 4 sequences, which together fill its 3072 rows; in every row the longest is exactly 1536.
All inputs are finite; a program needn't handle non-finite values.
Results may differ from a plain program's by a relative error of at most 0.022.
Values may be sent and summed in bfloat16 or wider, within the bound.
No kernel may reach another device: no remote copies, remote signals or barrier semaphores. Data moves between devices by JAX's collectives and lax.ppermute only.
A program may use at most 384 MiB of HBM per device.

v0:
```python
import jax
import jax.numpy as jnp
from jax import lax
from jax.sharding import PartitionSpec as P

STEP = 10


LOWER_BOUND = 0.8
RMS_EPSILON = 1e-06
BETA_ONE = 0.9
BETA_TWO = 0.999
ADAM_EPSILON = 1e-06
WEIGHT_DECAY = 0.01
LEARN_RATE = 0.5
NORM_EPSILON = 1e-12


def rms_forward(values, gain):
    scaling = lax.rsqrt(jnp.mean(values * values, axis=-1, keepdims=True) + RMS_EPSILON)
    unit_rows = values * scaling
    return (unit_rows * gain, unit_rows, scaling)


def rms_backward(d_normed, unit_rows, scaling, gain):
    d_unit = d_normed * gain
    d_values = scaling * (d_unit - unit_rows * jnp.mean(d_unit * unit_rows, axis=-1, keepdims=True))
    return (d_values, jnp.sum(d_normed * unit_rows, axis=0))


def start_keep(lengths, rows):
    offsets = jnp.cumsum(lengths) - lengths
    places = jnp.arange(rows, dtype=jnp.int32)
    starts = jnp.any(places[:, None] == offsets[None, :], axis=1)
    return jnp.where(starts, 0.0, 1.0).astype(jnp.float32)[:, None]


def combine(earlier, later):
    return (earlier[0] * later[0], later[0] * earlier[1] + later[1])


def linear_scan(rates, driving):
    return lax.associative_scan(combine, (rates, driving), axis=0)[1]


def silu_slope(values):
    sigma = jax.nn.sigmoid(values)
    return sigma * (1.0 + values * (1.0 - sigma))


def adam_moments(grad, weight, first, second, decay_rate):
    first_next = BETA_ONE * first + (1.0 - BETA_ONE) * grad
    second_next = BETA_TWO * second + (1.0 - BETA_TWO) * grad * grad
    update = (
        first_next
        / (1.0 - BETA_ONE**STEP)
        / (jnp.sqrt(second_next / (1.0 - BETA_TWO**STEP)) + ADAM_EPSILON)
        + decay_rate * weight
    )
    return (first_next, second_next, update)


def per_device(
    tokens,
    cotangent,
    doc_lengths,
    mix_in,
    mix_out,
    ffn_in,
    ffn_out,
    gains,
    mix_in_m,
    mix_out_m,
    ffn_in_m,
    ffn_out_m,
    gains_m,
    mix_in_v,
    mix_out_v,
    ffn_in_v,
    ffn_out_v,
    gains_v,
):
    w_mix_in, w_mix_out, w_ffn_in, w_ffn_out = (
        lax.all_gather(mix_in.astype(jnp.bfloat16), "dp", axis=1, tiled=True),
        lax.all_gather(mix_out.astype(jnp.bfloat16), "dp", axis=1, tiled=True),
        lax.all_gather(ffn_in.astype(jnp.bfloat16), "dp", axis=1, tiled=True),
        lax.all_gather(ffn_out.astype(jnp.bfloat16), "dp", axis=1, tiled=True),
    )
    inputs = tokens.astype(jnp.float32)
    normed_one, unit_one, scale_one = rms_forward(inputs, gains[0])
    whole_one = lax.all_gather(normed_one.astype(jnp.bfloat16), "tensor", axis=0, tiled=True)
    rows_all = whole_one.shape[0]
    pre_all = jnp.einsum("rd,kdc->krc", whole_one, w_mix_in, preferred_element_type=jnp.float32)
    pre_input = pre_all[0]
    pre_forget = pre_all[1]
    pre_gate = pre_all[2]
    keeping = start_keep(doc_lengths[0], rows_all)
    forget_sig = jax.nn.sigmoid(pre_forget)
    rates = keeping * (LOWER_BOUND + (1.0 - LOWER_BOUND) * forget_sig)
    act_input = jax.nn.silu(pre_input)
    states = linear_scan(rates, (1.0 - rates) * act_input)
    act_gate = jax.nn.silu(pre_gate)
    gated_low = (states * act_gate).astype(jnp.bfloat16)
    middle = inputs + lax.psum_scatter(
        jnp.dot(gated_low, w_mix_out, preferred_element_type=jnp.float32),
        "tensor",
        scatter_dimension=0,
        tiled=True,
    )
    normed_two, unit_two, scale_two = rms_forward(middle, gains[1])
    normed_two_low = normed_two.astype(jnp.bfloat16)
    whole_two = lax.all_gather(normed_two_low, "tensor", axis=0, tiled=True)
    gate_up = jnp.einsum("rd,kdf->krf", whole_two, w_ffn_in, preferred_element_type=jnp.float32)
    gate_proj = gate_up[0]
    up_proj = gate_up[1]
    act_proj = jax.nn.silu(gate_proj)
    hidden_low = (act_proj * up_proj).astype(jnp.bfloat16)
    mixed = (
        middle
        + lax.psum_scatter(
            jnp.dot(hidden_low, w_ffn_out, preferred_element_type=jnp.float32).astype(jnp.bfloat16),
            "tensor",
            scatter_dimension=0,
            tiled=True,
        ).astype(jnp.float32)
    ).astype(jnp.bfloat16)
    portion = lax.all_gather(cotangent, "tensor", axis=0, tiled=True)
    grad_down = jnp.einsum("rf,rd->fd", hidden_low, portion, preferred_element_type=jnp.float32)
    new_rows = jnp.einsum("rd,fd->rf", portion, w_ffn_out, preferred_element_type=jnp.float32)
    grad_hidden = new_rows
    g_ffn_out = grad_down
    d_gate = grad_hidden * up_proj * silu_slope(gate_proj)
    d_up = grad_hidden * act_proj
    d_gate_up = jnp.stack([d_gate, d_up]).astype(jnp.bfloat16)
    rows_block = d_gate_up
    d_normed_two = lax.psum_scatter(
        jnp.einsum("krf,kdf->rd", rows_block, w_ffn_in, preferred_element_type=jnp.float32),
        "tensor",
        scatter_dimension=0,
        tiled=True,
    )
    g_ffn_in = jnp.einsum("rd,krf->kdf", whole_two, d_gate_up, preferred_element_type=jnp.float32)
    d_middle_norm, gain_grad_two = rms_backward(d_normed_two, unit_two, scale_two, gains[1])
    d_middle = cotangent.astype(jnp.float32) + d_middle_norm
    channels = w_mix_out.shape[0]
    portion = lax.all_gather(d_middle.astype(jnp.bfloat16), "tensor", axis=0, tiled=True)
    grad_out = jnp.einsum("rc,rd->cd", gated_low, portion, preferred_element_type=jnp.float32)
    new_rows = jnp.einsum("rd,cd->rc", portion, w_mix_out, preferred_element_type=jnp.float32)
    g_mix_out = grad_out
    d_states = new_rows * act_gate
    d_pre_gate = new_rows * states * silu_slope(pre_gate)
    rates_next = jnp.concatenate([rates[1:], jnp.zeros((1, channels), jnp.float32)], axis=0)
    carried = jnp.flip(linear_scan(jnp.flip(rates_next, 0), jnp.flip(d_states, 0)), 0)
    states_prev = jnp.concatenate([jnp.zeros((1, channels), jnp.float32), states[:-1]], axis=0)
    d_rates = carried * states_prev - carried * act_input
    d_pre_input = carried * (1.0 - rates) * silu_slope(pre_input)
    d_pre_forget = d_rates * keeping * (1.0 - LOWER_BOUND) * forget_sig * (1.0 - forget_sig)
    d_pre_all = jnp.stack([d_pre_input, d_pre_forget, d_pre_gate]).astype(jnp.bfloat16)
    g_mix_in = jnp.einsum("rd,krc->kdc", whole_one, d_pre_all, preferred_element_type=jnp.float32)
    rows_block = d_pre_all
    d_normed_one = lax.psum_scatter(
        jnp.einsum("krc,kdc->rd", rows_block, w_mix_in, preferred_element_type=jnp.float32).astype(
            jnp.bfloat16
        ),
        "tensor",
        scatter_dimension=0,
        tiled=True,
    ).astype(jnp.float32)
    d_input_norm, gain_grad_one = rms_backward(d_normed_one, unit_one, scale_one, gains[0])
    input_grad = d_middle + d_input_norm
    g_mix_in, g_mix_out, g_ffn_in, g_ffn_out = (
        lax.psum_scatter(
            g_mix_in.astype(jnp.bfloat16), "dp", scatter_dimension=1, tiled=True
        ).astype(jnp.float32),
        lax.psum_scatter(
            g_mix_out.astype(jnp.bfloat16), "dp", scatter_dimension=1, tiled=True
        ).astype(jnp.float32),
        lax.psum_scatter(
            g_ffn_in.astype(jnp.bfloat16), "dp", scatter_dimension=1, tiled=True
        ).astype(jnp.float32),
        lax.psum_scatter(
            g_ffn_out.astype(jnp.bfloat16), "dp", scatter_dimension=1, tiled=True
        ).astype(jnp.float32),
    )
    mi_first, mi_second, mi_update = adam_moments(
        g_mix_in, mix_in, mix_in_m, mix_in_v, WEIGHT_DECAY
    )
    mo_first, mo_second, mo_update = adam_moments(
        g_mix_out, mix_out, mix_out_m, mix_out_v, WEIGHT_DECAY
    )
    fi_first, fi_second, fi_update = adam_moments(
        g_ffn_in, ffn_in, ffn_in_m, ffn_in_v, WEIGHT_DECAY
    )
    fo_first, fo_second, fo_update = adam_moments(
        g_ffn_out, ffn_out, ffn_out_m, ffn_out_v, WEIGHT_DECAY
    )
    weight_part = jnp.concatenate(
        [
            jnp.sum(mix_in * mix_in, axis=(1, 2)),
            jnp.sum(mix_out * mix_out)[None],
            jnp.sum(ffn_in * ffn_in, axis=(1, 2)),
            jnp.sum(ffn_out * ffn_out)[None],
        ]
    )
    update_part = jnp.concatenate(
        [
            jnp.sum(mi_update * mi_update, axis=(1, 2)),
            jnp.sum(mo_update * mo_update)[None],
            jnp.sum(fi_update * fi_update, axis=(1, 2)),
            jnp.sum(fo_update * fo_update)[None],
        ]
    )
    squares, gain_grads = lax.psum(
        (jnp.stack([weight_part, update_part]), jnp.stack([gain_grad_one, gain_grad_two])),
        ("dp", "tensor"),
    )
    gn_first, gn_second, gn_update = adam_moments(gain_grads, gains, gains_m, gains_v, 0.0)
    weight_sq = jnp.concatenate([squares[0], jnp.sum(gains * gains, axis=1)])
    update_sq = jnp.concatenate([squares[1], jnp.sum(gn_update * gn_update, axis=1)])
    trust = jnp.sqrt(weight_sq) / jnp.sqrt(update_sq + NORM_EPSILON)
    mix_in_next = mix_in - LEARN_RATE * trust[0:3][:, None, None] * mi_update
    mix_out_next = mix_out - LEARN_RATE * trust[3] * mo_update
    ffn_in_next = ffn_in - LEARN_RATE * trust[4:6][:, None, None] * fi_update
    ffn_out_next = ffn_out - LEARN_RATE * trust[6] * fo_update
    gains_next = gains - LEARN_RATE * trust[7:9][:, None] * gn_update
    layer_norms = jnp.stack([jnp.sqrt(weight_sq), jnp.sqrt(update_sq)])
    return (
        mixed,
        input_grad,
        mix_in_next,
        mix_out_next,
        ffn_in_next,
        ffn_out_next,
        gains_next,
        mi_first,
        mo_first,
        fi_first,
        fo_first,
        gn_first,
        mi_second,
        mo_second,
        fi_second,
        fo_second,
        gn_second,
        mix_in_next.astype(jnp.bfloat16),
        mix_out_next.astype(jnp.bfloat16),
        ffn_in_next.astype(jnp.bfloat16),
        ffn_out_next.astype(jnp.bfloat16),
        layer_norms,
    )


def solution(mesh):
    in_specs = (
        P(("dp", "tensor"), None),
        P(("dp", "tensor"), None),
        P("dp", None),
        P(None, "dp", "tensor"),
        P("tensor", "dp"),
        P(None, "dp", "tensor"),
        P("tensor", "dp"),
        P(),
        P(None, "dp", "tensor"),
        P("tensor", "dp"),
        P(None, "dp", "tensor"),
        P("tensor", "dp"),
        P(),
        P(None, "dp", "tensor"),
        P("tensor", "dp"),
        P(None, "dp", "tensor"),
        P("tensor", "dp"),
        P(),
    )
    out_specs = (
        P(("dp", "tensor"), None),
        P(("dp", "tensor"), None),
        P(None, "dp", "tensor"),
        P("tensor", "dp"),
        P(None, "dp", "tensor"),
        P("tensor", "dp"),
        P(),
        P(None, "dp", "tensor"),
        P("tensor", "dp"),
        P(None, "dp", "tensor"),
        P("tensor", "dp"),
        P(),
        P(None, "dp", "tensor"),
        P("tensor", "dp"),
        P(None, "dp", "tensor"),
        P("tensor", "dp"),
        P(),
        P(None, "dp", "tensor"),
        P("tensor", "dp"),
        P(None, "dp", "tensor"),
        P("tensor", "dp"),
        P(),
    )
    return jax.shard_map(
        per_device, mesh=mesh, in_specs=in_specs, out_specs=out_specs, check_vma=False
    )
```

profile of v0, /device:TPU:0, one launch (start us, length us, event | category | flops | bytes accessed | tf_op | source)
XLA Modules:
  0.0 2580.9 jit_solution(13305422216790063314)
XLA Ops:
  16.5 96.4 %all-gather.11.cloned.1.call-done = bf16[3,2048,512]{2,1,0:T(8,128)(2,1)} async-done(((bf16[3,256,512]{2,1,0:T(8,128)(2,1)}), bf16[3,2048,512]{2,1,0:T(8,128)(2,1)}) %all-gather.11.cloned.1.call-update) | async-done | bytes 6291472 | tf_op jit(solution)/shard_map/all_gather | solution.py:84
  112.8 82.4 %all-gather.9.cloned.1.call-done = bf16[3072,2048]{1,0:T(8,128)(2,1)} async-done(((bf16[768,2048]{1,0:T(8,128)(2,1)}), bf16[3072,2048]{1,0:T(8,128)(2,1)}) %all-gather.9.cloned.1.call-update) | async-done | bytes 12582928 | tf_op jit(solution)/shard_map/all_gather | solution.py:91
  195.3 24.0 fusion.16
  278.2 16.3 slice.678
  592.1 18.4 pad.156
  610.5 18.8 pad.157
  658.4 175.6 %reduce-scatter.9.cloned.1.call-done = f32[768,2048]{1,0:T(8,128)} async-done(((f32[3072,2048]{1,0:T(8,128)}), f32[768,2048]{1,0:T(8,128)}) %reduce-scatter.9.cloned.1.call-update) | async-done | bytes 6291472 | tf_op jit(solution)/shard_map/reduce_scatter | solution.py:104
  845.8 154.7 %all-gather.17.cloned.1.call-done = bf16[2,2048,1408]{2,1,0:T(8,128)(2,1)} async-done(((bf16[2,256,1408]{2,1,0:T(8,128)(2,1)}), bf16[2,2048,1408]{2,1,0:T(8,128)(2,1)}) %all-gather.17.cloned.1.call-update) | async-done | bytes 11534352 | tf_op jit(solution)/shard_map/all_gather | solution.py:86
  1000.6 81.8 %all-gather.15.cloned.1.call-done = bf16[3072,2048]{1,0:T(8,128)(2,1)} async-done(((bf16[768,2048]{1,0:T(8,128)(2,1)}), bf16[3072,2048]{1,0:T(8,128)(2,1)}) %all-gather.15.cloned.1.call-update) | async-done | bytes 12582928 | tf_op jit(solution)/shard_map/all_gather | solution.py:112
  1082.4 44.7 %convolution_bitcast_fusion = f32[2,3072,1408]{2,1,0:T(8,128)} fusion(bf16[2,2048,1408]{2,1,0:T(8,128)(2,1)} %all-gather.17.cloned.1.call-done, bf16[3072,2048]{1,0:T(8,128)(2,1)} %all-gather.15.cloned.1.call-done), kind=kOutput, calls=%fused_computation.1 | convolution fusion | flops 35433480192 | bytes 58720256 | tf_op jit(solution)/shard_map/rd,kdf->krf/dot_general | solution.py:113
  1127.0 51.8 %all-gather.19.cloned.1.call-done = bf16[1408,2048]{1,0:T(8,128)(2,1)} async-done(((bf16[1408,256]{1,0:T(8,128)(2,1)}), bf16[1408,2048]{1,0:T(8,128)(2,1)}) %all-gather.19.cloned.1.call-update) | async-done | bytes 5767184 | tf_op jit(solution)/shard_map/all_gather | solution.py:87
  1178.8 82.0 %all-gather.21.cloned.1.call-done = bf16[3072,2048]{1,0:T(8,128)(2,1)} async-done(((bf16[768,2048]{1,0:T(8,128)(2,1)}), bf16[3072,2048]{1,0:T(8,128)(2,1)}) %all-gather.21.cloned.1.call-update) | async-done | bytes 12582928 | tf_op jit(solution)/shard_map/all_gather | solution.py:127
  1260.8 35.8 %fusion.15 = (bf16[1,3072,1408]{2,1,0:T(8,128)(2,1)}, bf16[1,3072,1408]{2,1,0:T(8,128)(2,1)}, bf16[3072,1408]{1,0:T(8,128)(2,1)}) fusion(f32[2,3072,1408]{2,1,0:T(8,128)} %convolution_bitcast_fusion, bf16[3072,2048]{1,0:T(8,128)(2,1)} %all-gather.21.cloned.1.call-done, bf16[1408,2048]{1,0:T(8,128)(2,1)} %all-gather.19.cloned.1.call-done), kind=kOutput, calls=%fused_computation.29 | convolution fusion | flops 17781620736 | bytes 78905344 | tf_op jit(solution)/shard_map/rd,fd->rf/dot_general | solution.py:129
  1296.5 45.0 %convolution_bitcast_fusion.1 = f32[3072,2048]{1,0:T(8,128)} fusion(bf16[2,2048,1408]{2,1,0:T(8,128)(2,1)} %all-gather.17.cloned.1.call-done, bf16[1,3072,1408]{2,1,0:T(8,128)(2,1)} %get-tuple-element.109, bf16[1,3072,1408]{2,1,0:T(8,128)(2,1)} %get-tuple-element.108), kind=kOutput, calls=%fused_computation.10 | convolution fusion | flops 35442130944 | bytes 54001664 | tf_op jit(solution)/shard_map/krf,kdf->rd/dot_general | solution.py:137
  1341.6 180.5 %reduce-scatter.13.cloned.1.call-done = f32[768,2048]{1,0:T(8,128)} async-done(((f32[3072,2048]{1,0:T(8,128)}), f32[768,2048]{1,0:T(8,128)}) %reduce-scatter.13.cloned.1.call-update) | async-done | bytes 6291472 | tf_op jit(solution)/shard_map/reduce_scatter | solution.py:136
  1533.6 24.4 convolution_convert_fusion.1
  1558.0 46.2 %convert_bitcast_fusion = bf16[2,2048,1408]{1,2,0:T(8,128)(2,1)} fusion(bf16[3072,2048]{1,0:T(8,128)(2,1)} %all-gather.15.cloned.1.call-done, bf16[1,3072,1408]{2,1,0:T(8,128)(2,1)} %get-tuple-element.109, bf16[1,3072,1408]{2,1,0:T(8,128)(2,1)} %get-tuple-element.108), kind=kOutput, calls=%fused_computation.18 | convolution fusion | flops 35447898112 | bytes 41418752 | tf_op jit(solution)/shard_map/rd,krf->kdf/dot_general | solution.py:142
  1611.2 16.4 slice.685
  1658.2 25.5 slice.686
  1683.6 24.7 slice.695
  1732.9 17.7 fusion.49
  1797.4 24.7 slice.692
  2010.3 25.5 slice.774
  2083.0 18.6 pad.179
  2110.5 48.6 %rev.6 = f32[3072,512]{1,0:T(8,128)} reverse(f32[3072,512]{1,0:T(8,128)} %add.526), dimensions={0} | reverse | bytes 12582912 | tf_op jit(solution)/shard_map/jit(_flip)/rev | solution.py:153
  2184.6 25.0 convert_bitcast_fusion.1
  2209.7 25.4 bitcast_convert_fusion
  2235.1 25.4 convolution_convert_fusion
  2304.5 54.8 %reduce-scatter.17.cloned.1.call-done = bf16[3,256,512]{1,2,0:T(8,128)(2,1)} async-done(((bf16[3,2048,512]{1,2,0:T(8,128)(2,1)}), bf16[3,256,512]{1,2,0:T(8,128)(2,1)}) %reduce-scatter.17.cloned.1.call-update) | async-done | bytes 786448 | tf_op jit(solution)/shard_map/reduce_scatter | solution.py:172
  2368.9 91.1 %reduce-scatter.15.cloned.1.call-done = bf16[768,2048]{1,0:T(8,128)(2,1)} async-done(((bf16[3072,2048]{1,0:T(8,128)(2,1)}), bf16[768,2048]{1,0:T(8,128)(2,1)}) %reduce-scatter.15.cloned.1.call-update) | async-done | bytes 3145744 | tf_op jit(solution)/shard_map/reduce_scatter | solution.py:161
  2466.9 39.7 %all-reduce.46 = (f32[2,7]{1,0:T(2,128)S(1)}, f32[2,2048]{1,0:T(2,128)S(1)}) all-reduce(f32[2,7]{1,0:T(2,128)S(1)} %pad_maximum_fusion.31, f32[2,2048]{1,0:T(2,128)S(1)} %pad_maximum_fusion.26), channel_id=1, replica_groups=mesh['dp'=8,'tensor'=4] {'dp','tensor'}, use_global_device_ids=true, to_apply=%region_22.23 | all-reduce | flops 4110 | bytes 32880 | tf_op jit(solution)/shard_map/psum | solution.py:213
  2540.5 21.8 reduce-scatter.11.cloned.1.call-done
  (547 shorter events, 900.1 us)
Async XLA Ops:
  7.2 105.6 %all-gather.11.cloned.1.call-start = ((), (), s32[]{:S(2)}) async-start(), calls=%async_computation.9 | async-start | bytes 7077888 | tf_op jit(solution)/shard_map/all_gather | solution.py:84
  11.0 184.3 %all-gather.9.cloned.1.call-start = ((), (), s32[]{:S(2)}) async-start(), calls=%async_computation.8 | async-start | bytes 15728640 | tf_op jit(solution)/shard_map/all_gather | solution.py:91
  11.8 826.0 %copy-start.30 = (f32[1,2048]{1,0:T(1,128)}, f32[1,2048]{1,0:T(1,128)S(1)}, u32[]{:S(2)}) copy-start(f32[1,2048]{1,0:T(1,128)S(1)} %get-tuple-element.156) | copy-start | bytes 24580
  14.3 625.3 %all-gather.13.cloned.1.call-start = ((), (), s32[]{:S(2)}) async-start(), calls=%async_computation.10 | async-start | bytes 2359296 | tf_op jit(solution)/shard_map/all_gather | solution.py:85
  16.1 817.9 %reduce-scatter.9.cloned.1.call-start = ((), (), s32[]{:S(2)}) async-start(), calls=%async_computation.11 | async-start | bytes 31457280 | tf_op jit(solution)/shard_map/reduce_scatter | solution.py:104
  16.5 202.9 %copy-start.45 = (f32[3072]{0:T(1024)}, f32[3072]{0:T(1024)S(1)}, u32[]{:S(2)}) copy-start(f32[3072]{0:T(1024)S(1)} %broadcast_select_fusion) | copy-start | bytes 36868
  653.4 347.1 %all-gather.17.cloned.1.call-start = ((), (), s32[]{:S(2)}) async-start(), calls=%async_computation.13 | async-start | bytes 12976128 | tf_op jit(solution)/shard_map/all_gather | solution.py:86
  658.4 424.0 %all-gather.15.cloned.1.call-start = ((), (), s32[]{:S(2)}) async-start(), calls=%async_computation.12 | async-start | bytes 15728640 | tf_op jit(solution)/shard_map/all_gather | solution.py:112
  842.7 336.1 %all-gather.19.cloned.1.call-start = ((), (), s32[]{:S(2)}) async-start(), calls=%async_computation.14 | async-start | bytes 6488064 | tf_op jit(solution)/shard_map/all_gather | solution.py:87
  845.0 415.7 %all-gather.21.cloned.1.call-start = ((), (), s32[]{:S(2)}) async-start(), calls=%async_computation.16 | async-start | bytes 15728640 | tf_op jit(solution)/shard_map/all_gather | solution.py:127
  845.8 676.3 %reduce-scatter.13.cloned.1.call-start = ((), (), s32[]{:S(2)}) async-start(), calls=%async_computation.17 | async-start | bytes 31457280 | tf_op jit(solution)/shard_map/reduce_scatter | solution.py:136
  1341.5 180.6 %copy-start.31 = (f32[1,2048]{1,0:T(1,128)S(1)}, f32[1,2048]{1,0:T(1,128)}, u32[]{:S(2)}) copy-start(f32[1,2048]{1,0:T(1,128)} %copy-done.30) | copy-start | bytes 24580
  1341.5 180.6 %copy-start.48 = (f32[768]{0:T(1024)S(1)}, f32[768]{0:T(1024)}, u32[]{:S(2)}) copy-start(f32[768]{0:T(1024)} %copy-done.47) | copy-start | bytes 9220
  1341.5 187.8 %copy-start.6 = (bf16[768,2048]{1,0:T(8,128)(2,1)S(1)}, bf16[768,2048]{1,0:T(8,128)(2,1)}, u32[]{:S(2)}) copy-start(bf16[768,2048]{1,0:T(8,128)(2,1)} %param.19) | copy-start | bytes 9437188
  1341.5 391.3 %all-gather.23.cloned.1.call-start = ((), (), s32[]{:S(2)}) async-start(), calls=%async_computation.18 | async-start | bytes 15728640 | tf_op jit(solution)/shard_map/all_gather | solution.py:146
  1533.5 746.3 %reduce-scatter.23.cloned.1.call-start = ((), (), s32[]{:S(2)}) async-start(), calls=%async_computation.23 | async-start | bytes 6488064 | tf_op jit(solution)/shard_map/reduce_scatter | solution.py:181
  1558.0 727.8 %reduce-scatter.21.cloned.1.call-start = ((), (), s32[]{:S(2)}) async-start(), calls=%async_computation.22 | async-start | bytes 12976128 | tf_op jit(solution)/shard_map/reduce_scatter | solution.py:178
  1604.3 695.5 %reduce-scatter.19.cloned.1.call-start = ((), (), s32[]{:S(2)}) async-start(), calls=%async_computation.21 | async-start | bytes 2359296 | tf_op jit(solution)/shard_map/reduce_scatter | solution.py:175
  2010.2 26.1 %copy-start.28 = (f32[47,512]{1,0:T(8,128)S(1)}, f32[47,512]{1,0:T(8,128)}, u32[]{:S(2)}) copy-start(f32[47,512]{1,0:T(8,128)} %slice.763) | copy-start | bytes 288772
  2010.3 26.2 %copy-start.75 = (f32[1,512]{1,0:T(1,128)S(1)}, f32[1,512]{1,0:T(1,128)}, u32[]{:S(2)}) copy-start(f32[1,512]{1,0:T(1,128)} %slice.829) | copy-start | bytes 6148
  2110.5 48.6 %copy-start.22 = (bf16[3072,512]{1,0:T(8,128)(2,1)S(1)}, bf16[3072,512]{1,0:T(8,128)(2,1)}, u32[]{:S(2)}) copy-start(bf16[3072,512]{1,0:T(8,128)(2,1)} %get-tuple-element.102) | copy-start | bytes 9437188
  2170.2 189.1 %reduce-scatter.17.cloned.1.call-start = ((), (), s32[]{:S(2)}) async-start(), calls=%async_computation.20 | async-start | bytes 7077888 | tf_op jit(solution)/shard_map/reduce_scatter | solution.py:172
  2209.6 250.3 %reduce-scatter.15.cloned.1.call-start = ((), (), s32[]{:S(2)}) async-start(), calls=%async_computation.19 | async-start | bytes 15728640 | tf_op jit(solution)/shard_map/reduce_scatter | solution.py:161
  2235.1 327.2 %reduce-scatter.11.cloned.1.call-start = ((), (), s32[]{:S(2)}) async-start(), calls=%async_computation.15 | async-start | bytes 15728640 | tf_op jit(solution)/shard_map/reduce_scatter | solution.py:120
  2299.7 59.6 %copy-start.12 = (f32[3,256,512]{1,2,0:T(8,128)S(1)}, f32[3,256,512]{1,2,0:T(8,128)}, u32[]{:S(2)}) copy-start(f32[3,256,512]{1,2,0:T(8,128)} %copy.66) | copy-start | bytes 4718596
  2364.3 95.7 %copy-start.3 = (bf16[768,2048]{1,0:T(8,128)(2,1)S(1)}, bf16[768,2048]{1,0:T(8,128)(2,1)}, u32[]{:S(2)}) copy-start(bf16[768,2048]{1,0:T(8,128)(2,1)} %param.18) | copy-start | bytes 9437188
  2364.3 95.7 %copy-start.40 = (f32[1,2048]{1,0:T(1,128)S(1)}, f32[1,2048]{1,0:T(1,128)}, u32[]{:S(2)}) copy-start(f32[1,2048]{1,0:T(1,128)} %copy-done.39) | copy-start | bytes 24580
  2364.3 95.7 %copy-start.55 = (f32[768]{0:T(1024)S(1)}, f32[768]{0:T(1024)}, u32[]{:S(2)}) copy-start(f32[768]{0:T(1024)} %copy-done.54) | copy-start | bytes 9220
  2368.9 95.0 %copy-start.65 = (f32[2048]{0:T(1024)S(1)}, f32[2048]{0:T(1024)}, u32[]{:S(2)}) copy-start(f32[2048]{0:T(1024)} %get-tuple-element.66) | copy-start | bytes 24580
  2463.8 42.8 %copy-start.38 = (f32[2,2048]{1,0:T(2,128)S(1)}, f32[2,2048]{1,0:T(2,128)}, u32[]{:S(2)}) copy-start(f32[2,2048]{1,0:T(2,128)} %param.25) | copy-start | bytes 49156
  2463.8 42.8 %copy-start.66 = (f32[2,2048]{1,0:T(2,128)S(1)}, f32[2,2048]{1,0:T(2,128)}, u32[]{:S(2)}) copy-start(f32[2,2048]{1,0:T(2,128)} %param.30) | copy-start | bytes 49156
  2463.8 42.8 %copy-start.67 = (f32[2,2048]{1,0:T(2,128)S(1)}, f32[2,2048]{1,0:T(2,128)}, u32[]{:S(2)}) copy-start(f32[2,2048]{1,0:T(2,128)} %param.35) | copy-start | bytes 49156
  (75 other events, 1017.1 us)
Sparse Core Ops, SparseCore 0:
  11.1 101.7 all-gather.10
  115.0 80.2 all-gather.8
  197.9 51.0 all-gather.12
  653.6 180.4 reduce-scatter.8
  836.9 163.6 all-gather.16
  1002.0 80.2 all-gather.14
  1085.2 93.5 all-gather.18
  1180.4 80.2 all-gather.20
  1341.7 180.4 reduce-scatter.12
  1533.6 82.1 all-gather.22
  1619.5 110.3 reduce-scatter.22
  1733.3 192.8 reduce-scatter.20
  2170.3 67.3 reduce-scatter.18
  2241.8 117.4 reduce-scatter.16
  2361.7 98.2 reduce-scatter.14
  2462.4 99.8 reduce-scatter.10
where the time goes:
time: 2620 us; the launch traced here: 2580 us
  waiting for transfers between devices  1070 us (41%)
  local copies, waits for them, and re-layouts  866 us (33%)
  matrix products  338 us (13%)
  other arithmetic  245 us (9%)
  blocking collectives  39.7 us (2%)
    slice x146, local copies, waits for them, and re-layouts, linear_scan(): return lax.associative_scan(combine, (rates, driving), axis=0)[1]  629 us
    reduce_scatter x1, waiting for transfers between devices, per_device(): lax.psum_scatter(jnp.einsum('krf,kdf->rd', rows_block, w_ffn_in, preferre...  181 us
    reduce_scatter x1, waiting for transfers between devices, per_device(): lax.psum_scatter(jnp.dot(gated_low, w_mix_out, preferred_element_type=jnp...  176 us
    all_gather x1, waiting for transfers between devices, per_device(): lax.all_gather(ffn_in.astype(jnp.bfloat16), 'dp', axis=1, tiled=True)  155 us
    pad x42, local copies, waits for them, and re-layouts, linear_scan(): return lax.associative_scan(combine, (rates, driving), axis=0)[1]  123 us
    all_gather x1, waiting for transfers between devices, per_device(): lax.all_gather(mix_in.astype(jnp.bfloat16), 'dp', axis=1, tiled=True)  96.4 us
    reduce_scatter x1, waiting for transfers between devices, per_device(): lax.psum_scatter(jnp.einsum('krc,kdc->rd', rows_block, w_mix_in, preferre...  91.1 us
    all_gather x1, waiting for transfers between devices, per_device(): lax.all_gather(normed_one.astype(jnp.bfloat16), 'tensor', axis=0, tiled=T...  82.4 us
  transfers between devices with their start and end apart: 16, of which 11 were waited for; matrix products, arithmetic and copies ran while one was open for 51% of the time, Pallas kernels for 0%

commit v1 on v0

v1 whole, which is shorter than its diff:
```python
import functools

import jax
import jax.numpy as jnp
from jax import lax
from jax.experimental import pallas as pl
from jax.experimental.pallas import tpu as pltpu
from jax.sharding import PartitionSpec as P

STEP = 10
LOWER_BOUND = 0.8
RMS_EPSILON = 1e-06
BETA_ONE = 0.9
BETA_TWO = 0.999
ADAM_EPSILON = 1e-06
WEIGHT_DECAY = 0.01
LEARN_RATE = 0.5
NORM_EPSILON = 1e-12
CHUNKS = 2
BF = jnp.bfloat16
F32 = jnp.float32
LANES = 128
SUB = 8


def exchange(value, axis, size, offset):
    return lax.ppermute(value, axis, [(i, i ^ offset) for i in range(size)])


def after(value, *others):
    return lax.optimization_barrier((value,) + others)[0]


def mm(a, b):
    return jnp.dot(a, b, preferred_element_type=F32)


def mm_nt(a, b):
    return lax.dot_general(a, b, (((1,), (1,)), ((), ())), preferred_element_type=F32)


def mm_tn(a, b):
    return lax.dot_general(a, b, (((0,), (0,)), ((), ())), preferred_element_type=F32)


def offset_of(place, n):
    return 2 * (place % (n // 2)) + place // (n // 2)


def place_of(offset, n):
    return (offset % 2) * (n // 2) + offset // 2


def gather_blocks(own, axis, size):
    far = [own] + [exchange(own, axis, size, 2 * m) for m in range(1, size // 2)]
    near = [exchange(block, axis, size, 1) for block in far]
    return far + near


def reduce_rows(part, size, rows):
    half = size // 2
    near = exchange(part(half, size).astype(BF), "tensor", size, 1)
    far = (part(1, half) + near[rows:].astype(F32)).astype(BF)
    arrived = [
        exchange(far[(m - 1) * rows : m * rows], "tensor", size, 2 * m) for m in range(1, half)
    ]
    total = part(0, 1) + near[:rows].astype(F32)
    for value in arrived:
        total = total + value.astype(F32)
    return total


def reduce_grad(high, low, size, axis):
    half = size // 2
    near = exchange(high, "dp", size, 1)
    both = low.astype(F32) + near.astype(F32)
    width = both.shape[axis] // half
    parts = [lax.slice_in_dim(both, m * width, (m + 1) * width, axis=axis) for m in range(half)]
    total = parts[0]
    for m in range(1, half):
        total = total + exchange(parts[m].astype(BF), "dp", size, 2 * m).astype(F32)
    return total


def place_columns(values, source, width):
    rows, columns = values.shape

    def kernel(_, src, dst):
        dst[...] = src[...]

    return pl.pallas_call(
        kernel,
        grid_spec=pltpu.PrefetchScalarGridSpec(
            num_scalar_prefetch=1,
            grid=(columns // width,),
            in_specs=[pl.BlockSpec((rows, width), lambda j, s: (0, s[j]))],
            out_specs=pl.BlockSpec((rows, width), lambda j, s: (0, j)),
        ),
        out_shape=jax.ShapeDtypeStruct(values.shape, values.dtype),
        compiler_params=pltpu.CompilerParams(vmem_limit_bytes=32 * 2**20),
        name="place_columns",
    )(source, values)


def sigmoid(v):
    return 0.5 * jnp.tanh(0.5 * v) + 0.5


def keep_of(row0, offsets):
    places = row0 + lax.broadcasted_iota(jnp.int32, (SUB, LANES), 0)
    start = places == offsets[0]
    for d in range(1, offsets.shape[0]):
        start = start | (places == offsets[d])
    return jnp.where(start, 0.0, 1.0).astype(F32)


def forward_kernel(order, offsets, pin, pforget, pgate, gated, before, carry):
    block = pl.program_id(0)
    rows, channels = pin.shape[1:]

    @pl.when(block == 0)
    def _():
        carry[...] = jnp.zeros_like(carry)

    row_id = lax.broadcasted_iota(jnp.int32, (SUB, LANES), 0)

    def step(i, _):
        base = pl.multiple_of(i * 2 * SUB, 2 * SUB)
        keeps = [keep_of(block * rows + base + g * SUB, offsets) for g in range(2)]
        for c in range(channels // LANES):
            lanes = pl.ds(c * LANES, LANES)
            state = carry[:, lanes]
            outs = []
            for g in range(2):
                at = (0, pl.ds(base + g * SUB, SUB), lanes)
                vin, vforget, vgate = pin[at], pforget[at], pgate[at]
                rate = keeps[g] * (LOWER_BOUND + (1.0 - LOWER_BOUND) * sigmoid(vforget))
                drive = (1.0 - rate) * (vin * sigmoid(vin))
                a, b = rate, drive
                for s in (1, 2, 4):
                    inside = row_id >= s
                    a_up = jnp.where(inside, pltpu.roll(a, s, 0), 1.0)
                    b_up = jnp.where(inside, pltpu.roll(b, s, 0), 0.0)
                    b = a * b_up + b
                    a = a * a_up
                whole = b + a * state
                before[at] = jnp.where(row_id == 0, state, pltpu.roll(whole, 1, 0))
                last_a = jnp.broadcast_to(a[SUB - 1 : SUB], (SUB, LANES))
                last_b = jnp.broadcast_to(b[SUB - 1 : SUB], (SUB, LANES))
                state = last_b + last_a * state
                outs.append(whole * (vgate * sigmoid(vgate)))
            carry[:, lanes] = state
            gated[0, pl.ds(base, 2 * SUB), lanes] = jnp.concatenate(outs, axis=0).astype(BF)
        return 0

    lax.fori_loop(0, rows // (2 * SUB), step, 0)


def backward_kernel(order, offsets, pin, pforget, pgate, before, dgated, dpre, carry):
    step_id = pl.program_id(0)
    block = pl.num_programs(0) - 1 - step_id
    rows, channels = pin.shape[1:]

    @pl.when(step_id == 0)
    def _():
        carry[...] = jnp.zeros_like(carry)

    row_id = lax.broadcasted_iota(jnp.int32, (SUB, LANES), 0)
    groups = rows // (2 * SUB)

    def step(i, _):
        base = pl.multiple_of((groups - 1 - i) * 2 * SUB, 2 * SUB)
        keeps = [keep_of(block * rows + base + g * SUB, offsets) for g in range(2)]
        for c in range(channels // LANES):
            lanes = pl.ds(c * LANES, LANES)
            flow = carry[:, lanes]
            outs = [None, None]
            for g in (1, 0):
                at = (0, pl.ds(base + g * SUB, SUB), lanes)
                vin, vforget, vgate = pin[at], pforget[at], pgate[at]
                keep, prev, dg = keeps[g], before[at], dgated[at].astype(F32)
                s_forget = sigmoid(vforget)
                rate = keep * (LOWER_BOUND + (1.0 - LOWER_BOUND) * s_forget)
                s_in = sigmoid(vin)
                act_in = vin * s_in
                rest = 1.0 - rate
                state = rate * prev + rest * act_in
                s_gate = sigmoid(vgate)
                x = dg * (vgate * s_gate)
                a, b = rate, rate * x
                for s in (1, 2, 4):
                    inside = row_id < SUB - s
                    a_down = jnp.where(inside, pltpu.roll(a, SUB - s, 0), 1.0)
                    b_down = jnp.where(inside, pltpu.roll(b, SUB - s, 0), 0.0)
                    b = a * b_down + b
                    a = a * a_down
                q = b + a * flow
                carried = x + jnp.where(row_id == SUB - 1, flow, pltpu.roll(q, SUB - 1, 0))
                first_a = jnp.broadcast_to(a[0:1], (SUB, LANES))
                first_b = jnp.broadcast_to(b[0:1], (SUB, LANES))
                flow = first_b + first_a * flow
                d_in = carried * rest * (s_in * (1.0 + vin * (1.0 - s_in)))
                d_forget = (
                    carried
                    * (prev - act_in)
                    * keep
                    * ((1.0 - LOWER_BOUND) * s_forget * (1.0 - s_forget))
                )
                d_gate = dg * state * (s_gate * (1.0 + vgate * (1.0 - s_gate)))
                outs[g] = (d_in, d_forget, d_gate)
            carry[:, lanes] = flow
            for k in range(3):
                dpre[0, pl.ds(base, 2 * SUB), pl.ds(k * channels + c * LANES, LANES)] = (
                    jnp.concatenate([outs[0][k], outs[1][k]], axis=0).astype(BF)
                )
        return 0

    lax.fori_loop(0, groups, step, 0)


def recurrence_call(kernel, order, offsets, operands, outs, name):
    blocks, rows, channels = operands[0].shape

    def spec(width):
        return pl.BlockSpec((1, rows, width), lambda a, o, f: (o[a], 0, 0))

    return pl.pallas_call(
        kernel,
        grid_spec=pltpu.PrefetchScalarGridSpec(
            num_scalar_prefetch=2,
            grid=(blocks,),
            in_specs=[spec(v.shape[2]) for v in operands],
            out_specs=[spec(v.shape[2]) for v in outs],
            scratch_shapes=[pltpu.VMEM((SUB, channels), F32)],
        ),
        out_shape=outs,
        compiler_params=pltpu.CompilerParams(vmem_limit_bytes=48 * 2**20),
        cost_estimate=pl.CostEstimate(
            flops=blocks * rows * channels * 100,
            bytes_accessed=blocks * rows * channels * 4 * 6,
            transcendentals=blocks * rows * channels * 3,
        ),
        name=name,
    )(order, offsets, *operands)


def unit(values):
    scaling = lax.rsqrt(jnp.mean(values * values, axis=-1, keepdims=True) + RMS_EPSILON)
    return values * scaling, scaling


def norm_backward(d_normed, unit_rows, scaling, gain):
    d_unit = d_normed * gain
    d_values = scaling * (d_unit - unit_rows * jnp.mean(d_unit * unit_rows, axis=-1, keepdims=True))
    return d_values, jnp.sum(d_normed * unit_rows, axis=0)


def adam_moments(grad, weight, first, second, decay_rate):
    first_next = BETA_ONE * first + (1.0 - BETA_ONE) * grad
    second_next = BETA_TWO * second + (1.0 - BETA_TWO) * grad * grad
    update = (
        first_next
        / (1.0 - BETA_ONE**STEP)
        / (jnp.sqrt(second_next / (1.0 - BETA_TWO**STEP)) + ADAM_EPSILON)
        + decay_rate * weight
    )
    return (first_next, second_next, update)


def total_over_mesh(values, n_dp, n_tensor):
    for axis, size in (("tensor", n_tensor), ("dp", n_dp)):
        offset = 1
        while offset < size:
            values = values + exchange(values, axis, size, offset)
            offset *= 2
    return values


def per_device(
    n_dp,
    n_tensor,
    tokens,
    cotangent,
    doc_lengths,
    mix_in,
    mix_out,
    ffn_in,
    ffn_out,
    gains,
    mix_in_m,
    mix_out_m,
    ffn_in_m,
    ffn_out_m,
    gains_m,
    mix_in_v,
    mix_out_v,
    ffn_in_v,
    ffn_out_v,
    gains_v,
):
    rows, width = tokens.shape
    depth = mix_in.shape[1]
    channels = mix_in.shape[2]
    hidden_units = ffn_in.shape[2]
    piece = rows // CHUNKS
    half_width = width // 2
    dp_id = lax.axis_index("dp")
    tensor_id = lax.axis_index("tensor")
    place_source = jnp.stack([dp_id ^ offset_of(p, n_dp) for p in range(n_dp)]).astype(jnp.int32)
    place_back = jnp.stack([place_of(a ^ dp_id, n_dp) for a in range(n_dp)]).astype(jnp.int32)
    order = jnp.stack([place_of(a ^ tensor_id, n_tensor) for a in range(n_tensor)]).astype(jnp.int32)
    offsets = (jnp.cumsum(doc_lengths[0]) - doc_lengths[0]).astype(jnp.int32)

    tokens_p = place_columns(tokens, place_source, depth)
    gains_p = place_columns(gains, place_source, depth)
    inputs = tokens_p.astype(F32)
    unit_one, scale_one = unit(inputs)
    normed_one = (unit_one * gains_p[0]).astype(BF)

    def gather_rows(own):
        return jnp.concatenate(gather_blocks(own, "tensor", n_tensor), axis=0)

    w_mix_in = [
        jnp.concatenate(gather_blocks(mix_in[k].astype(BF), "dp", n_dp), axis=0) for k in range(3)
    ]
    whole_one = gather_rows(normed_one)
    w_mix_out = jnp.concatenate(
        gather_blocks(after(mix_out.astype(BF), w_mix_in[2]), "dp", n_dp), axis=1
    )
    w_ffn_in = [
        jnp.concatenate(
            gather_blocks(after(ffn_in[k].astype(BF), w_mix_in[2]), "dp", n_dp), axis=0
        )
        for k in range(2)
    ]
    w_ffn_out = jnp.concatenate(
        gather_blocks(after(ffn_out.astype(BF), w_ffn_in[1]), "dp", n_dp), axis=1
    )
    cot_p = place_columns(cotangent, place_source, depth)
    cot_pieces = [
        gather_rows(after(cot_p[i * piece : (i + 1) * piece], whole_one)) for i in range(CHUNKS)
    ]

    pre = [mm(whole_one, w).reshape(n_tensor, rows, channels) for w in w_mix_in]
    blocked = (n_tensor, rows, channels)
    gated, before = recurrence_call(
        forward_kernel,
        order,
        offsets,
        pre,
        [jax.ShapeDtypeStruct(blocked, BF), jax.ShapeDtypeStruct(blocked, F32)],
        "recurrence_forward",
    )

    def piece_of(values, i):
        return values[:, i * piece : (i + 1) * piece]

    middle, unit_two, scale_two, whole_two = [], [], [], []
    for i in range(CHUNKS):
        gated_i = piece_of(gated, i)

        def part(lo, hi, gated_i=gated_i):
            return mm(gated_i[lo:hi].reshape(-1, channels), w_mix_out)

        middle_i = inputs[i * piece : (i + 1) * piece] + reduce_rows(part, n_tensor, piece)
        unit_i, scale_i = unit(middle_i)
        middle.append(middle_i)
        unit_two.append(unit_i)
        scale_two.append(scale_i)
        whole_two.append(gather_rows((unit_i * gains_p[1]).astype(BF)))

    hidden, d_gate, d_up, d_middle, gain_two, whole_d = [], [], [], [], 0.0, []
    for i in range(CHUNKS):
        gate = mm(whole_two[i], w_ffn_in[0])
        up = mm(whole_two[i], w_ffn_in[1])
        s_gate = jax.nn.sigmoid(gate)
        act = gate * s_gate
        hidden.append((act * up).astype(BF))
        d_hidden = mm_nt(cot_pieces[i], w_ffn_out)
        d_gate.append((d_hidden * up * (s_gate * (1.0 + gate * (1.0 - s_gate)))).astype(BF))
        d_up.append((d_hidden * act).astype(BF))

        def part(lo, hi, i=i):
            at = slice(lo * piece, hi * piece)
            return mm_nt(d_gate[i][at], w_ffn_in[0]) + mm_nt(d_up[i][at], w_ffn_in[1])

        d_normed = reduce_rows(part, n_tensor, piece)
        d_norm, gain_i = norm_backward(d_normed, unit_two[i], scale_two[i], gains_p[1])
        d_middle_i = cot_p[i * piece : (i + 1) * piece].astype(F32) + d_norm
        gain_two = gain_two + gain_i
        d_middle.append(d_middle_i)
        whole_d.append(gather_rows(d_middle_i.astype(BF)))
    mixed = []
    for i in range(CHUNKS):

        def part(lo, hi, i=i):
            return mm(hidden[i][lo * piece : hi * piece], w_ffn_out)

        mixed.append((middle[i] + reduce_rows(part, n_tensor, piece)).astype(BF))

    def grad_of(lefts, rights):
        total = mm_tn(lefts[0], rights[0])
        for left, right in zip(lefts[1:], rights[1:]):
            total = total + mm_tn(left, right)
        return total.astype(BF)

    g_ffn_out = grad_of(hidden, cot_pieces)
    g_ffn_out = reduce_grad(g_ffn_out[:, half_width:], g_ffn_out[:, :half_width], n_dp, 1)
    g_ffn_in = []
    for side in (d_gate, d_up):
        grad = grad_of(whole_two, side)
        g_ffn_in.append(reduce_grad(grad[half_width:], grad[:half_width], n_dp, 0))

    d_gated = [mm_nt(v, w_mix_out).reshape(n_tensor, piece, channels) for v in whole_d]
    d_gated = jnp.concatenate(d_gated, axis=1)
    (d_pre,) = recurrence_call(
        backward_kernel,
        order[::-1],
        offsets,
        pre + [before, d_gated],
        [jax.ShapeDtypeStruct((n_tensor, rows, 3 * channels), BF)],
        "recurrence_backward",
    )
    w_mix_all = jnp.concatenate(w_mix_in, axis=1)
    g_mix_out = grad_of([piece_of(gated, i).reshape(-1, channels) for i in range(CHUNKS)], whole_d)
    g_mix_out = reduce_grad(g_mix_out[:, half_width:], g_mix_out[:, :half_width], n_dp, 1)
    d_flat = d_pre.reshape(n_tensor * rows, 3 * channels)
    g_mix_in = []
    for k in range(3):
        grad = mm_tn(whole_one, d_flat[:, k * channels : (k + 1) * channels]).astype(BF)
        g_mix_in.append(reduce_grad(grad[half_width:], grad[:half_width], n_dp, 0))
    input_grad, gain_one = [], 0.0
    for i in range(CHUNKS):
        d_i = piece_of(d_pre, i)

        def part(lo, hi, d_i=d_i):
            return mm_nt(d_i[lo:hi].reshape(-1, 3 * channels), w_mix_all)

        at = slice(i * piece, (i + 1) * piece)
        d_norm, gain_i = norm_backward(
            reduce_rows(part, n_tensor, piece), unit_one[at], scale_one[at], gains_p[0]
        )
        gain_one = gain_one + gain_i
        input_grad.append(d_middle[i] + d_norm)

    mixed = place_columns(jnp.concatenate(mixed, axis=0), place_back, depth)
    input_grad = place_columns(jnp.concatenate(input_grad, axis=0), place_back, depth)
    gain_grads = place_columns(jnp.stack([gain_one, gain_two]), place_back, depth)

    weights = [mix_in[0], mix_in[1], mix_in[2], mix_out, ffn_in[0], ffn_in[1], ffn_out]
    firsts = [mix_in_m[0], mix_in_m[1], mix_in_m[2], mix_out_m, ffn_in_m[0], ffn_in_m[1], ffn_out_m]
    seconds = [mix_in_v[0], mix_in_v[1], mix_in_v[2], mix_out_v, ffn_in_v[0], ffn_in_v[1], ffn_out_v]
    grads = g_mix_in + [g_mix_out] + g_ffn_in + [g_ffn_out]
    moments = [
        adam_moments(g, w, m, v, WEIGHT_DECAY)
        for g, w, m, v in zip(grads, weights, firsts, seconds)
    ]
    squares = jnp.stack(
        [jnp.sum(w * w) for w in weights] + [jnp.sum(u * u) for _, _, u in moments]
    )
    packed = jnp.concatenate([gain_grads.reshape(-1), jnp.pad(squares, (0, SUB * LANES - 14))])
    packed = total_over_mesh(packed.reshape(-1, LANES), n_dp, n_tensor).reshape(-1)
    gain_grads = packed[: 2 * width].reshape(2, width)
    squares = packed[2 * width : 2 * width + 14].reshape(2, 7)
    gn_first, gn_second, gn_update = adam_moments(gain_grads, gains, gains_m, gains_v, 0.0)
    weight_sq = jnp.concatenate([squares[0], jnp.sum(gains * gains, axis=1)])
    update_sq = jnp.concatenate([squares[1], jnp.sum(gn_update * gn_update, axis=1)])
    trust = jnp.sqrt(weight_sq) / jnp.sqrt(update_sq + NORM_EPSILON)
    nexts = [w - LEARN_RATE * trust[i] * moments[i][2] for i, w in enumerate(weights)]
    gains_next = gains - LEARN_RATE * trust[7:9][:, None] * gn_update
    layer_norms = jnp.stack([jnp.sqrt(weight_sq), jnp.sqrt(update_sq)])

    def grouped(values):
        return (jnp.stack(values[0:3]), values[3], jnp.stack(values[4:6]), values[6])

    return (
        (mixed, input_grad)
        + grouped(nexts)
        + (gains_next,)
        + grouped([m for m, _, _ in moments])
        + (gn_first,)
        + grouped([v for _, v, _ in moments])
        + (gn_second,)
        + grouped([n.astype(BF) for n in nexts])
        + (layer_norms,)
    )


def solution(mesh):
    rows = P(("dp", "tensor"), None)
    inner = P(None, "dp", "tensor")
    outer = P("tensor", "dp")
    matrices = (inner, outer, inner, outer)
    in_specs = (rows, rows, P("dp", None)) + (matrices + (P(),)) * 3
    out_specs = (rows, rows) + (matrices + (P(),)) * 3 + matrices + (P(),)
    body = functools.partial(per_device, mesh.shape["dp"], mesh.shape["tensor"])
    return jax.shard_map(
        body, mesh=mesh, in_specs=in_specs, out_specs=out_specs, check_vma=False
    )
```

time: 2620 us -> 1600 us (0.61); the launches traced: 2580 us -> 1590 us
  local copies, waits for them, and re-layouts: 866 us -> 76.5 us
  waiting for transfers between devices: 1070 us -> 733 us
  starting transfers between devices: 0.66 us -> 179 us
  other arithmetic: 245 us -> 83.8 us
  matrix products: 338 us -> 457 us
  Pallas kernels: 0 us -> 54.4 us
  blocking collectives: 39.7 us -> 0 us
    ppermute x0 -> x119, waiting for transfers between devices: none -> 733 us  [exchange(): return lax.ppermute(value, axis, [(i, i ^ offset) for i in range(size)])]
    slice x150 -> x22, local copies, waits for them, and re-layouts: 633 us -> 17.7 us  [the longest x7 4.42 us: reduce_grad(): lax.slice_in_dim(both, m * width, (m + 1) * width, axis=axis)]
    all_gather x8 -> x0, waiting for transfers between devices: 549 us -> none  [the longest x1 155 us: per_device(): lax.all_gather(ffn_in.astype(jnp.bfloat16), 'dp', axis=1, tiled=True)]
    reduce_scatter x8 -> x0, waiting for transfers between devices: 524 us -> none  [the longest x1 181 us: per_device(): lax.psum_scatter(jnp.einsum('krf,kdf->rd', rows_block, w_ffn_in, preferre...]
    ppermute x0 -> x119, starting transfers between devices: none -> 179 us  [exchange(): return lax.ppermute(value, axis, [(i, i ^ offset) for i in range(size)])]
    pad x42 -> x0, local copies, waits for them, and re-layouts: 123 us -> none  [linear_scan(): return lax.associative_scan(combine, (rates, driving), axis=0)[1]]
    dot_general x12 -> x52, matrix products: 338 us -> 457 us  [the longest x19 165 us: mm(): return jnp.dot(a, b, preferred_element_type=F32)]
    mul x22 -> x1, other arithmetic: 63.1 us -> 4.55 us  [unit(): return (values * scaling, scaling)]
  transfers between devices with their start and end apart: 16 -> 119, of which waited for: 11 -> 51; matrix products, arithmetic and copies ran while one was open for 51% -> 29% of each run, Pallas kernels for 0% -> 2%
where the time goes in v1:
time: 1600 us; the launch traced here: 1590 us
  waiting for transfers between devices  733 us (46%)
  matrix products  457 us (29%)
  starting transfers between devices  179 us (11%)
  other arithmetic  83.8 us (5%)
  local copies, waits for them, and re-layouts  76.5 us (5%)
  Pallas kernels  54.4 us (3%)
    ppermute x119, waiting for transfers between devices, exchange(): return lax.ppermute(value, axis, [(i, i ^ offset) for i in range(size)])  733 us
    ppermute x119, starting transfers between devices, exchange(): return lax.ppermute(value, axis, [(i, i ^ offset) for i in range(size)])  179 us
    dot_general x19, matrix products, mm(): return jnp.dot(a, b, preferred_element_type=F32)  165 us
    dot_general x22, matrix products, mm_nt(): lax.dot_general(a, b, (((1,), (1,)), ((), ())), preferred_element_type=F32)  165 us
    dot_general x11, matrix products, mm_tn(): lax.dot_general(a, b, (((0,), (0,)), ((), ())), preferred_element_type=F32)  127 us
    unnamed x396, local copies, waits for them, and re-layouts  45.2 us
    pallas_call x2, Pallas kernels, recurrence_call(): pl.pallas_call(kernel, grid_spec=pltpu.PrefetchScalarGridSpec(num_scalar_...  40.8 us
  transfers between devices with their start and end apart: 119, of which 51 were waited for; matrix products, arithmetic and copies ran while one was open for 29% of the time, Pallas kernels for 2%

profile of v1, /device:TPU:0, one launch (start us, length us, event | category | flops | bytes accessed | tf_op | source)
XLA Modules:
  0.0 1592.0 jit_solution(13372413300673429889)
XLA Ops:
  216.1 16.8 %recurrence_forward.1 = (bf16[4,768,512]{2,1,0:T(8,128)(2,1)S(1)}, f32[4,768,512]{2,1,0:T(8,128)}) custom-call(s32[4]{0:T(128)S(1)} %get-tuple-element.216.order, s32[4]{0:T(128)S(1)} %get-tuple-element.217.offsets, f32[4,768,512]{2,1,0:T(8,128)} %bitcast.358, f32[4,768,512]{2,1,0:T(8,128)} %bitcast.360, f32[4,768,512]{2,1,0:T(8,128)} %bitcast.356), custom_call_target="tpu_custom_call" | custom-call | flops 157286400 | bytes 37748736 | tf_op jit(solution)/shard_map/recurrence_forward/pallas_call | solution.py:227
  246.8 34.1 %collective-permute-done.37 = bf16[256,1408]{1,0:T(8,128)(2,1)} collective-permute-done((bf16[256,1408]{1,0:T(8,128)(2,1)S(1)}, bf16[256,1408]{1,0:T(8,128)(2,1)}, u32[]{:S(2)}, u32[]{:S(2)}) %collective-permute-start.37) | collective-permute-done | bytes 720928 | tf_op jit(solution)/shard_map/ppermute | solution.py:27
  316.5 19.8 %collective-permute-start.50 = (bf16[1408,256]{1,0:T(8,128)(2,1)S(1)}, bf16[1408,256]{1,0:T(8,128)(2,1)S(1)}, u32[]{:S(2)}, u32[]{:S(2)}) collective-permute-start(bf16[1408,256]{1,0:T(8,128)(2,1)S(1)} %copy-done.46), channel_id=1, source_target_pairs={{0,8},{4,12},{8,0},{12,4},{16,24},{20,28},{24,16},{28,20},{1,9},{5... | collective-permute-start | bytes 2162696 | tf_op jit(solution)/shard_map/ppermute | solution.py:27
  363.9 32.0 %collective-permute-done.51 = bf16[1408,256]{1,0:T(8,128)(2,1)S(1)} collective-permute-done((bf16[1408,256]{1,0:T(8,128)(2,1)S(1)}, bf16[1408,256]{1,0:T(8,128)(2,1)S(1)}, u32[]{:S(2)}, u32[]{:S(2)}) %collective-permute-start.51) | collective-permute-done | bytes 720928 | tf_op jit(solution)/shard_map/ppermute | solution.py:27
  399.8 15.1 collective-permute-done.54
  415.1 15.3 collective-permute-done.55
  445.7 23.8 %collective-permute-done.33 = bf16[384,2048]{1,0:T(8,128)(2,1)S(1)} collective-permute-done((bf16[384,2048]{1,0:T(8,128)(2,1)S(1)}, bf16[384,2048]{1,0:T(8,128)(2,1)S(1)}, u32[]{:S(2)}, u32[]{:S(2)}) %collective-permute-start.33) | collective-permute-done | bytes 1572896 | tf_op jit(solution)/shard_map/ppermute | solution.py:27
  483.2 15.5 fusion.138
  498.8 22.5 %multiply_convert_fusion.3 = (bf16[1536,1408]{1,0:T(8,128)(2,1)S(1)}, bf16[1536,1408]{1,0:T(8,128)(2,1)}, bf16[1536,1408]{1,0:T(8,128)(2,1)}) fusion(f32[1536,1408]{1,0:T(8,128)} %fusion.172, f32[1536,1408]{1,0:T(8,128)} %fusion.138, bf16[2048,1408]{1,0:T(8,128)(2,1)} %copy-done.36, bf16[384,2048]{1,0:T(8,128)(2,1)} %collective-permute-done.35, ...), kind=kOutput, calls=%fused_computation.7 | convolution fusion | flops 8915976192 | bytes 42336256 | tf_op jit(solution)/shard_map/dot_general | solution.py:35
  545.0 32.0 %collective-permute-done.74 = bf16[384,2048]{1,0:T(8,128)(2,1)} collective-permute-done((bf16[384,2048]{1,0:T(8,128)(2,1)}, bf16[384,2048]{1,0:T(8,128)(2,1)}, u32[]{:S(2)}, u32[]{:S(2)}) %collective-permute-start.74) | collective-permute-done | bytes 1572896 | tf_op jit(solution)/shard_map/ppermute | solution.py:27
  600.0 16.9 %collective-permute-done.60 = bf16[384,2048]{1,0:T(8,128)(2,1)S(1)} collective-permute-done((bf16[384,2048]{1,0:T(8,128)(2,1)S(1)}, bf16[384,2048]{1,0:T(8,128)(2,1)S(1)}, u32[]{:S(2)}, u32[]{:S(2)}) %collective-permute-start.60) | collective-permute-done | bytes 1572896 | tf_op jit(solution)/shard_map/ppermute | solution.py:27
  624.7 25.5 %collective-permute-done.70 = bf16[384,2048]{1,0:T(8,128)(2,1)S(1)} collective-permute-done((bf16[384,2048]{1,0:T(8,128)(2,1)S(1)}, bf16[384,2048]{1,0:T(8,128)(2,1)S(1)}, u32[]{:S(2)}, u32[]{:S(2)}) %collective-permute-start.70) | collective-permute-done | bytes 1572896 | tf_op jit(solution)/shard_map/ppermute | solution.py:27
  675.2 19.3 %collective-permute-done.61 = bf16[384,2048]{1,0:T(8,128)(2,1)S(1)} collective-permute-done((bf16[384,2048]{1,0:T(8,128)(2,1)S(1)}, bf16[384,2048]{1,0:T(8,128)(2,1)S(1)}, u32[]{:S(2)}, u32[]{:S(2)}) %collective-permute-start.61) | collective-permute-done | bytes 1572896 | tf_op jit(solution)/shard_map/ppermute | solution.py:27
  707.7 19.2 %collective-permute-done.58 = bf16[384,2048]{1,0:T(8,128)(2,1)S(1)} collective-permute-done((bf16[384,2048]{1,0:T(8,128)(2,1)}, bf16[384,2048]{1,0:T(8,128)(2,1)S(1)}, u32[]{:S(2)}, u32[]{:S(2)}) %collective-permute-start.58) | collective-permute-done | bytes 1572896 | tf_op jit(solution)/shard_map/ppermute | solution.py:27
  748.2 24.1 %multiply_convert_fusion.1 = (bf16[1536,1408]{1,0:T(8,128)(2,1)}, bf16[1536,1408]{1,0:T(8,128)(2,1)}, bf16[1536,1408]{1,0:T(8,128)(2,1)}) fusion(f32[1536,1408]{1,0:T(8,128)} %fusion.173, f32[1536,1408]{1,0:T(8,128)} %fusion.136, bf16[2048,1408]{1,0:T(8,128)(2,1)} %copy-done.36, bf16[384,2048]{1,0:T(8,128)(2,1)} %collective-permute-done.63, ...), kind=kOutput, calls=%fused_computation.5 | convolution fusion | flops 8915976192 | bytes 42336256 | tf_op jit(solution)/shard_map/dot_general | solution.py:35
  829.7 14.7 add_convert_fusion.1
  848.9 15.7 fusion.135
  864.6 15.1 add_convert_fusion.2
  882.9 14.5 add_convert_fusion
  919.1 52.8 %collective-permute-done.102 = bf16[1024,1408]{1,0:T(8,128)(2,1)S(1)} collective-permute-done((bf16[1024,1408]{1,0:T(8,128)(2,1)}, bf16[1024,1408]{1,0:T(8,128)(2,1)S(1)}, u32[]{:S(2)}, u32[]{:S(2)}) %collective-permute-start.102) | collective-permute-done | bytes 2883616 | tf_op jit(solution)/shard_map/ppermute | solution.py:27
  976.0 56.8 %collective-permute-done.110 = bf16[1408,1024]{1,0:T(8,128)(2,1)} collective-permute-done((bf16[1408,1024]{1,0:T(8,128)(2,1)S(1)}, bf16[1408,1024]{1,0:T(8,128)(2,1)}, u32[]{:S(2)}, u32[]{:S(2)}) %collective-permute-start.110) | collective-permute-done | bytes 2883616 | tf_op jit(solution)/shard_map/ppermute | solution.py:27
  1052.4 24.8 %collective-permute-done.78 = bf16[384,2048]{1,0:T(8,128)(2,1)S(1)} collective-permute-done((bf16[384,2048]{1,0:T(8,128)(2,1)S(1)}, bf16[384,2048]{1,0:T(8,128)(2,1)S(1)}, u32[]{:S(2)}, u32[]{:S(2)}) %collective-permute-start.78) | collective-permute-done | bytes 1572896 | tf_op jit(solution)/shard_map/ppermute | solution.py:27
  1097.6 42.9 %collective-permute-done.104 = bf16[256,1408]{1,0:T(8,128)(2,1)} collective-permute-done((bf16[256,1408]{1,0:T(8,128)(2,1)}, bf16[256,1408]{1,0:T(8,128)(2,1)}, u32[]{:S(2)}, u32[]{:S(2)}) %collective-permute-start.104) | collective-permute-done | bytes 720928 | tf_op jit(solution)/shard_map/ppermute | solution.py:27
  1148.3 24.7 %collective-permute-done.112 = bf16[1408,256]{1,0:T(8,128)(2,1)S(1)} collective-permute-done((bf16[1408,256]{1,0:T(8,128)(2,1)}, bf16[1408,256]{1,0:T(8,128)(2,1)S(1)}, u32[]{:S(2)}, u32[]{:S(2)}) %collective-permute-start.112) | collective-permute-done | bytes 720928 | tf_op jit(solution)/shard_map/ppermute | solution.py:27
  1184.9 16.7 %collective-permute-done.79 = bf16[384,2048]{1,0:T(8,128)(2,1)} collective-permute-done((bf16[384,2048]{1,0:T(8,128)(2,1)}, bf16[384,2048]{1,0:T(8,128)(2,1)}, u32[]{:S(2)}, u32[]{:S(2)}) %collective-permute-start.79) | collective-permute-done | bytes 1572896 | tf_op jit(solution)/shard_map/ppermute | solution.py:27
  1247.0 24.1 %recurrence_backward.1 = bf16[4,768,1536]{2,1,0:T(8,128)(2,1)} custom-call(s32[4]{0:T(128)S(1)} %rev.3.order, s32[4]{0:T(128)S(1)} %copy-done.8, f32[4,768,512]{2,1,0:T(8,128)} %bitcast.359, f32[4,768,512]{2,1,0:T(8,128)} %bitcast.361, f32[4,768,512]{2,1,0:T(8,128)} %bitcast.357, f32[4,768,512]{2,1,0:T(8,128)} %get-tuple-element.36.before, ...), custom_call_target="tpu_custom_call" | custom-call | flops 157286400 | bytes 37748736 | tf_op jit(solution)/shard_map/recurrence_backward/pallas_call | solution.py:227
  1340.3 22.0 %collective-permute-done.86 = bf16[1024,512]{1,0:T(8,128)(2,1)S(1)} collective-permute-done((bf16[1024,512]{1,0:T(8,128)(2,1)S(1)}, bf16[1024,512]{1,0:T(8,128)(2,1)S(1)}, u32[]{:S(2)}, u32[]{:S(2)}) %collective-permute-start.86) | collective-permute-done | bytes 1048608 | tf_op jit(solution)/shard_map/ppermute | solution.py:27
  1366.0 18.7 %collective-permute-done.94 = bf16[1024,512]{1,0:T(8,128)(2,1)S(1)} collective-permute-done((bf16[1024,512]{1,0:T(8,128)(2,1)S(1)}, bf16[1024,512]{1,0:T(8,128)(2,1)S(1)}, u32[]{:S(2)}, u32[]{:S(2)}) %collective-permute-start.94) | collective-permute-done | bytes 1048608 | tf_op jit(solution)/shard_map/ppermute | solution.py:27
  1384.8 21.6 %collective-permute-done.98 = bf16[512,1024]{1,0:T(8,128)(2,1)S(1)} collective-permute-done((bf16[512,1024]{1,0:T(8,128)(2,1)S(1)}, bf16[512,1024]{1,0:T(8,128)(2,1)S(1)}, u32[]{:S(2)}, u32[]{:S(2)}) %collective-permute-start.98) | collective-permute-done | bytes 1048608 | tf_op jit(solution)/shard_map/ppermute | solution.py:27
  1425.1 15.8 collective-permute-done.88
  1447.1 16.2 %collective-permute-done.96 = bf16[256,512]{1,0:T(8,128)(2,1)S(1)} collective-permute-done((bf16[256,512]{1,0:T(8,128)(2,1)S(1)}, bf16[256,512]{1,0:T(8,128)(2,1)S(1)}, u32[]{:S(2)}, u32[]{:S(2)}) %collective-permute-start.96) | collective-permute-done | bytes 262176 | tf_op jit(solution)/shard_map/ppermute | solution.py:27
  1521.3 23.0 %collective-permute-done.83 = bf16[384,2048]{1,0:T(8,128)(2,1)} collective-permute-done((bf16[384,2048]{1,0:T(8,128)(2,1)}, bf16[384,2048]{1,0:T(8,128)(2,1)}, u32[]{:S(2)}, u32[]{:S(2)}) %collective-permute-start.83) | collective-permute-done | bytes 1572896 | tf_op jit(solution)/shard_map/ppermute | solution.py:27
  (779 shorter events, 831.7 us)
Async XLA Ops:
  10.4 71.4 %collective-permute-start = (bf16[768,2048]{1,0:T(8,128)(2,1)}, bf16[768,2048]{1,0:T(8,128)(2,1)}, u32[]{:S(2)}, u32[]{:S(2)}) collective-permute-start(bf16[768,2048]{1,0:T(8,128)(2,1)} %get-tuple-element.124), channel_id=1, source_target_pairs={{0,2},{1,3},{2,0},{3,1},{4,6},{5,7},{6,4},{7,5},{8,10},{9,11},{10,... | collective-permute-start | bytes 9437192 | tf_op jit(solution)/shard_map/ppermute | solution.py:27
  30.6 145.9 %collective-permute-start.1 = (bf16[768,2048]{1,0:T(8,128)(2,1)}, bf16[768,2048]{1,0:T(8,128)(2,1)S(1)}, u32[]{:S(2)}, u32[]{:S(2)}) collective-permute-start(bf16[768,2048]{1,0:T(8,128)(2,1)} %get-tuple-element.124), channel_id=1, source_target_pairs={{0,1},{1,0},{2,3},{3,2},{4,5},{5,4},{6,7},{7,6},{8,9},{9,8},{10,11... | collective-permute-start | bytes 9437192 | tf_op jit(solution)/shard_map/ppermute | solution.py:27
  81.7 99.4 %collective-permute-start.2 = (bf16[768,2048]{1,0:T(8,128)(2,1)}, bf16[768,2048]{1,0:T(8,128)(2,1)S(1)}, u32[]{:S(2)}, u32[]{:S(2)}) collective-permute-start(bf16[768,2048]{1,0:T(8,128)(2,1)} %collective-permute-done), channel_id=1, source_target_pairs={{0,1},{1,0},{2,3},{3,2},{4,5},{5,4},{6,7},{7,6},{8,9},{9,8},{10,11... | collective-permute-start | bytes 9437192 | tf_op jit(solution)/shard_map/ppermute | solution.py:27
  166.6 68.3 %collective-permute-start.44 = (bf16[256,1408]{1,0:T(8,128)(2,1)S(1)}, bf16[256,1408]{1,0:T(8,128)(2,1)}, u32[]{:S(2)}, u32[]{:S(2)}) collective-permute-start(bf16[256,1408]{1,0:T(8,128)(2,1)S(1)} %copy-done.48), channel_id=1, source_target_pairs={{0,16},{4,20},{8,24},{12,28},{16,0},{20,4},{24,8},{28,12},{1,17},{... | collective-permute-start | bytes 2162696 | tf_op jit(solution)/shard_map/ppermute | solution.py:27
  173.4 63.6 %collective-permute-start.45 = (bf16[256,1408]{1,0:T(8,128)(2,1)S(1)}, bf16[256,1408]{1,0:T(8,128)(2,1)}, u32[]{:S(2)}, u32[]{:S(2)}) collective-permute-start(bf16[256,1408]{1,0:T(8,128)(2,1)S(1)} %copy-done.48), channel_id=1, source_target_pairs={{0,24},{4,28},{8,16},{12,20},{16,8},{20,12},{24,0},{28,4},{1,25},{... | collective-permute-start | bytes 2162696 | tf_op jit(solution)/shard_map/ppermute | solution.py:27
  174.0 67.5 %collective-permute-start.46 = (bf16[256,1408]{1,0:T(8,128)(2,1)S(1)}, bf16[256,1408]{1,0:T(8,128)(2,1)}, u32[]{:S(2)}, u32[]{:S(2)}) collective-permute-start(bf16[256,1408]{1,0:T(8,128)(2,1)S(1)} %copy-done.48), channel_id=1, source_target_pairs={{0,4},{4,0},{8,12},{12,8},{16,20},{20,16},{24,28},{28,24},{1,5},{5... | collective-permute-start | bytes 2162696 | tf_op jit(solution)/shard_map/ppermute | solution.py:27
  176.5 67.8 %collective-permute-start.36 = (bf16[256,1408]{1,0:T(8,128)(2,1)S(1)}, bf16[256,1408]{1,0:T(8,128)(2,1)}, u32[]{:S(2)}, u32[]{:S(2)}) collective-permute-start(bf16[256,1408]{1,0:T(8,128)(2,1)S(1)} %copy-done.47), channel_id=1, source_target_pairs={{0,8},{4,12},{8,0},{12,4},{16,24},{20,28},{24,16},{28,20},{1,9},{5... | collective-permute-start | bytes 2162696 | tf_op jit(solution)/shard_map/ppermute | solution.py:27
  181.1 99.7 %collective-permute-start.37 = (bf16[256,1408]{1,0:T(8,128)(2,1)S(1)}, bf16[256,1408]{1,0:T(8,128)(2,1)}, u32[]{:S(2)}, u32[]{:S(2)}) collective-permute-start(bf16[256,1408]{1,0:T(8,128)(2,1)S(1)} %copy-done.47), channel_id=1, source_target_pairs={{0,16},{4,20},{8,24},{12,28},{16,0},{20,4},{24,8},{28,12},{1,17},{... | collective-permute-start | bytes 2162696 | tf_op jit(solution)/shard_map/ppermute | solution.py:27
  234.9 118.6 %collective-permute-start.31 = (bf16[768,2048]{1,0:T(8,128)(2,1)S(1)}, bf16[768,2048]{1,0:T(8,128)(2,1)S(1)}, u32[]{:S(2)}, u32[]{:S(2)}) collective-permute-start(bf16[768,2048]{1,0:T(8,128)(2,1)S(1)} %convolution_convert_fusion.1), channel_id=1, source_target_pairs={{0,1},{1,0},{2,3},{3,2},{4,5},{5,4},{6,7},{7,6},{8,9},{9,8},{10,11... | collective-permute-start | bytes 9437192 | tf_op jit(solution)/shard_map/ppermute | solution.py:27
  285.9 64.5 %collective-permute-start.41 = (bf16[256,1408]{1,0:T(8,128)(2,1)}, bf16[256,1408]{1,0:T(8,128)(2,1)S(1)}, u32[]{:S(2)}, u32[]{:S(2)}) collective-permute-start(bf16[256,1408]{1,0:T(8,128)(2,1)} %collective-permute-done.37), channel_id=1, source_target_pairs={{0,4},{4,0},{8,12},{12,8},{16,20},{20,16},{24,28},{28,24},{1,5},{5... | collective-permute-start | bytes 2162696 | tf_op jit(solution)/shard_map/ppermute | solution.py:27
  353.5 77.1 %collective-permute-start.66 = (bf16[384,2048]{1,0:T(8,128)(2,1)S(1)}, bf16[384,2048]{1,0:T(8,128)(2,1)S(1)}, u32[]{:S(2)}, u32[]{:S(2)}) collective-permute-start(bf16[384,2048]{1,0:T(8,128)(2,1)S(1)} %copy-done.37), channel_id=1, source_target_pairs={{0,2},{1,3},{2,0},{3,1},{4,6},{5,7},{6,4},{7,5},{8,10},{9,11},{10,... | collective-permute-start | bytes 4718600 | tf_op jit(solution)/shard_map/ppermute | solution.py:27
  360.5 70.6 %collective-permute-start.32 = (bf16[384,2048]{1,0:T(8,128)(2,1)S(1)}, bf16[384,2048]{1,0:T(8,128)(2,1)S(1)}, u32[]{:S(2)}, u32[]{:S(2)}) collective-permute-start(bf16[384,2048]{1,0:T(8,128)(2,1)S(1)} %add_convert_fusion.15), channel_id=1, source_target_pairs={{0,2},{1,3},{2,0},{3,1},{4,6},{5,7},{6,4},{7,5},{8,10},{9,11},{10,... | collective-permute-start | bytes 4718600 | tf_op jit(solution)/shard_map/ppermute | solution.py:27
  444.5 132.5 %collective-permute-start.59 = (bf16[768,2048]{1,0:T(8,128)(2,1)}, bf16[768,2048]{1,0:T(8,128)(2,1)}, u32[]{:S(2)}, u32[]{:S(2)}) collective-permute-start(bf16[768,2048]{1,0:T(8,128)(2,1)} %convolution_convert_fusion), channel_id=1, source_target_pairs={{0,1},{1,0},{2,3},{3,2},{4,5},{5,4},{6,7},{7,6},{8,9},{9,8},{10,11... | collective-permute-start | bytes 9437192 | tf_op jit(solution)/shard_map/ppermute | solution.py:27
  543.0 119.0 %collective-permute-start.75 = (bf16[384,2048]{1,0:T(8,128)(2,1)}, bf16[384,2048]{1,0:T(8,128)(2,1)}, u32[]{:S(2)}, u32[]{:S(2)}) collective-permute-start(bf16[384,2048]{1,0:T(8,128)(2,1)} %get-tuple-element.37), channel_id=1, source_target_pairs={{0,1},{1,0},{2,3},{3,2},{4,5},{5,4},{6,7},{7,6},{8,9},{9,8},{10,11... | collective-permute-start | bytes 4718600 | tf_op jit(solution)/shard_map/ppermute | solution.py:27
  577.0 86.5 %collective-permute-start.76 = (bf16[384,2048]{1,0:T(8,128)(2,1)}, bf16[384,2048]{1,0:T(8,128)(2,1)}, u32[]{:S(2)}, u32[]{:S(2)}) collective-permute-start(bf16[384,2048]{1,0:T(8,128)(2,1)} %collective-permute-done.74), channel_id=1, source_target_pairs={{0,1},{1,0},{2,3},{3,2},{4,5},{5,4},{6,7},{7,6},{8,9},{9,8},{10,11... | collective-permute-start | bytes 4718600 | tf_op jit(solution)/shard_map/ppermute | solution.py:27
  600.0 65.2 %collective-permute-start.57 = (bf16[768,2048]{1,0:T(8,128)(2,1)}, bf16[768,2048]{1,0:T(8,128)(2,1)}, u32[]{:S(2)}, u32[]{:S(2)}) collective-permute-start(bf16[768,2048]{1,0:T(8,128)(2,1)} %convolution_convert_fusion.5), channel_id=1, source_target_pairs={{0,1},{1,0},{2,3},{3,2},{4,5},{5,4},{6,7},{7,6},{8,9},{9,8},{10,11... | collective-permute-start | bytes 9437192 | tf_op jit(solution)/shard_map/ppermute | solution.py:27
  796.3 250.0 %collective-permute-start.64 = (bf16[768,2048]{1,0:T(8,128)(2,1)}, bf16[768,2048]{1,0:T(8,128)(2,1)}, u32[]{:S(2)}, u32[]{:S(2)}) collective-permute-start(bf16[768,2048]{1,0:T(8,128)(2,1)} %convolution_convert_fusion.4), channel_id=1, source_target_pairs={{0,1},{1,0},{2,3},{3,2},{4,5},{5,4},{6,7},{7,6},{8,9},{9,8},{10,11... | collective-permute-start | bytes 9437192 | tf_op jit(solution)/shard_map/ppermute | solution.py:27
  814.7 221.7 %collective-permute-start.77 = (bf16[768,2048]{1,0:T(8,128)(2,1)}, bf16[768,2048]{1,0:T(8,128)(2,1)}, u32[]{:S(2)}, u32[]{:S(2)}) collective-permute-start(bf16[768,2048]{1,0:T(8,128)(2,1)} %add_convert_fusion.3), channel_id=1, source_target_pairs={{0,1},{1,0},{2,3},{3,2},{4,5},{5,4},{6,7},{7,6},{8,9},{9,8},{10,11... | collective-permute-start | bytes 9437192 | tf_op jit(solution)/shard_map/ppermute | solution.py:27
  844.7 67.3 %collective-permute-start.106 = (bf16[1024,1408]{1,0:T(8,128)(2,1)S(1)}, bf16[1024,1408]{1,0:T(8,128)(2,1)}, u32[]{:S(2)}, u32[]{:S(2)}) collective-permute-start(bf16[1024,1408]{1,0:T(8,128)(2,1)S(1)} %slice.655), channel_id=1, source_target_pairs={{0,4},{4,0},{8,12},{12,8},{16,20},{20,16},{24,28},{28,24},{1,5},{5... | collective-permute-start | bytes 8650760 | tf_op jit(solution)/shard_map/ppermute | solution.py:27
  881.5 90.4 %collective-permute-start.102 = (bf16[1024,1408]{1,0:T(8,128)(2,1)}, bf16[1024,1408]{1,0:T(8,128)(2,1)S(1)}, u32[]{:S(2)}, u32[]{:S(2)}) collective-permute-start(bf16[1024,1408]{1,0:T(8,128)(2,1)} %slice.649), channel_id=1, source_target_pairs={{0,4},{4,0},{8,12},{12,8},{16,20},{20,16},{24,28},{28,24},{1,5},{5... | collective-permute-start | bytes 8650760 | tf_op jit(solution)/shard_map/ppermute | solution.py:27
  897.9 134.9 %collective-permute-start.110 = (bf16[1408,1024]{1,0:T(8,128)(2,1)S(1)}, bf16[1408,1024]{1,0:T(8,128)(2,1)}, u32[]{:S(2)}, u32[]{:S(2)}) collective-permute-start(bf16[1408,1024]{1,0:T(8,128)(2,1)S(1)} %slice.661), channel_id=1, source_target_pairs={{0,4},{4,0},{8,12},{12,8},{16,20},{20,16},{24,28},{28,24},{1,5},{5... | collective-permute-start | bytes 8650760 | tf_op jit(solution)/shard_map/ppermute | solution.py:27
  918.3 169.6 %collective-permute-start.109 = (bf16[256,1408]{1,0:T(8,128)(2,1)}, bf16[256,1408]{1,0:T(8,128)(2,1)}, u32[]{:S(2)}, u32[]{:S(2)}) collective-permute-start(bf16[256,1408]{1,0:T(8,128)(2,1)} %get-tuple-element.146), channel_id=1, source_target_pairs={{0,24},{4,28},{8,16},{12,20},{16,8},{20,12},{24,0},{28,4},{1,25},{... | collective-permute-start | bytes 2162696 | tf_op jit(solution)/shard_map/ppermute | solution.py:27
  971.9 121.3 %collective-permute-start.108 = (bf16[256,1408]{1,0:T(8,128)(2,1)}, bf16[256,1408]{1,0:T(8,128)(2,1)}, u32[]{:S(2)}, u32[]{:S(2)}) collective-permute-start(bf16[256,1408]{1,0:T(8,128)(2,1)} %get-tuple-element.147), channel_id=1, source_target_pairs={{0,16},{4,20},{8,24},{12,28},{16,0},{20,4},{24,8},{28,12},{1,17},{... | collective-permute-start | bytes 2162696 | tf_op jit(solution)/shard_map/ppermute | solution.py:27
  1078.3 62.2 %collective-permute-start.104 = (bf16[256,1408]{1,0:T(8,128)(2,1)}, bf16[256,1408]{1,0:T(8,128)(2,1)}, u32[]{:S(2)}, u32[]{:S(2)}) collective-permute-start(bf16[256,1408]{1,0:T(8,128)(2,1)} %get-tuple-element.150), channel_id=1, source_target_pairs={{0,16},{4,20},{8,24},{12,28},{16,0},{20,4},{24,8},{28,12},{1,17},{... | collective-permute-start | bytes 2162696 | tf_op jit(solution)/shard_map/ppermute | solution.py:27
  1095.0 78.1 %collective-permute-start.112 = (bf16[1408,256]{1,0:T(8,128)(2,1)}, bf16[1408,256]{1,0:T(8,128)(2,1)S(1)}, u32[]{:S(2)}, u32[]{:S(2)}) collective-permute-start(bf16[1408,256]{1,0:T(8,128)(2,1)} %get-tuple-element.153), channel_id=1, source_target_pairs={{0,16},{4,20},{8,24},{12,28},{16,0},{20,4},{24,8},{28,12},{1,17},{... | collective-permute-start | bytes 2162696 | tf_op jit(solution)/shard_map/ppermute | solution.py:27
  1095.3 77.7 %collective-permute-start.111 = (bf16[1408,256]{1,0:T(8,128)(2,1)}, bf16[1408,256]{1,0:T(8,128)(2,1)S(1)}, u32[]{:S(2)}, u32[]{:S(2)}) collective-permute-start(bf16[1408,256]{1,0:T(8,128)(2,1)} %get-tuple-element.151), channel_id=1, source_target_pairs={{0,8},{4,12},{8,0},{12,4},{16,24},{20,28},{24,16},{28,20},{1,9},{5... | collective-permute-start | bytes 2162696 | tf_op jit(solution)/shard_map/ppermute | solution.py:27
  1140.5 78.0 %collective-permute-start.65 = (bf16[384,2048]{1,0:T(8,128)(2,1)}, bf16[384,2048]{1,0:T(8,128)(2,1)}, u32[]{:S(2)}, u32[]{:S(2)}) collective-permute-start(bf16[384,2048]{1,0:T(8,128)(2,1)} %add_convert_fusion.11), channel_id=1, source_target_pairs={{0,2},{1,3},{2,0},{3,1},{4,6},{5,7},{6,4},{7,5},{8,10},{9,11},{10,... | collective-permute-start | bytes 4718600 | tf_op jit(solution)/shard_map/ppermute | solution.py:27
  1147.1 71.4 %collective-permute-start.71 = (bf16[384,2048]{1,0:T(8,128)(2,1)}, bf16[384,2048]{1,0:T(8,128)(2,1)}, u32[]{:S(2)}, u32[]{:S(2)}) collective-permute-start(bf16[384,2048]{1,0:T(8,128)(2,1)} %get-tuple-element.121), channel_id=1, source_target_pairs={{0,2},{1,3},{2,0},{3,1},{4,6},{5,7},{6,4},{7,5},{8,10},{9,11},{10,... | collective-permute-start | bytes 4718600 | tf_op jit(solution)/shard_map/ppermute | solution.py:27
  1312.0 158.6 %collective-permute-start.84 = (bf16[768,2048]{1,0:T(8,128)(2,1)}, bf16[768,2048]{1,0:T(8,128)(2,1)}, u32[]{:S(2)}, u32[]{:S(2)}) collective-permute-start(bf16[768,2048]{1,0:T(8,128)(2,1)} %convolution_convert_fusion.2), channel_id=1, source_target_pairs={{0,1},{1,0},{2,3},{3,2},{4,5},{5,4},{6,7},{7,6},{8,9},{9,8},{10,11... | collective-permute-start | bytes 9437192 | tf_op jit(solution)/shard_map/ppermute | solution.py:27
  1315.8 68.9 %collective-permute-start.94 = (bf16[1024,512]{1,0:T(8,128)(2,1)S(1)}, bf16[1024,512]{1,0:T(8,128)(2,1)S(1)}, u32[]{:S(2)}, u32[]{:S(2)}) collective-permute-start(bf16[1024,512]{1,0:T(8,128)(2,1)S(1)} %slice.637), channel_id=1, source_target_pairs={{0,4},{4,0},{8,12},{12,8},{16,20},{20,16},{24,28},{28,24},{1,5},{5... | collective-permute-start | bytes 3145736 | tf_op jit(solution)/shard_map/ppermute | solution.py:27
  1329.8 76.6 %collective-permute-start.98 = (bf16[512,1024]{1,0:T(8,128)(2,1)S(1)}, bf16[512,1024]{1,0:T(8,128)(2,1)S(1)}, u32[]{:S(2)}, u32[]{:S(2)}) collective-permute-start(bf16[512,1024]{1,0:T(8,128)(2,1)S(1)} %slice.643), channel_id=1, source_target_pairs={{0,4},{4,0},{8,12},{12,8},{16,20},{20,16},{24,28},{28,24},{1,5},{5... | collective-permute-start | bytes 3145736 | tf_op jit(solution)/shard_map/ppermute | solution.py:27
  1339.8 139.6 %collective-permute-start.82 = (bf16[768,2048]{1,0:T(8,128)(2,1)}, bf16[768,2048]{1,0:T(8,128)(2,1)}, u32[]{:S(2)}, u32[]{:S(2)}) collective-permute-start(bf16[768,2048]{1,0:T(8,128)(2,1)} %convolution_convert_fusion.3), channel_id=1, source_target_pairs={{0,1},{1,0},{2,3},{3,2},{4,5},{5,4},{6,7},{7,6},{8,9},{9,8},{10,11... | collective-permute-start | bytes 9437192 | tf_op jit(solution)/shard_map/ppermute | solution.py:27
  (258 other events, 6983.9 us)

commit v2 on v1

v2 whole, which is shorter than its diff:
```python
import functools

import jax
import jax.numpy as jnp
from jax import lax
from jax.experimental import pallas as pl
from jax.experimental.pallas import tpu as pltpu
from jax.sharding import PartitionSpec as P

STEP = 10
LOWER_BOUND = 0.8
RMS_EPSILON = 1e-06
BETA_ONE = 0.9
BETA_TWO = 0.999
ADAM_EPSILON = 1e-06
WEIGHT_DECAY = 0.01
LEARN_RATE = 0.5
NORM_EPSILON = 1e-12
CHUNKS = 2
BF = jnp.bfloat16
F32 = jnp.float32
LANES = 128
SUB = 8


def likely_flops(flops):
    return int(1.6 * flops) + 4_000_000_000


def exchange(value, axis, size, offset):
    return lax.ppermute(value, axis, [(i, i ^ offset) for i in range(size)])


def after(value, *others):
    return lax.optimization_barrier((value,) + others)[0]


def mm(a, b):
    return jnp.dot(a, b, preferred_element_type=F32)


def mm_nt(a, b):
    return lax.dot_general(a, b, (((1,), (1,)), ((), ())), preferred_element_type=F32)


def mm_tn(a, b):
    return lax.dot_general(a, b, (((0,), (0,)), ((), ())), preferred_element_type=F32)


class Sequence:
    def __init__(self):
        self.last = None

    def run(self, call, *operands):
        if self.last is not None:
            operands = (after(operands[0], self.last),) + operands[1:]
        result = call(*operands)
        self.last = jax.tree.leaves(result)[0]
        return result

    def pin(self, *values):
        out = lax.optimization_barrier(values + (self.last,))
        self.last = out[0]
        return out[:-1]


def join(axis):
    return lambda *blocks: jnp.concatenate(blocks, axis=axis)


def halving(n):
    offsets, offset = [], 1
    while offset < n:
        offsets.append(offset)
        offset *= 2
    return offsets


def offsets_by_place(exchanges):
    offsets = [0]
    for offset in reversed(exchanges):
        offsets = offsets + [o ^ offset for o in offsets]
    return offsets


def owners(index, exchanges):
    return jnp.stack([index ^ o for o in offsets_by_place(exchanges)]).astype(jnp.int32)


def spread(blocks, owner):
    rows, columns = blocks[0].shape
    whole = jnp.zeros((rows * len(blocks), columns), blocks[0].dtype)
    for p, block in enumerate(blocks):
        whole = lax.dynamic_update_slice(whole, block, (owner[p] * rows, 0))
    return whole


class SummedGrad:
    def __init__(self, sequence, halves, size, exchanges):
        self.sequence, self.size, self.exchanges = sequence, size, exchanges
        self.send(*halves)

    def send(self, sent, kept):
        self.kept = kept
        self.coming = exchange(sent, "dp", self.size, self.exchanges[0])
        self.exchanges = self.exchanges[1:]

    def step(self):
        def added(a, b):
            total = (a.astype(F32) + b.astype(F32)).astype(BF)
            half = total.shape[0] // 2
            return total[half:], total[:half]

        self.send(*self.sequence.run(added, self.kept, self.coming))

    def steps(self):
        while self.exchanges:
            self.step()


class Gathered:
    def __init__(self, own, size):
        self.size, self.held = size, [own]
        offset = size // 2
        while offset > 1:
            self.held = self.held + [exchange(part, "tensor", size, offset) for part in self.held]
            offset //= 2
        self.near = [exchange(own, "tensor", size, 1)]

    def relay(self, *done):
        self.near += [exchange(after(part, *done), "tensor", self.size, 1) for part in self.held[1:]]

    def parts(self):
        return self.held + self.near


class SummedRows:
    def __init__(self, sequence, operand, weight, size, rows):
        self.sequence, self.weight, self.size, self.rows = sequence, weight, size, rows
        self.operand = operand

    def high(self):
        half = self.size // 2 * self.rows
        if isinstance(self.operand, tuple):
            self.operand, upper = self.operand
            call = lambda v, w: mm_nt(v, w).astype(BF)
        else:
            upper = self.operand
            call = lambda v, w: mm_nt(v[half:], w).astype(BF)
        sent = self.sequence.run(call, upper, self.weight)
        self.near = exchange(sent, "tensor", self.size, 1)

    def rest(self):
        size, rows, offset, places = self.size, self.rows, 2, self.size // 4
        far, self.kept = self.sequence.run(
            lambda v, w, n: near_added(v, w, n, places * rows), self.operand, self.weight, self.near
        )
        self.coming = exchange(far, "tensor", size, offset)
        while places > 1:
            total = self.kept + self.coming.astype(F32)
            offset, places = 2 * offset, places // 2
            self.kept = total[: places * rows]
            self.coming = exchange(total[places * rows :].astype(BF), "tensor", size, offset)


def near_added(operand, weight, near, tile):
    width = weight.shape[0]

    def kernel(v, w, n, far, kept):
        step = pl.program_id(0)
        total = mm_nt(v[...], w[...]) + n[...].astype(F32)

        @pl.when(step == 0)
        def _():
            far[...] = total.astype(BF)

        @pl.when(step == 1)
        def _():
            kept[...] = total

    def rowed(v):
        return pl.BlockSpec((tile, v.shape[1]), lambda i: (1 - i, 0))

    fixed = pl.BlockSpec((tile, width), lambda i: (0, 0))
    return pl.pallas_call(
        kernel,
        grid=(2,),
        in_specs=[
            rowed(operand),
            pl.BlockSpec(weight.shape, lambda i: (0, 0), pipeline_mode=pl.Buffered(1)),
            rowed(near),
        ],
        out_specs=[fixed, fixed],
        out_shape=[jax.ShapeDtypeStruct((tile, width), BF), jax.ShapeDtypeStruct((tile, width), F32)],
        compiler_params=pltpu.CompilerParams(vmem_limit_bytes=56 * 2**20),
        cost_estimate=pl.CostEstimate(
            flops=likely_flops(4 * tile * weight.size), bytes_accessed=2 * weight.size, transcendentals=0
        ),
        name="near_added",
    )(operand, weight, near)


def sigmoid(v):
    return 0.5 * jnp.tanh(0.5 * v) + 0.5


def gate_up_kernel(x, w, hidden, slope, act):
    units = hidden.shape[1]
    for n in range(0, units, 256):
        at = slice(n, min(n + 256, units))
        up_at = slice(units + n, units + min(n + 256, units))
        gate = jnp.dot(x[...], w[:, at], preferred_element_type=F32)
        up = jnp.dot(x[...], w[:, up_at], preferred_element_type=F32)
        s = sigmoid(gate)
        a = gate * s
        hidden[:, at] = (a * up).astype(BF)
        act[:, at] = a.astype(BF)
        slope[:, at] = (up * (s * (1.0 + gate * (1.0 - s)))).astype(BF)


def gate_up_back_kernel(c, w, slope, act, out):
    units = slope.shape[1]
    for n in range(0, units, 256):
        at = slice(n, min(n + 256, units))
        up_at = slice(units + n, units + min(n + 256, units))
        d = jnp.dot(c[...], w[:, at], preferred_element_type=F32)
        out[:, at] = (d * slope[:, at].astype(F32)).astype(BF)
        out[:, up_at] = (d * act[:, at].astype(F32)).astype(BF)


def pre_kernel(x, w, out):
    out[...] = jnp.dot(x[...], w[...], preferred_element_type=F32)


def row_tiles(kernel, parts, weight, others, outs, flops, name):
    count = len(parts)
    tile, depth = parts[0].shape

    def body(*refs):
        sources, w, rest = refs[:count], refs[count], refs[count + 1 : -2]
        buffer, arrived = refs[-2:]
        step = pl.program_id(0)

        def copy(p):
            return pltpu.make_async_copy(sources[p], buffer.at[p % 2], arrived.at[p % 2])

        @pl.when(step == 0)
        def _():
            copy(0).start()

        for p in range(count):

            @pl.when(step == p)
            def _(p=p):
                if p + 1 < count:
                    copy(p + 1).start()
                copy(p).wait()

        kernel(buffer.at[lax.rem(step, 2)], w, *rest)

    def spec(v):
        return pl.BlockSpec((tile, v.shape[1]), lambda i: (i, 0))

    return pl.pallas_call(
        body,
        grid=(count,),
        in_specs=[pl.BlockSpec(memory_space=pl.ANY)] * count
        + [pl.BlockSpec(weight.shape, lambda i: (0, 0), pipeline_mode=pl.Buffered(1))]
        + [spec(v) for v in others],
        out_specs=[spec(v) for v in outs],
        out_shape=outs,
        scratch_shapes=[pltpu.VMEM((2, tile, depth), BF), pltpu.SemaphoreType.DMA((2,))],
        compiler_params=pltpu.CompilerParams(vmem_limit_bytes=56 * 2**20),
        cost_estimate=pl.CostEstimate(
            flops=likely_flops(flops), bytes_accessed=weight.size * 4, transcendentals=0
        ),
        name=name,
    )(*parts, weight, *others)


def grad_kernel(lefts, rights, moving, wide, name, fixed=(0, 1), owner=None):
    part, parts = fixed
    mover, other = (lefts, rights) if moving == "left" else (rights, lefts)
    rows = sum(v.shape[0] for v in mover)
    steps = mover[0].shape[1] // wide
    held = other[0].shape[1] // parts
    shape = (wide, held) if moving == "left" else (held, wide)
    half = steps // 2
    count, others = len(mover), len(other)

    def body(owners_ref, sources, write):
        movers, fixers = sources[:count], sources[count : count + others]
        moved, kept, arrived, ready = sources[-4:]
        step = pl.program_id(0)

        def copies(at, slot):
            column = at if owners_ref is None else owners_ref[lax.rem(at + half, steps)]
            columns = pl.ds(pl.multiple_of(column * wide, wide), wide)
            made, row = [], 0
            for p, source in enumerate(movers):
                size = source.shape[0]
                made.append(
                    pltpu.make_async_copy(
                        source.at[:, columns],
                        moved.at[slot, pl.ds(row, size), :],
                        arrived.at[slot, p],
                    )
                )
                row += size
            return made

        def fixed_copies():
            made, row = [], 0
            for p, source in enumerate(fixers):
                size = source.shape[0]
                made.append(
                    pltpu.make_async_copy(
                        source.at[:, pl.ds(part * held, held)],
                        kept.at[pl.ds(row, size), :],
                        ready.at[p],
                    )
                )
                row += size
            return made

        @pl.when(step == 0)
        def _():
            for copy in copies(0, 0) + fixed_copies():
                copy.start()

        slot = lax.rem(step, 2)

        @pl.when(step + 1 < steps)
        def _():
            for copy in copies(step + 1, 1 - slot):
                copy.start()

        for copy in copies(step, slot):
            copy.wait()

        @pl.when(step == 0)
        def _():
            for copy in fixed_copies():
                copy.wait()

        pair = (moved[slot], kept[...]) if moving == "left" else (kept[...], moved[slot])
        total = lax.dot_general(
            *pair, (((0,), (0,)), ((), ())), preferred_element_type=F32
        ).astype(BF)
        write(step, total)

    settings = dict(
        compiler_params=pltpu.CompilerParams(vmem_limit_bytes=56 * 2**20),
        cost_estimate=pl.CostEstimate(
            flops=likely_flops(2 * steps * shape[0] * shape[1] * rows),
            bytes_accessed=2 * steps * shape[0] * shape[1],
            transcendentals=0,
        ),
        name=name,
    )
    in_specs = [pl.BlockSpec(memory_space=pl.ANY)] * (count + others)
    scratch = [
        pltpu.VMEM((2, rows, wide), BF),
        pltpu.VMEM((rows, held), BF),
        pltpu.SemaphoreType.DMA((2, count)),
        pltpu.SemaphoreType.DMA((others,)),
    ]
    if owner is None:

        def kernel(*refs):
            out = refs[count + others]

            def write(step, total):
                out[...] = total

            body(None, refs[: count + others] + refs[-4:], write)

        whole = (shape[0] * steps, shape[1]) if moving == "left" else (shape[0], shape[1] * steps)
        place = (lambda p: (p, 0)) if moving == "left" else (lambda p: (0, p))
        return pl.pallas_call(
            kernel,
            grid=(steps,),
            in_specs=in_specs,
            out_specs=pl.BlockSpec(shape, place),
            out_shape=jax.ShapeDtypeStruct(whole, BF),
            scratch_shapes=scratch,
            **settings,
        )(*mover, *other)

    def kernel_by_place(owners_ref, *refs):
        sent, kept = refs[count + others : count + others + 2]

        def write(step, total):
            @pl.when(step < half)
            def _():
                sent[0] = total

            @pl.when(step >= half)
            def _():
                kept[0] = total

        body(owners_ref, refs[: count + others] + refs[-4:], write)

    return pl.pallas_call(
        kernel_by_place,
        grid_spec=pltpu.PrefetchScalarGridSpec(
            num_scalar_prefetch=1,
            grid=(steps,),
            in_specs=in_specs,
            out_specs=[
                pl.BlockSpec((1,) + shape, lambda p, o: (jnp.minimum(p, half - 1), 0, 0)),
                pl.BlockSpec((1,) + shape, lambda p, o: (jnp.maximum(p - half, 0), 0, 0)),
            ],
            scratch_shapes=scratch,
        ),
        out_shape=[jax.ShapeDtypeStruct((half,) + shape, BF)] * 2,
        **settings,
    )(owner, *mover, *other)


def keep_of(row0, offsets):
    places = row0 + lax.broadcasted_iota(jnp.int32, (SUB, LANES), 0)
    start = places == offsets[0]
    for d in range(1, offsets.shape[0]):
        start = start | (places == offsets[d])
    return jnp.where(start, 0.0, 1.0).astype(F32)


def forward_kernel(order, offsets, pre, before, *rest):
    gated, carry = rest[:-1], rest[-1]
    block = pl.program_id(0)
    rows = pre.shape[1]
    channels = before.shape[2]
    piece = rows // len(gated)

    @pl.when(block == 0)
    def _():
        carry[...] = jnp.zeros_like(carry)

    row_id = lax.broadcasted_iota(jnp.int32, (SUB, LANES), 0)

    def step(i, _, p):
        local = pl.multiple_of(i * 2 * SUB, 2 * SUB)
        base = pl.multiple_of(p * piece + i * 2 * SUB, 2 * SUB)
        keeps = [keep_of(block * rows + base + g * SUB, offsets) for g in range(2)]
        for c in range(channels // LANES):
            lanes = pl.ds(c * LANES, LANES)
            state = carry[:, lanes]
            outs = []
            for g in range(2):
                here = pl.ds(base + g * SUB, SUB)
                vin, vforget, vgate = (
                    pre[0, here, pl.ds(k * channels + c * LANES, LANES)] for k in range(3)
                )
                rate = keeps[g] * (LOWER_BOUND + (1.0 - LOWER_BOUND) * sigmoid(vforget))
                drive = (1.0 - rate) * (vin * sigmoid(vin))
                a, b = rate, drive
                for s in (1, 2, 4):
                    inside = row_id >= s
                    a_up = jnp.where(inside, pltpu.roll(a, s, 0), 1.0)
                    b_up = jnp.where(inside, pltpu.roll(b, s, 0), 0.0)
                    b = a * b_up + b
                    a = a * a_up
                whole = b + a * state
                before[0, here, lanes] = jnp.where(row_id == 0, state, pltpu.roll(whole, 1, 0))
                last_a = jnp.broadcast_to(a[SUB - 1 : SUB], (SUB, LANES))
                last_b = jnp.broadcast_to(b[SUB - 1 : SUB], (SUB, LANES))
                state = last_b + last_a * state
                outs.append(whole * (vgate * sigmoid(vgate)))
            carry[:, lanes] = state
            gated[p][0, pl.ds(local, 2 * SUB), lanes] = jnp.concatenate(outs, axis=0).astype(BF)
        return 0

    for p in range(len(gated)):
        lax.fori_loop(0, piece // (2 * SUB), functools.partial(step, p=p), 0)


def backward_kernel(order, offsets, pre, before, *rest):
    pieces = (len(rest) - 2) // 2
    dgated, dpieces, dpre, carry = rest[:pieces], rest[pieces : 2 * pieces], rest[-2], rest[-1]
    step_id = pl.program_id(0)
    block = pl.num_programs(0) - 1 - step_id
    rows = pre.shape[1]
    channels = before.shape[2]
    piece = rows // pieces
    groups = piece // (2 * SUB)

    @pl.when(step_id == 0)
    def _():
        carry[...] = jnp.zeros_like(carry)

    row_id = lax.broadcasted_iota(jnp.int32, (SUB, LANES), 0)

    def step(i, _, p):
        local = pl.multiple_of((groups - 1 - i) * 2 * SUB, 2 * SUB)
        base = pl.multiple_of(p * piece + (groups - 1 - i) * 2 * SUB, 2 * SUB)
        keeps = [keep_of(block * rows + base + g * SUB, offsets) for g in range(2)]
        for c in range(channels // LANES):
            lanes = pl.ds(c * LANES, LANES)
            flow = carry[:, lanes]
            outs = [None, None]
            for g in (1, 0):
                here = pl.ds(base + g * SUB, SUB)
                vin, vforget, vgate = (
                    pre[0, here, pl.ds(k * channels + c * LANES, LANES)] for k in range(3)
                )
                keep, prev = keeps[g], before[0, here, lanes]
                dg = dgated[p][0, pl.ds(local + g * SUB, SUB), lanes]
                s_forget = sigmoid(vforget)
                rate = keep * (LOWER_BOUND + (1.0 - LOWER_BOUND) * s_forget)
                s_in = sigmoid(vin)
                act_in = vin * s_in
                rest_in = 1.0 - rate
                state = rate * prev + rest_in * act_in
                s_gate = sigmoid(vgate)
                x = dg * (vgate * s_gate)
                a, b = rate, rate * x
                for s in (1, 2, 4):
                    inside = row_id < SUB - s
                    a_down = jnp.where(inside, pltpu.roll(a, SUB - s, 0), 1.0)
                    b_down = jnp.where(inside, pltpu.roll(b, SUB - s, 0), 0.0)
                    b = a * b_down + b
                    a = a * a_down
                q = b + a * flow
                carried = x + jnp.where(row_id == SUB - 1, flow, pltpu.roll(q, SUB - 1, 0))
                first_a = jnp.broadcast_to(a[0:1], (SUB, LANES))
                first_b = jnp.broadcast_to(b[0:1], (SUB, LANES))
                flow = first_b + first_a * flow
                d_in = carried * rest_in * (s_in * (1.0 + vin * (1.0 - s_in)))
                d_forget = (
                    carried
                    * (prev - act_in)
                    * keep
                    * ((1.0 - LOWER_BOUND) * s_forget * (1.0 - s_forget))
                )
                d_gate = dg * state * (s_gate * (1.0 + vgate * (1.0 - s_gate)))
                outs[g] = (d_in, d_forget, d_gate)
            carry[:, lanes] = flow
            for k in range(3):
                value = jnp.concatenate([outs[0][k], outs[1][k]], axis=0).astype(BF)
                at = pl.ds(k * channels + c * LANES, LANES)
                dpre[0, pl.ds(base, 2 * SUB), at] = value
                dpieces[p][0, pl.ds(local, 2 * SUB), at] = value
        return 0

    for p in reversed(range(pieces)):
        lax.fori_loop(0, groups, functools.partial(step, p=p), 0)


def recurrence_call(kernel, order, offsets, operands, outs, channels, name):
    blocks, rows = operands[0].shape[:2]

    def spec(v):
        return pl.BlockSpec((1,) + v.shape[1:], lambda a, o, f: (o[a], 0, 0))

    return pl.pallas_call(
        kernel,
        grid_spec=pltpu.PrefetchScalarGridSpec(
            num_scalar_prefetch=2,
            grid=(blocks,),
            in_specs=[spec(v) for v in operands],
            out_specs=[spec(v) for v in outs],
            scratch_shapes=[pltpu.VMEM((SUB, channels), F32)],
        ),
        out_shape=outs,
        compiler_params=pltpu.CompilerParams(vmem_limit_bytes=48 * 2**20),
        cost_estimate=pl.CostEstimate(
            flops=blocks * rows * channels * 15000,
            bytes_accessed=blocks * rows * channels * 4 * 6,
            transcendentals=blocks * rows * channels * 3,
        ),
        name=name,
    )(order, offsets, *operands)


def unit(values):
    scaling = lax.rsqrt(jnp.mean(values * values, axis=-1, keepdims=True) + RMS_EPSILON)
    return values * scaling, scaling


def norm_backward(d_normed, unit_rows, scaling, gain):
    d_unit = d_normed * gain
    d_values = scaling * (d_unit - unit_rows * jnp.mean(d_unit * unit_rows, axis=-1, keepdims=True))
    return d_values, jnp.sum(d_normed * unit_rows, axis=0)


def adam_moments(grad, weight, first, second, decay_rate):
    first_next = BETA_ONE * first + (1.0 - BETA_ONE) * grad
    second_next = BETA_TWO * second + (1.0 - BETA_TWO) * grad * grad
    update = (
        first_next
        / (1.0 - BETA_ONE**STEP)
        / (jnp.sqrt(second_next / (1.0 - BETA_TWO**STEP)) + ADAM_EPSILON)
        + decay_rate * weight
    )
    return (first_next, second_next, update)


def total_over_mesh(values, n_dp, n_tensor):
    for axis, size in (("tensor", n_tensor), ("dp", n_dp)):
        offset = 1
        while offset < size:
            values = values + exchange(values, axis, size, offset)
            offset *= 2
    return values


def per_device(
    n_dp,
    n_tensor,
    tokens,
    cotangent,
    doc_lengths,
    mix_in,
    mix_out,
    ffn_in,
    ffn_out,
    gains,
    mix_in_m,
    mix_out_m,
    ffn_in_m,
    ffn_out_m,
    gains_m,
    mix_in_v,
    mix_out_v,
    ffn_in_v,
    ffn_out_v,
    gains_v,
):
    rows, width = tokens.shape
    depth = mix_in.shape[1]
    channels = mix_in.shape[2]
    hidden_units = ffn_in.shape[2]
    units = -(-hidden_units // LANES) * LANES
    piece = rows // CHUNKS
    pieces = range(CHUNKS)
    dp_id = lax.axis_index("dp")
    tensor_id = lax.axis_index("tensor")
    near_first = halving(n_dp)
    owner = owners(dp_id, near_first)
    z_first = near_first[1:2] + near_first[:1] + near_first[2:]
    owner_z = owners(dp_id, z_first)
    row_places = offsets_by_place(halving(n_tensor))
    place_of = jnp.array([row_places.index(o) for o in range(n_tensor)], jnp.int32)
    order = place_of[jnp.arange(n_tensor) ^ tensor_id]
    offsets = (jnp.cumsum(doc_lengths[0]) - doc_lengths[0]).astype(jnp.int32)
    sequence = Sequence()
    run = sequence.run

    def cut(i):
        return slice(i * piece, (i + 1) * piece)

    def padded(v):
        return jnp.pad(v, ((0, 0), (0, units - hidden_units)))

    weights = [mix_in[0], mix_in[1], mix_in[2], mix_out, ffn_in[0], ffn_in[1], ffn_out]

    own_mix_in = jnp.concatenate([mix_in[k] for k in range(3)], axis=1).astype(BF)
    halves, scales_one = [], []
    for i in range(2):
        half = tokens[i * (rows // 2) : (i + 1) * (rows // 2)]
        unit_i, scale_i = unit(after(half, own_mix_in).astype(F32))
        halves.append((unit_i * gains[0]).astype(BF))
        scales_one.append(scale_i)
    scale_one = jnp.concatenate(scales_one, axis=0)
    far_offsets = offsets_by_place(near_first)[1 : n_dp // 2]
    early = sorted(far_offsets, key=lambda o: (o & near_first[1] == 0, o))
    early, late = early[: len(early) // 2 + 1], early[len(early) // 2 + 1 :]
    all_offsets = [0] + far_offsets
    owner_far = [dp_id ^ j for j in all_offsets]
    owner_near = [dp_id ^ j ^ 1 for j in all_offsets]

    def distant(half):
        held, offset = [half], n_tensor // 2
        while offset > 1:
            held = held + [exchange(part, "tensor", n_tensor, offset) for part in held]
            offset //= 2
        return held

    far = {j: exchange(own_mix_in, "dp", n_dp, j) for j in early}
    near = {0: exchange(own_mix_in, "dp", n_dp, 1)}
    far_a = distant(halves[0])
    first = lax.optimization_barrier((far_a, near, far))
    far_a, near, far = first
    own_ffn_in = jnp.concatenate([padded(ffn_in[k].astype(BF)) for k in range(2)], axis=1)
    far.update({j: exchange(after(own_mix_in, far_a[0]), "dp", n_dp, j) for j in late})
    near.update({j: exchange(far[j], "dp", n_dp, 1) for j in early})
    own_b = after(halves[1], far_a[0])
    far_b = distant(own_b)
    weight_sq = jnp.stack([jnp.sum(w * w) for w in [after(weights[0], far_a[0])] + weights[1:]])
    second = lax.optimization_barrier((far_a, far_b, near, far, weight_sq, own_ffn_in))
    far_a, far_b, near, far, weight_sq, own_ffn_in = second
    near.update({j: exchange(far[j], "dp", n_dp, 1) for j in late})
    near_a = [exchange(part, "tensor", n_tensor, 1) for part in far_a]
    near_b = [exchange(part, "tensor", n_tensor, 1) for part in far_b]
    known = [(dp_id, after(own_mix_in, far_a[0]))] + [(dp_id ^ j, far[j]) for j in far_offsets]
    known += [(dp_id ^ j ^ 1, near[j]) for j in [0] + early]
    w_mix_in = jnp.zeros((width, 3 * channels), BF)
    for place, block in known:
        w_mix_in = lax.dynamic_update_slice(w_mix_in, block, (place * depth, 0))
    own_mix_out = after(mix_out.astype(BF).T, *near_a, *near_b)
    far_mo = [own_mix_out] + [exchange(own_mix_out, "dp", n_dp, j) for j in far_offsets]
    third = lax.optimization_barrier(
        (near_a, near_b, w_mix_in, own_ffn_in, [near[j] for j in late], far_mo)
    )
    near_a, near_b, w_mix_in, own_ffn_in, last, far_mo = third
    w_ffn_in = lax.all_gather(own_ffn_in, "dp", axis=0, tiled=True)
    w_ffn_out = lax.all_gather(padded(ffn_out.astype(BF).T), "dp", axis=0, tiled=True)
    cots = [Gathered(after(cotangent[cut(0)], near_b[0]), n_tensor)]
    for j, block in zip(late, last):
        w_mix_in = lax.dynamic_update_slice(w_mix_in, block, ((dp_id ^ j ^ 1) * depth, 0))
    sequence.last = near_b[0]
    whole_one = [v for pair in zip(far_a + near_a, far_b + near_b) for v in pair]
    near_mo = [exchange(block, "dp", n_dp, 1) for block in far_mo]
    (pre,) = run(
        lambda w, *parts: row_tiles(
            pre_kernel,
            parts,
            w,
            [],
            [jax.ShapeDtypeStruct((n_tensor * rows, 3 * channels), F32)],
            2 * n_tensor * rows * width * 3 * channels,
            "pre",
        ),
        w_mix_in,
        *whole_one,
    )
    pre = pre.reshape(n_tensor, rows, 3 * channels)
    scanned = recurrence_call(
        forward_kernel,
        order,
        offsets,
        [after(pre, sequence.last)],
        [jax.ShapeDtypeStruct((n_tensor, rows, channels), F32)]
        + [jax.ShapeDtypeStruct((n_tensor, piece, channels), BF)] * CHUNKS,
        channels,
        "recurrence_forward",
    )
    before, gated = scanned[0], scanned[1:]
    sequence.last = before

    w_mix_out = run(
        lambda *blocks: spread(blocks, owner_far + owner_near), far_mo[0], *far_mo[1:], *near_mo
    )

    sums = [
        SummedRows(sequence, gated[i].reshape(-1, channels), w_mix_out, n_tensor, piece) for i in pieces
    ]
    (cots[0].held[1],) = sequence.pin(cots[0].held[1])
    for i in pieces:
        sums[i].high()
    for i in pieces:
        sums[i].rest()
    comings = sequence.pin(*[v.coming for v in sums])

    def middle_of(kept, coming, own):
        middle = own.astype(F32) + kept + coming.astype(F32)
        unit_rows, scaling = unit(middle)
        return (unit_rows * gains[1]).astype(BF), middle, scaling

    middle, scale_two, whole_two = [], [], []
    for i in pieces:
        normed_i, middle_i, scale_i = run(middle_of, sums[i].kept, comings[i], tokens[cut(i)])
        middle.append(middle_i)
        scale_two.append(scale_i)
        if i > 0:
            normed_i = after(normed_i, whole_two[i - 1].held[1])
        whole_two.append(Gathered(normed_i, n_tensor))
    hidden, slope, act = [], [], []
    many = n_tensor * piece
    flops = 2 * many * width * units
    whole_two[0].relay()
    one = jax.ShapeDtypeStruct((many // 2, units), BF)
    for i in pieces:
        if i > 0:
            whole_two[i].relay(sequence.last)
        halves = [
            run(
                lambda w, *parts: row_tiles(
                    gate_up_kernel, parts, w, [], [one] * 3, flops, "gate_up"
                ),
                w_ffn_in,
                *parts,
            )
            for parts in (whole_two[i].held, whole_two[i].near)
        ]
        if i > 0:
            cots[i].relay(sequence.last)
        elif CHUNKS > 1:
            cots[0].relay(sequence.last)
            cots.append(
                Gathered(after(cotangent[cut(1)], whole_two[1].held[1], sequence.last), n_tensor)
            )
        hidden.append((halves[0][0], halves[1][0]))
        slope.append((halves[0][1], halves[1][1]))
        act.append((halves[0][2], halves[1][2]))

    def listed(chunks):
        return [part for gathered in chunks for part in gathered.parts()]

    def grad(lefts, rights, *settings, **more):
        def call(*values):
            return grad_kernel(values[: len(lefts)], values[len(lefts) :], *settings, **more)

        return run(call, *lefts, *rights)

    def flat(pairs):
        return [v for pair in pairs for v in pair]

    grad_fo = grad(flat(hidden), listed(cots), "right", min(256, depth), "grad_out")
    grad_fo = lax.psum_scatter(grad_fo, "dp", scatter_dimension=1, tiled=True)

    def gate_up_back(i, half):
        (d,) = run(
            lambda w, v, a, *parts: row_tiles(
                gate_up_back_kernel,
                parts,
                w,
                [v, a],
                [jax.ShapeDtypeStruct((many // 2, 2 * units), BF)],
                flops // 2,
                "gate_up_back",
            ),
            w_ffn_out,
            slope[i][half],
            act[i][half],
            *(cots[i].near if half else cots[i].held),
        )
        return d

    sums = [SummedRows(sequence, None, w_ffn_in, n_tensor, piece) for i in pieces]
    downs = [SummedRows(sequence, h, w_ffn_out, n_tensor, piece) for h in hidden]
    upper = []
    for i in pieces:
        upper.append(gate_up_back(i, 1))
        sums[i].operand = (None, upper[i])
        sums[i].high()
    d_two = []
    for i in pieces:
        lower = gate_up_back(i, 0)
        d_two.append((lower, upper[i]))
        sums[i].operand = lower
        sums[i].rest()
    for i in pieces:
        downs[i].high()
    (grad_fo,) = sequence.pin(grad_fo)
    grad_fi = grad(listed(whole_two), flat(d_two), "left", min(256, depth), "grad_in")
    grad_fi = lax.psum_scatter(grad_fi, "dp", scatter_dimension=0, tiled=True)
    comings = sequence.pin(*[v.coming for v in sums])

    def middle_back(kept, coming, mid, scaling, cot):
        unit_rows = mid * scaling
        d_norm, gain = norm_backward(kept + coming.astype(F32), unit_rows, scaling, gains[1])
        d_mid = cot.astype(F32) + d_norm
        return d_mid.astype(BF), d_mid, gain

    d_middle, gain_two, lows, whole_d = [], 0.0, [], []
    for i in pieces:
        low, d_mid, gain_i = run(
            middle_back, sums[i].kept, comings[i], middle[i], scale_two[i], cotangent[cut(i)]
        )
        d_middle.append(d_mid)
        gain_two = gain_two + gain_i
        lows.append(low)
    whole_d.append(Gathered(lows[0], n_tensor))
    for i in pieces:
        downs[i].rest()
    for i in range(1, CHUNKS):
        whole_d.append(
            Gathered(after(lows[i], whole_d[i - 1].held[1], sequence.last), n_tensor)
        )
    for gathered in whole_d:
        gathered.relay(sequence.last)

    d_gated = []
    for i in pieces:
        (d_i,) = run(
            lambda w, *parts: row_tiles(
                pre_kernel,
                parts,
                w,
                [],
                [jax.ShapeDtypeStruct((many, channels), F32)],
                2 * many * width * channels,
                "d_gated",
            ),
            w_mix_out,
            *whole_d[i].parts(),
        )
        d_gated.append(d_i.reshape(n_tensor, piece, channels))
    scanned = recurrence_call(
        backward_kernel,
        order[::-1],
        offsets,
        [pre, before, *d_gated[:-1], after(d_gated[-1], sequence.last)],
        [jax.ShapeDtypeStruct((n_tensor, piece, 3 * channels), BF)] * CHUNKS
        + [jax.ShapeDtypeStruct((n_tensor, rows, 3 * channels), BF)],
        channels,
        "recurrence_backward",
    )
    d_pieces, d_pre = scanned[:-1], scanned[-1]
    sequence.last = d_pre
    d_flat = d_pre.reshape(n_tensor * rows, 3 * channels)
    sums_one = [
        SummedRows(sequence, d.reshape(-1, 3 * channels), w_mix_in, n_tensor, piece) for d in d_pieces
    ]
    grad_mi = []

    def grad_mix_in(k):
        halves = grad(
            whole_one, [d_flat], "left", depth, "grad_mix_in", fixed=(k, 3), owner=owner
        )
        grad_mi.append(SummedGrad(sequence, halves, n_dp, near_first))

    def grad_mix_out():
        halves = grad(
            [g.reshape(-1, channels) for g in gated],
            listed(whole_d),
            "right",
            depth,
            "grad_mix_out",
            owner=owner,
        )
        return SummedGrad(sequence, halves, n_dp, near_first)

    moments = [None] * 7

    def lamb(at, grad):
        tall, wide = weights[at].shape

        def call(kept, *coming):
            if coming:
                total = kept[0].astype(F32) + coming[0][0].astype(F32)
            else:
                total = kept.astype(F32)
            first, second, update = adam_moments(
                total[:tall, :wide], weights[at], firsts[at], seconds[at], WEIGHT_DECAY
            )
            return update, first, second, jnp.sum(update * update)

        if isinstance(grad, SummedGrad):
            grad.steps()
            update, first, second, square = run(call, grad.kept, grad.coming)
        else:
            update, first, second, square = run(call, grad)
        moments[at] = (first, second, update, square)

    firsts = [mix_in_m[0], mix_in_m[1], mix_in_m[2], mix_out_m, ffn_in_m[0], ffn_in_m[1], ffn_out_m]
    seconds = [mix_in_v[0], mix_in_v[1], mix_in_v[2], mix_out_v, ffn_in_v[0], ffn_in_v[1], ffn_out_v]
    grad_mix_in(0)
    for i in pieces:
        sums_one[i].high()
    grad_mix_in(1)
    sums_one[0].rest()
    grad_mi[0].step()
    grad_mix_in(2)
    for i in range(1, CHUNKS):
        sums_one[i].rest()
    grad_mi[1].step()
    grad_mi[0].step()
    grad_mo = grad_mix_out()
    mixed = run(
        lambda *parts: jnp.concatenate(
            [
                m + k + c.astype(F32)
                for m, k, c in zip(parts[:CHUNKS], parts[CHUNKS : 2 * CHUNKS], parts[2 * CHUNKS :])
            ],
            axis=0,
        ).astype(BF),
        *middle,
        *[v.kept for v in downs],
        *[v.coming for v in downs],
    )
    lamb(6, grad_fo)
    grad_mi[1].step()

    def input_back(kept, coming, own, scaling, d_mid):
        unit_rows = own.astype(F32) * scaling
        d_norm, gain = norm_backward(kept + coming.astype(F32), unit_rows, scaling, gains[0])
        return d_mid + d_norm, gain

    input_grad, gain_one = [], 0.0
    for i in pieces:
        at = cut(i)
        grad_i, gain_i = run(
            input_back, sums_one[i].kept, sums_one[i].coming, tokens[at], scale_one[at], d_middle[i]
        )
        gain_one = gain_one + gain_i
        input_grad.append(grad_i)
        if i == 0:
            lamb(0, grad_mi[0])
            grad_mo.step()
            grad_mi[2].step()
    input_grad = jnp.concatenate(input_grad, axis=0)
    gain_grads = jnp.stack([gain_one, gain_two])
    grad_mo.step()
    lamb(1, grad_mi[1])
    lamb(4, grad_fi[:, :units])
    lamb(5, grad_fi[:, units:])
    lamb(2, grad_mi[2])
    lamb(3, grad_mo)
    squares = jnp.concatenate([weight_sq, jnp.stack([m[3] for m in moments])])
    packed = jnp.concatenate([gain_grads.reshape(-1), jnp.pad(squares, (0, SUB * LANES - 14))])
    packed = total_over_mesh(packed.reshape(-1, LANES), n_dp, n_tensor).reshape(-1)
    gain_grads = packed[: 2 * width].reshape(2, width)
    squares = packed[2 * width : 2 * width + 14].reshape(2, 7)
    gn_first, gn_second, gn_update = adam_moments(gain_grads, gains, gains_m, gains_v, 0.0)
    weight_sq = jnp.concatenate([squares[0], jnp.sum(gains * gains, axis=1)])
    update_sq = jnp.concatenate([squares[1], jnp.sum(gn_update * gn_update, axis=1)])
    trust = jnp.sqrt(weight_sq) / jnp.sqrt(update_sq + NORM_EPSILON)
    nexts = [w - LEARN_RATE * trust[i] * moments[i][2] for i, w in enumerate(weights)]
    gains_next = gains - LEARN_RATE * trust[7:9][:, None] * gn_update
    layer_norms = jnp.stack([jnp.sqrt(weight_sq), jnp.sqrt(update_sq)])

    def grouped(values):
        return (jnp.stack(values[0:3]), values[3], jnp.stack(values[4:6]), values[6])

    return (
        (mixed, input_grad)
        + grouped(nexts)
        + (gains_next,)
        + grouped([m[0] for m in moments])
        + (gn_first,)
        + grouped([m[1] for m in moments])
        + (gn_second,)
        + grouped([n.astype(BF) for n in nexts])
        + (layer_norms,)
    )


def solution(mesh):
    rows = P(("dp", "tensor"), None)
    inner = P(None, "dp", "tensor")
    outer = P("tensor", "dp")
    matrices = (inner, outer, inner, outer)
    in_specs = (rows, rows, P("dp", None)) + (matrices + (P(),)) * 3
    out_specs = (rows, rows) + (matrices + (P(),)) * 3 + matrices + (P(),)
    body = functools.partial(per_device, mesh.shape["dp"], mesh.shape["tensor"])
    return jax.shard_map(
        body, mesh=mesh, in_specs=in_specs, out_specs=out_specs, check_vma=False
    )
```

time: 1600 us -> 1050 us (0.66)
  waiting for transfers between devices: 733 us -> 293 us
  matrix products: 457 us -> 68.8 us
  Pallas kernels: 54.4 us -> 438 us
  starting transfers between devices: 179 us -> 65 us
    ppermute x119 -> x71, waiting for transfers between devices: 733 us -> 293 us  [exchange(): return lax.ppermute(value, axis, [(i, i ^ offset) for i in range(size)])]
    pallas_call x6 -> x25, Pallas kernels: 13.6 us -> 395 us  [the longest x11 167 us: row_tiles(): pl.pallas_call(body, grid=(count,), in_specs=[pl.BlockSpec(memory_space=p...]
    dot_general x30 -> x0, matrix products: 292 us -> none  [the longest x19 165 us: mm(): return jnp.dot(a, b, preferred_element_type=F32)]
    ppermute x119 -> x71, starting transfers between devices: 179 us -> 64.7 us  [exchange(): return lax.ppermute(value, axis, [(i, i ^ offset) for i in range(size)])]
    dot_general x22 -> x8, matrix products: 165 us -> 68.8 us  [mm_nt(): lax.dot_general(a, b, (((1,), (1,)), ((), ())), preferred_element_type=F32)]
    unnamed x396 -> x241, local copies, waits for them, and re-layouts: 45.2 us -> 19.7 us
    dynamic_update_slice x0 -> x16, local copies, waits for them, and re-layouts: none -> 19.2 us  [the longest x7 12.4 us: per_device(): w_mix_in = lax.dynamic_update_slice(w_mix_in, block, (place * depth, 0))]
    reduce_sum x4 -> x16, other arithmetic: 15.6 us -> 32.6 us  [the longest x7 18.8 us: call(): return (update, first, second, jnp.sum(update * update))]
  transfers between devices with their start and end apart: 119 -> 75, of which waited for: 51 -> 22; matrix products, arithmetic and copies ran while one was open for 29% -> 17% of each run, Pallas kernels for 2% -> 42%
where the time goes in v2:
time: 1050 us; the launch traced here: 1040 us
  Pallas kernels  438 us (42%)
  waiting for transfers between devices  293 us (28%)
  other arithmetic  94.8 us (9%)
  matrix products  68.8 us (7%)
  local copies, waits for them, and re-layouts  65.2 us (6%)
  starting transfers between devices  65 us (6%)
  between operations  20.1 us (2%)
    ppermute x71, waiting for transfers between devices, exchange(): return lax.ppermute(value, axis, [(i, i ^ offset) for i in range(size)])  293 us
    pallas_call x11, Pallas kernels, row_tiles(): pl.pallas_call(body, grid=(count,), in_specs=[pl.BlockSpec(memory_space=p...  167 us
    pallas_call x8, Pallas kernels, near_added(): pl.pallas_call(kernel, grid=(2,), in_specs=[rowed(operand), pl.BlockSpec(...  96.1 us
    pallas_call x2, Pallas kernels, grad_kernel(): pl.pallas_call(kernel, grid=(steps,), in_specs=in_specs, out_specs=pl.Blo...  72.4 us
    dot_general x8, matrix products, mm_nt(): lax.dot_general(a, b, (((1,), (1,)), ((), ())), preferred_element_type=F32)  68.8 us
    ppermute x71, starting transfers between devices, exchange(): return lax.ppermute(value, axis, [(i, i ^ offset) for i in range(size)])  64.7 us
    pallas_call x4, Pallas kernels, grad_kernel(): pl.pallas_call(kernel_by_place, grid_spec=pltpu.PrefetchScalarGridSpec(nu...  59.9 us
    pallas_call x2, Pallas kernels, recurrence_call(): pl.pallas_call(kernel, grid_spec=pltpu.PrefetchScalarGridSpec(num_scalar_...  42.9 us
  transfers between devices with their start and end apart: 75, of which 22 were waited for; matrix products, arithmetic and copies ran while one was open for 17% of the time, Pallas kernels for 42%

profile of v2, /device:TPU:0, one launch (start us, length us, event | category | flops | bytes accessed | tf_op | source)
XLA Modules:
  0.0 1044.9 jit_solution(17753039180887836835)
XLA Ops:
  21.5 17.3 %collective-permute-done.3 = bf16[256,1536]{1,0:T(8,128)(2,1)} collective-permute-done((bf16[256,1536]{1,0:T(8,128)(2,1)S(1)}, bf16[256,1536]{1,0:T(8,128)(2,1)}, u32[]{:S(2)}, u32[]{:S(2)}) %collective-permute-start.3) | collective-permute-done | bytes 786464 | tf_op jit(solution)/shard_map/ppermute | solution.py:31
  38.8 15.5 %collective-permute-done.2 = bf16[256,1536]{1,0:T(8,128)(2,1)} collective-permute-done((bf16[256,1536]{1,0:T(8,128)(2,1)S(1)}, bf16[256,1536]{1,0:T(8,128)(2,1)}, u32[]{:S(2)}, u32[]{:S(2)}) %collective-permute-start.2) | collective-permute-done | bytes 786464 | tf_op jit(solution)/shard_map/ppermute | solution.py:31
  68.4 25.6 %collective-permute-done.7 = bf16[256,1536]{1,0:T(8,128)(2,1)} collective-permute-done((bf16[256,1536]{1,0:T(8,128)(2,1)S(1)}, bf16[256,1536]{1,0:T(8,128)(2,1)}, u32[]{:S(2)}, u32[]{:S(2)}) %collective-permute-start.7) | collective-permute-done | bytes 786464 | tf_op jit(solution)/shard_map/ppermute | solution.py:31
  144.8 26.6 %pre.1 = f32[3072,1536]{1,0:T(8,128)} custom-call(bf16[384,2048]{1,0:T(8,128)(2,1)} %copy-done.59, bf16[384,2048]{1,0:T(8,128)(2,1)} %copy-done.58, bf16[384,2048]{1,0:T(8,128)(2,1)} %copy-done.103, bf16[384,2048]{1,0:T(8,128)(2,1)} %collective-permute-done.4.refs_3_, bf16[384,2048]{1,0:T(8,128)(2,1)} %collective-permute-done.8.refs_4_, ...), custom_call_target="tpu_custom_call" | custom-call | flops 34923765760 | bytes 12582912 | tf_op jit(solution)/shard_map/pre/pallas_call | solution.py:264
  171.4 18.9 %recurrence_forward.1 = (f32[4,768,512]{2,1,0:T(8,128)}, bf16[4,384,512]{2,1,0:T(8,128)(2,1)S(1)}, bf16[4,384,512]{2,1,0:T(8,128)(2,1)S(1)}) custom-call(s32[4]{0:T(128)S(1)} %gather_fusion, s32[4]{0:T(128)S(1)} %bitcast_subtract_fusion.2.offsets, f32[4,768,1536]{2,1,0:T(8,128)} %bitcast.256), custom_call_target="tpu_custom_call" | custom-call | flops 23592960000 | bytes 37748736 | tf_op jit(solution)/shard_map/recurrence_forward/pallas_call | solution.py:556
  221.4 35.4 %collective-permute-done.24 = bf16[384,2048]{1,0:T(8,128)(2,1)S(1)} collective-permute-done((bf16[384,2048]{1,0:T(8,128)(2,1)}, bf16[384,2048]{1,0:T(8,128)(2,1)S(1)}, u32[]{:S(2)}, u32[]{:S(2)}) %collective-permute-start.24) | collective-permute-done | bytes 1572896 | tf_op jit(solution)/shard_map/ppermute | solution.py:31
  256.8 33.0 %collective-permute-done.22 = bf16[384,2048]{1,0:T(8,128)(2,1)S(1)} collective-permute-done((bf16[384,2048]{1,0:T(8,128)(2,1)}, bf16[384,2048]{1,0:T(8,128)(2,1)S(1)}, u32[]{:S(2)}, u32[]{:S(2)}) %collective-permute-start.22) | collective-permute-done | bytes 1572896 | tf_op jit(solution)/shard_map/ppermute | solution.py:31
  302.4 26.7 %collective-permute-done.25.refs_1_ = bf16[384,2048]{1,0:T(8,128)(2,1)} collective-permute-done((bf16[384,2048]{1,0:T(8,128)(2,1)}, bf16[384,2048]{1,0:T(8,128)(2,1)}, u32[]{:S(2)}, u32[]{:S(2)}) %collective-permute-start.25) | collective-permute-done | bytes 1572896 | tf_op jit(solution)/shard_map/ppermute | solution.py:31
  330.6 18.8 %gate_up.4 = (bf16[768,1408]{1,0:T(8,128)(2,1)}, bf16[768,1408]{1,0:T(8,128)(2,1)}, bf16[768,1408]{1,0:T(8,128)(2,1)}) custom-call(bf16[384,2048]{1,0:T(8,128)(2,1)} %multiply_convert_fusion.1.refs_0_, bf16[384,2048]{1,0:T(8,128)(2,1)} %collective-permute-done.25.refs_1_, bf16[2048,2816]{1,0:T(8,128)(2,1)} %all-gather.5.cloned.1.call-done.refs_2_.w), custom_call_target="tpu_custom_call" | custom-call | flops 18173392896 | bytes 23068672 | tf_op jit(solution)/shard_map/gate_up/pallas_call | solution.py:264
  349.4 18.8 %gate_up.5 = (bf16[768,1408]{1,0:T(8,128)(2,1)}, bf16[768,1408]{1,0:T(8,128)(2,1)}, bf16[768,1408]{1,0:T(8,128)(2,1)}) custom-call(bf16[384,2048]{1,0:T(8,128)(2,1)} %collective-permute-done.27.refs_0_.refs_2_, bf16[384,2048]{1,0:T(8,128)(2,1)} %collective-permute-done.28.refs_1_.refs_3_, bf16[2048,2816]{1,0:T(8,128)(2,1)} %all-gather.5.cloned.1.call-done.refs_2_.w), custom_call_target="tpu_custom_call" | custom-call | flops 18173392896 | bytes 23068672 | tf_op jit(solution)/shard_map/gate_up/pallas_call | solution.py:264
  369.6 18.6 %gate_up.6 = (bf16[768,1408]{1,0:T(8,128)(2,1)}, bf16[768,1408]{1,0:T(8,128)(2,1)}, bf16[768,1408]{1,0:T(8,128)(2,1)}) custom-call(bf16[384,2048]{1,0:T(8,128)(2,1)} %copy-done.62, bf16[384,2048]{1,0:T(8,128)(2,1)} %collective-permute-done.26.refs_1_.refs_5_, bf16[2048,2816]{1,0:T(8,128)(2,1)} %all-gather.5.cloned.1.call-done.refs_2_.w), custom_call_target="tpu_custom_call" | custom-call | flops 18173392896 | bytes 23068672 | tf_op jit(solution)/shard_map/gate_up/pallas_call | solution.py:264
  389.4 19.0 %gate_up.7 = (bf16[768,1408]{1,0:T(8,128)(2,1)}, bf16[768,1408]{1,0:T(8,128)(2,1)}, bf16[768,1408]{1,0:T(8,128)(2,1)}) custom-call(bf16[384,2048]{1,0:T(8,128)(2,1)} %collective-permute-done.31.refs_0_.refs_6_, bf16[384,2048]{1,0:T(8,128)(2,1)} %copy-done.106, bf16[2048,2816]{1,0:T(8,128)(2,1)} %all-gather.5.cloned.1.call-done.refs_2_.w), custom_call_target="tpu_custom_call" | custom-call | flops 18173392896 | bytes 23068672 | tf_op jit(solution)/shard_map/gate_up/pallas_call | solution.py:264
  413.2 25.7 %grad_out.1 = bf16[1408,2048]{1,0:T(8,128)(2,1)} custom-call(bf16[384,2048]{1,0:T(8,128)(2,1)} %copy-done.61, bf16[384,2048]{1,0:T(8,128)(2,1)} %copy-done.104, bf16[384,2048]{1,0:T(8,128)(2,1)} %collective-permute-done.34.refs_2_.refs_0_, bf16[384,2048]{1,0:T(8,128)(2,1)} %copy-done.108, bf16[384,2048]{1,0:T(8,128)(2,1)} %get-tuple-element.231.refs_4_.refs_0_, ...), custom_call_target="tpu_custom_call" | custom-call | flops 32346783744 | bytes 5767168 | tf_op jit(solution)/shard_map/grad_out/pallas_call | solution.py:380
  439.0 11.9 %gate_up_back.4.refs_9_ = bf16[768,2816]{1,0:T(8,128)(2,1)} custom-call(bf16[384,2048]{1,0:T(8,128)(2,1)} %collective-permute-done.34.refs_2_.refs_0_, bf16[384,2048]{1,0:T(8,128)(2,1)} %copy-done.108, bf16[2048,1408]{1,0:T(8,128)(2,1)} %all-gather.3.cloned.1.call-done.refs_2_.w, bf16[768,1408]{1,0:T(8,128)(2,1)} %get-tuple-element.241.refs_3_, ...), custom_call_target="tpu_custom_call" | custom-call | flops 11086696448 | bytes 11534336 | tf_op jit(solution)/shard_map/gate_up_back/pallas_call | solution.py:264
  450.9 14.5 %convolution_convert_fusion.7 = bf16[768,2048]{1,0:T(8,128)(2,1)} fusion(bf16[768,2816]{1,0:T(8,128)(2,1)} %gate_up_back.4.refs_9_, bf16[2048,2816]{1,0:T(8,128)(2,1)} %all-gather.5.cloned.1.call-done.refs_2_.w), kind=kOutput, calls=%fused_computation.23 | convolution fusion | flops 8859942912 | bytes 19005440 | tf_op jit(solution)/shard_map/dot_general | solution.py:43
  465.7 12.0 %gate_up_back.5.refs_11_ = bf16[768,2816]{1,0:T(8,128)(2,1)} custom-call(bf16[384,2048]{1,0:T(8,128)(2,1)} %collective-permute-done.29.refs_6_.refs_0_, bf16[384,2048]{1,0:T(8,128)(2,1)} %copy-done.109, bf16[2048,1408]{1,0:T(8,128)(2,1)} %all-gather.3.cloned.1.call-done.refs_2_.w, bf16[768,1408]{1,0:T(8,128)(2,1)} %get-tuple-element.245.refs_3_, ...), custom_call_target="tpu_custom_call" | custom-call | flops 11086696448 | bytes 11534336 | tf_op jit(solution)/shard_map/gate_up_back/pallas_call | solution.py:264
  477.7 14.4 %convolution_convert_fusion.6 = bf16[768,2048]{1,0:T(8,128)(2,1)} fusion(bf16[768,2816]{1,0:T(8,128)(2,1)} %gate_up_back.5.refs_11_, bf16[2048,2816]{1,0:T(8,128)(2,1)} %all-gather.5.cloned.1.call-done.refs_2_.w), kind=kOutput, calls=%fused_computation.22 | convolution fusion | flops 8859942912 | bytes 19005440 | tf_op jit(solution)/shard_map/dot_general | solution.py:43
  492.4 11.8 %gate_up_back.6.v.refs_8_ = bf16[768,2816]{1,0:T(8,128)(2,1)} custom-call(bf16[384,2048]{1,0:T(8,128)(2,1)} %copy-done.61, bf16[384,2048]{1,0:T(8,128)(2,1)} %copy-done.104, bf16[2048,1408]{1,0:T(8,128)(2,1)} %all-gather.3.cloned.1.call-done.refs_2_.w, bf16[768,1408]{1,0:T(8,128)(2,1)} %get-tuple-element.249.refs_3_, ...), custom_call_target="tpu_custom_call" | custom-call | flops 11086696448 | bytes 11534336 | tf_op jit(solution)/shard_map/gate_up_back/pallas_call | solution.py:264
  505.9 17.4 %near_added.10 = (bf16[384,2048]{1,0:T(8,128)(2,1)}, f32[384,2048]{1,0:T(8,128)}) custom-call(bf16[768,2816]{1,0:T(8,128)(2,1)} %gate_up_back.6.v.refs_8_, bf16[2048,2816]{1,0:T(8,128)(2,1)} %all-gather.5.cloned.1.call-done.refs_2_.w, bf16[768,2048]{1,0:T(8,128)(2,1)} %copy-done.101), custom_call_target="tpu_custom_call" | custom-call | flops 18173392896 | bytes 11534336 | tf_op jit(solution)/shard_map/near_added/pallas_call | solution.py:185
  536.7 17.6 %near_added.11 = (bf16[384,2048]{1,0:T(8,128)(2,1)}, f32[384,2048]{1,0:T(8,128)}) custom-call(bf16[768,2816]{1,0:T(8,128)(2,1)} %gate_up_back.7.v.refs_10_, bf16[2048,2816]{1,0:T(8,128)(2,1)} %all-gather.5.cloned.1.call-done.refs_2_.w, bf16[768,2048]{1,0:T(8,128)(2,1)} %copy-done.100), custom_call_target="tpu_custom_call" | custom-call | flops 18173392896 | bytes 11534336 | tf_op jit(solution)/shard_map/near_added/pallas_call | solution.py:185
  572.8 46.7 %grad_in.1 = bf16[2048,2816]{1,0:T(8,128)(2,1)} custom-call(bf16[384,2048]{1,0:T(8,128)(2,1)} %multiply_convert_fusion.1.refs_0_, bf16[384,2048]{1,0:T(8,128)(2,1)} %collective-permute-done.25.refs_1_, bf16[384,2048]{1,0:T(8,128)(2,1)} %collective-permute-done.27.refs_0_.refs_2_, bf16[384,2048]{1,0:T(8,128)(2,1)} %collective-permute-done.28.refs_1_.refs_3_, ...), custom_call_target="tpu_custom_call" | custom-call | flops 60693569536 | bytes 11534336 | tf_op jit(solution)/shard_map/grad_in/pallas_call | solution.py:380
  642.6 11.9 %near_added.12 = (bf16[384,2048]{1,0:T(8,128)(2,1)}, f32[384,2048]{1,0:T(8,128)}) custom-call(bf16[768,1408]{1,0:T(8,128)(2,1)} %get-tuple-element.268.refs_8_.v, bf16[2048,1408]{1,0:T(8,128)(2,1)} %all-gather.3.cloned.1.call-done.refs_2_.w, bf16[768,2048]{1,0:T(8,128)(2,1)} %collective-permute-done.42.n), custom_call_target="tpu_custom_call" | custom-call | flops 11086696448 | bytes 5767168 | tf_op jit(solution)/shard_map/near_added/pallas_call | solution.py:185
  672.0 33.1 %collective-permute-done.45.refs_1_.refs_5_ = bf16[384,2048]{1,0:T(8,128)(2,1)} collective-permute-done((bf16[384,2048]{1,0:T(8,128)(2,1)S(1)}, bf16[384,2048]{1,0:T(8,128)(2,1)}, u32[]{:S(2)}, u32[]{:S(2)}) %collective-permute-start.45) | collective-permute-done | bytes 1572896 | tf_op jit(solution)/shard_map/ppermute | solution.py:31
  726.0 24.0 %recurrence_backward.1 = (bf16[4,384,1536]{2,1,0:T(8,128)(2,1)}, bf16[4,384,1536]{2,1,0:T(8,128)(2,1)}, bf16[4,768,1536]{2,1,0:T(8,128)(2,1)}) custom-call(s32[4]{0:T(128)S(1)} %rev.3.order, s32[4]{0:T(128)S(1)} %copy-done.4, f32[4,768,1536]{2,1,0:T(8,128)} %bitcast.257, f32[4,768,512]{2,1,0:T(8,128)} %get-tuple-element.207.before, ...), custom_call_target="tpu_custom_call" | custom-call | flops 23592960000 | bytes 37748736 | tf_op jit(solution)/shard_map/recurrence_backward/pallas_call | solution.py:556
  750.0 15.4 %grad_mix_in.3 = (bf16[4,256,512]{2,1,0:T(8,128)(2,1)}, bf16[4,256,512]{2,1,0:T(8,128)(2,1)}) custom-call(s32[8]{0:T(128)} %stack.158.owners_ref, bf16[384,2048]{1,0:T(8,128)(2,1)} %copy-done.59, bf16[384,2048]{1,0:T(8,128)(2,1)} %copy-done.58, bf16[384,2048]{1,0:T(8,128)(2,1)} %copy-done.103, bf16[384,2048]{1,0:T(8,128)(2,1)} %collective-permute-done.4.refs_3_, ...), custom_call_target="tpu_custom_call" | custom-call | flops 14307921920 | bytes 2097152 | tf_op jit(solution)/shard_map/grad_mix_in/pallas_call | solution.py:404
  787.3 14.6 %grad_mix_in.4 = (bf16[4,256,512]{2,1,0:T(8,128)(2,1)}, bf16[4,256,512]{2,1,0:T(8,128)(2,1)}) custom-call(s32[8]{0:T(128)} %stack.158.owners_ref, bf16[384,2048]{1,0:T(8,128)(2,1)} %copy-done.59, bf16[384,2048]{1,0:T(8,128)(2,1)} %copy-done.58, bf16[384,2048]{1,0:T(8,128)(2,1)} %copy-done.103, bf16[384,2048]{1,0:T(8,128)(2,1)} %collective-permute-done.4.refs_3_, ...), custom_call_target="tpu_custom_call" | custom-call | flops 14307921920 | bytes 2097152 | tf_op jit(solution)/shard_map/grad_mix_in/pallas_call | solution.py:404
  816.8 14.5 %grad_mix_in.5 = (bf16[4,256,512]{2,1,0:T(8,128)(2,1)}, bf16[4,256,512]{2,1,0:T(8,128)(2,1)}) custom-call(s32[8]{0:T(128)} %stack.158.owners_ref, bf16[384,2048]{1,0:T(8,128)(2,1)} %copy-done.59, bf16[384,2048]{1,0:T(8,128)(2,1)} %copy-done.58, bf16[384,2048]{1,0:T(8,128)(2,1)} %copy-done.103, bf16[384,2048]{1,0:T(8,128)(2,1)} %collective-permute-done.4.refs_3_, ...), custom_call_target="tpu_custom_call" | custom-call | flops 14307921920 | bytes 2097152 | tf_op jit(solution)/shard_map/grad_mix_in/pallas_call | solution.py:404
  831.6 11.9 %near_added.15 = (bf16[384,2048]{1,0:T(8,128)(2,1)}, f32[384,2048]{1,0:T(8,128)}) custom-call(bf16[1536,1536]{1,0:T(8,128)(2,1)} %bitcast.261, bf16[2048,1536]{1,0:T(8,128)(2,1)} %constant_dynamic-update-slice_fusion.8.refs_8_.w, bf16[768,2048]{1,0:T(8,128)(2,1)} %collective-permute-done.50.n), custom_call_target="tpu_custom_call" | custom-call | flops 11730940928 | bytes 6291456 | tf_op jit(solution)/shard_map/near_added/pallas_call | solution.py:185
  851.0 15.4 %grad_mix_out.1 = (bf16[4,512,256]{2,1,0:T(8,128)(2,1)}, bf16[4,512,256]{2,1,0:T(8,128)(2,1)}) custom-call(s32[8]{0:T(128)} %stack.158.owners_ref, bf16[384,2048]{1,0:T(8,128)(2,1)} %get-tuple-element.373.refs_0_, bf16[384,2048]{1,0:T(8,128)(2,1)} %collective-permute-done.40.refs_1_, bf16[384,2048]{1,0:T(8,128)(2,1)} %collective-permute-done.41.refs_2_, ...), custom_call_target="tpu_custom_call" | custom-call | flops 14307921920 | bytes 2097152 | tf_op jit(solution)/shard_map/grad_mix_out/pallas_call | solution.py:404
  880.3 33.0 %collective-permute-done.56 = bf16[384,2048]{1,0:T(8,128)(2,1)S(1)} collective-permute-done((bf16[384,2048]{1,0:T(8,128)(2,1)}, bf16[384,2048]{1,0:T(8,128)(2,1)S(1)}, u32[]{:S(2)}, u32[]{:S(2)}) %collective-permute-start.56) | collective-permute-done | bytes 1572896 | tf_op jit(solution)/shard_map/ppermute | solution.py:31
  931.6 16.6 %collective-permute-done.61 = bf16[2,512,256]{2,1,0:T(8,128)(2,1)S(1)} collective-permute-done((bf16[2,512,256]{2,1,0:T(8,128)(2,1)S(1)}, bf16[2,512,256]{2,1,0:T(8,128)(2,1)S(1)}, u32[]{:S(2)}, u32[]{:S(2)}) %collective-permute-start.61) | collective-permute-done | bytes 524320 | tf_op jit(solution)/shard_map/ppermute | solution.py:31
  966.4 15.1 %collective-permute-done.64 = bf16[1,256,512]{2,1,0:T(8,128)(2,1)S(1)} collective-permute-done((bf16[1,256,512]{2,1,0:T(8,128)(2,1)S(1)}, bf16[1,256,512]{2,1,0:T(8,128)(2,1)S(1)}, u32[]{:S(2)}, u32[]{:S(2)}) %collective-permute-start.64) | collective-permute-done | bytes 262176 | tf_op jit(solution)/shard_map/ppermute | solution.py:31
  (520 shorter events, 373.2 us)
Async XLA Ops:
  7.2 323.4 %all-gather.5.cloned.1.call-start = ((), (), s32[]{:S(2)}) async-start(), calls=%async_computation.3 | async-start | bytes 12976128 | tf_op jit(solution)/shard_map/all_gather | solution.py:707
  13.4 40.9 %collective-permute-start = (bf16[384,2048]{1,0:T(8,128)(2,1)S(1)}, bf16[384,2048]{1,0:T(8,128)(2,1)S(1)}, u32[]{:S(2)}, u32[]{:S(2)}) collective-permute-start(bf16[384,2048]{1,0:T(8,128)(2,1)S(1)} %get-tuple-element.292.refs_0_), channel_id=1, source_target_pairs={{0,2},{1,3},{2,0},{3,1},{4,6},{5,7},{6,4},{7,5},{8,10},{9,11},{10,... | collective-permute-start | bytes 4718600 | tf_op jit(solution)/shard_map/ppermute | solution.py:31
  54.3 39.7 %collective-permute-start.4 = (bf16[384,2048]{1,0:T(8,128)(2,1)S(1)}, bf16[384,2048]{1,0:T(8,128)(2,1)}, u32[]{:S(2)}, u32[]{:S(2)}) collective-permute-start(bf16[384,2048]{1,0:T(8,128)(2,1)S(1)} %get-tuple-element.183.refs_1_), channel_id=1, source_target_pairs={{0,2},{1,3},{2,0},{3,1},{4,6},{5,7},{6,4},{7,5},{8,10},{9,11},{10,... | collective-permute-start | bytes 4718600 | tf_op jit(solution)/shard_map/ppermute | solution.py:31
  134.4 304.6 %all-gather.3.cloned.1.call-start = ((), (), s32[]{:S(2)}) async-start(), calls=%async_computation.2 | async-start | bytes 6488064 | tf_op jit(solution)/shard_map/all_gather | solution.py:708
  139.5 55.0 %collective-permute-start.17 = (bf16[256,512]{1,0:T(8,128)(2,1)}, bf16[256,512]{1,0:T(8,128)(2,1)S(1)}, u32[]{:S(2)}, u32[]{:S(2)}) collective-permute-start(bf16[256,512]{1,0:T(8,128)(2,1)} %bitcast.191), channel_id=1, source_target_pairs={{0,4},{4,0},{8,12},{12,8},{16,20},{20,16},{24,28},{28,24},{1,5},{5... | collective-permute-start | bytes 786440 | tf_op jit(solution)/shard_map/ppermute | solution.py:31
  140.0 54.6 %collective-permute-start.18 = (bf16[256,512]{1,0:T(8,128)(2,1)}, bf16[256,512]{1,0:T(8,128)(2,1)S(1)}, u32[]{:S(2)}, u32[]{:S(2)}) collective-permute-start(bf16[256,512]{1,0:T(8,128)(2,1)} %collective-permute-done.13), channel_id=1, source_target_pairs={{0,4},{4,0},{8,12},{12,8},{16,20},{20,16},{24,28},{28,24},{1,5},{5... | collective-permute-start | bytes 786440 | tf_op jit(solution)/shard_map/ppermute | solution.py:31
  141.5 53.1 %collective-permute-start.19 = (bf16[256,512]{1,0:T(8,128)(2,1)}, bf16[256,512]{1,0:T(8,128)(2,1)S(1)}, u32[]{:S(2)}, u32[]{:S(2)}) collective-permute-start(bf16[256,512]{1,0:T(8,128)(2,1)} %collective-permute-done.14), channel_id=1, source_target_pairs={{0,4},{4,0},{8,12},{12,8},{16,20},{20,16},{24,28},{28,24},{1,5},{5... | collective-permute-start | bytes 786440 | tf_op jit(solution)/shard_map/ppermute | solution.py:31
  142.0 52.6 %collective-permute-start.20 = (bf16[256,512]{1,0:T(8,128)(2,1)}, bf16[256,512]{1,0:T(8,128)(2,1)S(1)}, u32[]{:S(2)}, u32[]{:S(2)}) collective-permute-start(bf16[256,512]{1,0:T(8,128)(2,1)} %collective-permute-done.15), channel_id=1, source_target_pairs={{0,4},{4,0},{8,12},{12,8},{16,20},{20,16},{24,28},{28,24},{1,5},{5... | collective-permute-start | bytes 786440 | tf_op jit(solution)/shard_map/ppermute | solution.py:31
  143.6 51.2 %collective-permute-start.16 = (bf16[384,2048]{1,0:T(8,128)(2,1)S(1)}, bf16[384,2048]{1,0:T(8,128)(2,1)S(1)}, u32[]{:S(2)}, u32[]{:S(2)}) collective-permute-start(bf16[384,2048]{1,0:T(8,128)(2,1)S(1)} %get-tuple-element.205.refs_0_), channel_id=1, source_target_pairs={{0,2},{1,3},{2,0},{3,1},{4,6},{5,7},{6,4},{7,5},{8,10},{9,11},{10,... | collective-permute-start | bytes 4718600 | tf_op jit(solution)/shard_map/ppermute | solution.py:31
  220.8 69.0 %collective-permute-start.22 = (bf16[384,2048]{1,0:T(8,128)(2,1)}, bf16[384,2048]{1,0:T(8,128)(2,1)S(1)}, u32[]{:S(2)}, u32[]{:S(2)}) collective-permute-start(bf16[384,2048]{1,0:T(8,128)(2,1)} %get-tuple-element.217), channel_id=1, source_target_pairs={{0,2},{1,3},{2,0},{3,1},{4,6},{5,7},{6,4},{7,5},{8,10},{9,11},{10,... | collective-permute-start | bytes 4718600 | tf_op jit(solution)/shard_map/ppermute | solution.py:31
  296.8 275.9 %reduce-scatter.3.cloned.1.call-start = ((), (), s32[]{:S(2)}) async-start(), calls=%async_computation.4 | async-start | bytes 6488064 | tf_op jit(solution)/shard_map/reduce_scatter | solution.py:811
  296.9 112.1 %collective-permute-start.34 = (bf16[384,2048]{1,0:T(8,128)(2,1)}, bf16[384,2048]{1,0:T(8,128)(2,1)}, u32[]{:S(2)}, u32[]{:S(2)}) collective-permute-start(bf16[384,2048]{1,0:T(8,128)(2,1)} %copy-done.61), channel_id=1, source_target_pairs={{0,1},{1,0},{2,3},{3,2},{4,5},{5,4},{6,7},{7,6},{8,9},{9,8},{10,11... | collective-permute-start | bytes 4718600 | tf_op jit(solution)/shard_map/ppermute | solution.py:31
  297.0 52.4 %collective-permute-start.27 = (bf16[384,2048]{1,0:T(8,128)(2,1)}, bf16[384,2048]{1,0:T(8,128)(2,1)}, u32[]{:S(2)}, u32[]{:S(2)}) collective-permute-start(bf16[384,2048]{1,0:T(8,128)(2,1)} %multiply_convert_fusion.1.refs_0_), channel_id=1, source_target_pairs={{0,1},{1,0},{2,3},{3,2},{4,5},{5,4},{6,7},{7,6},{8,9},{9,8},{10,11... | collective-permute-start | bytes 4718600 | tf_op jit(solution)/shard_map/ppermute | solution.py:31
  329.1 59.1 %collective-permute-start.31 = (bf16[384,2048]{1,0:T(8,128)(2,1)S(1)}, bf16[384,2048]{1,0:T(8,128)(2,1)}, u32[]{:S(2)}, u32[]{:S(2)}) collective-permute-start(bf16[384,2048]{1,0:T(8,128)(2,1)S(1)} %multiply_convert_fusion.refs_0_.refs_4_), channel_id=1, source_target_pairs={{0,1},{1,0},{2,3},{3,2},{4,5},{5,4},{6,7},{7,6},{8,9},{9,8},{10,11... | collective-permute-start | bytes 4718600 | tf_op jit(solution)/shard_map/ppermute | solution.py:31
  368.2 40.2 %collective-permute-start.30 = (bf16[384,2048]{1,0:T(8,128)(2,1)S(1)}, bf16[384,2048]{1,0:T(8,128)(2,1)S(1)}, u32[]{:S(2)}, u32[]{:S(2)}) collective-permute-start(bf16[384,2048]{1,0:T(8,128)(2,1)S(1)} %copy-done.60), channel_id=1, source_target_pairs={{0,2},{1,3},{2,0},{3,1},{4,6},{5,7},{6,4},{7,5},{8,10},{9,11},{10,... | collective-permute-start | bytes 4718600 | tf_op jit(solution)/shard_map/ppermute | solution.py:31
  369.1 40.0 %collective-permute-start.29 = (bf16[384,2048]{1,0:T(8,128)(2,1)S(1)}, bf16[384,2048]{1,0:T(8,128)(2,1)}, u32[]{:S(2)}, u32[]{:S(2)}) collective-permute-start(bf16[384,2048]{1,0:T(8,128)(2,1)S(1)} %copy-done.60), channel_id=1, source_target_pairs={{0,1},{1,0},{2,3},{3,2},{4,5},{5,4},{6,7},{7,6},{8,9},{9,8},{10,11... | collective-permute-start | bytes 4718600 | tf_op jit(solution)/shard_map/ppermute | solution.py:31
  438.9 512.0 %reduce-scatter.5.cloned.1.call-start = ((), (), s32[]{:S(2)}) async-start(), calls=%async_computation.5 | async-start | bytes 12976128 | tf_op jit(solution)/shard_map/reduce_scatter | solution.py:848
  492.2 42.8 %collective-permute-start.38 = (bf16[768,2048]{1,0:T(8,128)(2,1)}, bf16[768,2048]{1,0:T(8,128)(2,1)S(1)}, u32[]{:S(2)}, u32[]{:S(2)}) collective-permute-start(bf16[768,2048]{1,0:T(8,128)(2,1)} %convolution_convert_fusion.6), channel_id=1, source_target_pairs={{0,1},{1,0},{2,3},{3,2},{4,5},{5,4},{6,7},{7,6},{8,9},{9,8},{10,11... | collective-permute-start | bytes 9437192 | tf_op jit(solution)/shard_map/ppermute | solution.py:31
  554.3 65.2 %collective-permute-start.39 = (bf16[384,2048]{1,0:T(8,128)(2,1)}, bf16[384,2048]{1,0:T(8,128)(2,1)}, u32[]{:S(2)}, u32[]{:S(2)}) collective-permute-start(bf16[384,2048]{1,0:T(8,128)(2,1)} %get-tuple-element.258), channel_id=1, source_target_pairs={{0,2},{1,3},{2,0},{3,1},{4,6},{5,7},{6,4},{7,5},{8,10},{9,11},{10,... | collective-permute-start | bytes 4718600 | tf_op jit(solution)/shard_map/ppermute | solution.py:31
  555.6 69.3 %collective-permute-start.37 = (bf16[384,2048]{1,0:T(8,128)(2,1)}, bf16[384,2048]{1,0:T(8,128)(2,1)}, u32[]{:S(2)}, u32[]{:S(2)}) collective-permute-start(bf16[384,2048]{1,0:T(8,128)(2,1)} %get-tuple-element.253), channel_id=1, source_target_pairs={{0,2},{1,3},{2,0},{3,1},{4,6},{5,7},{6,4},{7,5},{8,10},{9,11},{10,... | collective-permute-start | bytes 4718600 | tf_op jit(solution)/shard_map/ppermute | solution.py:31
  565.8 76.8 %collective-permute-start.42 = (bf16[768,2048]{1,0:T(8,128)(2,1)}, bf16[768,2048]{1,0:T(8,128)(2,1)}, u32[]{:S(2)}, u32[]{:S(2)}) collective-permute-start(bf16[768,2048]{1,0:T(8,128)(2,1)} %convolution_convert_fusion.5), channel_id=1, source_target_pairs={{0,1},{1,0},{2,3},{3,2},{4,5},{5,4},{6,7},{7,6},{8,9},{9,8},{10,11... | collective-permute-start | bytes 9437192 | tf_op jit(solution)/shard_map/ppermute | solution.py:31
  572.4 82.1 %collective-permute-start.43 = (bf16[768,2048]{1,0:T(8,128)(2,1)}, bf16[768,2048]{1,0:T(8,128)(2,1)}, u32[]{:S(2)}, u32[]{:S(2)}) collective-permute-start(bf16[768,2048]{1,0:T(8,128)(2,1)} %convolution_convert_fusion.4), channel_id=1, source_target_pairs={{0,1},{1,0},{2,3},{3,2},{4,5},{5,4},{6,7},{7,6},{8,9},{9,8},{10,11... | collective-permute-start | bytes 9437192 | tf_op jit(solution)/shard_map/ppermute | solution.py:31
  672.0 45.1 %collective-permute-start.46 = (bf16[384,2048]{1,0:T(8,128)(2,1)S(1)}, bf16[384,2048]{1,0:T(8,128)(2,1)}, u32[]{:S(2)}, u32[]{:S(2)}) collective-permute-start(bf16[384,2048]{1,0:T(8,128)(2,1)S(1)} %get-tuple-element.273.refs_0_.refs_4_), channel_id=1, source_target_pairs={{0,1},{1,0},{2,3},{3,2},{4,5},{5,4},{6,7},{7,6},{8,9},{9,8},{10,11... | collective-permute-start | bytes 4718600 | tf_op jit(solution)/shard_map/ppermute | solution.py:31
  705.8 69.0 %collective-permute-start.54 = (bf16[384,2048]{1,0:T(8,128)(2,1)}, bf16[384,2048]{1,0:T(8,128)(2,1)S(1)}, u32[]{:S(2)}, u32[]{:S(2)}) collective-permute-start(bf16[384,2048]{1,0:T(8,128)(2,1)} %get-tuple-element.271), channel_id=1, source_target_pairs={{0,2},{1,3},{2,0},{3,1},{4,6},{5,7},{6,4},{7,5},{8,10},{9,11},{10,... | collective-permute-start | bytes 4718600 | tf_op jit(solution)/shard_map/ppermute | solution.py:31
  707.2 159.2 %collective-permute-start.53 = (bf16[384,2048]{1,0:T(8,128)(2,1)}, bf16[384,2048]{1,0:T(8,128)(2,1)}, u32[]{:S(2)}, u32[]{:S(2)}) collective-permute-start(bf16[384,2048]{1,0:T(8,128)(2,1)} %get-tuple-element.269), channel_id=1, source_target_pairs={{0,2},{1,3},{2,0},{3,1},{4,6},{5,7},{6,4},{7,5},{8,10},{9,11},{10,... | collective-permute-start | bytes 4718600 | tf_op jit(solution)/shard_map/ppermute | solution.py:31
  786.8 44.8 %collective-permute-start.50 = (bf16[768,2048]{1,0:T(8,128)(2,1)}, bf16[768,2048]{1,0:T(8,128)(2,1)}, u32[]{:S(2)}, u32[]{:S(2)}) collective-permute-start(bf16[768,2048]{1,0:T(8,128)(2,1)} %convolution_convert_fusion.2), channel_id=1, source_target_pairs={{0,1},{1,0},{2,3},{3,2},{4,5},{5,4},{6,7},{7,6},{8,9},{9,8},{10,11... | collective-permute-start | bytes 9437192 | tf_op jit(solution)/shard_map/ppermute | solution.py:31
  801.9 43.4 %collective-permute-start.51 = (bf16[4,256,512]{2,1,0:T(8,128)(2,1)}, bf16[4,256,512]{2,1,0:T(8,128)(2,1)S(1)}, u32[]{:S(2)}, u32[]{:S(2)}) collective-permute-start(bf16[4,256,512]{2,1,0:T(8,128)(2,1)} %get-tuple-element.287), channel_id=1, source_target_pairs={{0,4},{4,0},{8,12},{12,8},{16,20},{20,16},{24,28},{28,24},{1,5},{5... | collective-permute-start | bytes 3145736 | tf_op jit(solution)/shard_map/ppermute | solution.py:31
  831.3 91.3 %collective-permute-start.59 = (bf16[4,256,512]{2,1,0:T(8,128)(2,1)}, bf16[4,256,512]{2,1,0:T(8,128)(2,1)}, u32[]{:S(2)}, u32[]{:S(2)}) collective-permute-start(bf16[4,256,512]{2,1,0:T(8,128)(2,1)} %get-tuple-element.293), channel_id=1, source_target_pairs={{0,4},{4,0},{8,12},{12,8},{16,20},{20,16},{24,28},{28,24},{1,5},{5... | collective-permute-start | bytes 3145736 | tf_op jit(solution)/shard_map/ppermute | solution.py:31
  843.5 83.4 %collective-permute-start.60 = (bf16[384,2048]{1,0:T(8,128)(2,1)}, bf16[384,2048]{1,0:T(8,128)(2,1)S(1)}, u32[]{:S(2)}, u32[]{:S(2)}) collective-permute-start(bf16[384,2048]{1,0:T(8,128)(2,1)} %get-tuple-element.295), channel_id=1, source_target_pairs={{0,2},{1,3},{2,0},{3,1},{4,6},{5,7},{6,4},{7,5},{8,10},{9,11},{10,... | collective-permute-start | bytes 4718600 | tf_op jit(solution)/shard_map/ppermute | solution.py:31
  847.6 65.8 %collective-permute-start.56 = (bf16[384,2048]{1,0:T(8,128)(2,1)}, bf16[384,2048]{1,0:T(8,128)(2,1)S(1)}, u32[]{:S(2)}, u32[]{:S(2)}) collective-permute-start(bf16[384,2048]{1,0:T(8,128)(2,1)} %get-tuple-element.289), channel_id=1, source_target_pairs={{0,2},{1,3},{2,0},{3,1},{4,6},{5,7},{6,4},{7,5},{8,10},{9,11},{10,... | collective-permute-start | bytes 4718600 | tf_op jit(solution)/shard_map/ppermute | solution.py:31
  866.4 53.9 %collective-permute-start.57 = (bf16[1,256,512]{2,1,0:T(8,128)(2,1)}, bf16[1,256,512]{2,1,0:T(8,128)(2,1)S(1)}, u32[]{:S(2)}, u32[]{:S(2)}) collective-permute-start(bf16[1,256,512]{2,1,0:T(8,128)(2,1)} %get-tuple-element.424), channel_id=1, source_target_pairs={{0,16},{4,20},{8,24},{12,28},{16,0},{20,4},{24,8},{28,12},{1,17},{... | collective-permute-start | bytes 786440 | tf_op jit(solution)/shard_map/ppermute | solution.py:31
  878.4 43.3 %collective-permute-start.58 = (bf16[4,512,256]{2,1,0:T(8,128)(2,1)S(1)}, bf16[4,512,256]{2,1,0:T(8,128)(2,1)S(1)}, u32[]{:S(2)}, u32[]{:S(2)}) collective-permute-start(bf16[4,512,256]{2,1,0:T(8,128)(2,1)S(1)} %copy-done.110), channel_id=1, source_target_pairs={{0,4},{4,0},{8,12},{12,8},{16,20},{20,16},{24,28},{28,24},{1,5},{5... | collective-permute-start | bytes 3145736 | tf_op jit(solution)/shard_map/ppermute | solution.py:31
  (162 other events, 3023.6 us)
Sparse Core Ops, SparseCore 0:
  134.5 167.7 all-gather.4
  305.1 90.9 all-gather.2
  439.0 110.0 reduce-scatter.2
  706.0 236.5 reduce-scatter.4

commit v3 on v2

--- a/solution.py
+++ b/solution.py
@@ -50,6 +50,7 @@
 class Sequence:
     def __init__(self):
         self.last = None
+        self.held = {}
 
     def run(self, call, *operands):
         if self.last is not None:
@@ -58,14 +59,14 @@
         self.last = jax.tree.leaves(result)[0]
         return result
 
-    def pin(self, *values):
-        out = lax.optimization_barrier(values + (self.last,))
-        self.last = out[0]
-        return out[:-1]
-
-
-def join(axis):
-    return lambda *blocks: jnp.concatenate(blocks, axis=axis)
+    def close(self, **named):
+        names = list(named)
+        out = lax.optimization_barrier(tuple(named[n] for n in names) + (self.last,))
+        self.last = jax.tree.leaves(out[0])[0]
+        self.held.update(zip(names, out[:-1]))
+
+    def __getattr__(self, name):
+        return self.__dict__["held"][name]
 
 
 def halving(n):
@@ -95,78 +96,49 @@
     return whole
 
 
-class SummedGrad:
-    def __init__(self, sequence, halves, size, exchanges):
-        self.sequence, self.size, self.exchanges = sequence, size, exchanges
-        self.send(*halves)
-
-    def send(self, sent, kept):
-        self.kept = kept
-        self.coming = exchange(sent, "dp", self.size, self.exchanges[0])
-        self.exchanges = self.exchanges[1:]
-
-    def step(self):
-        def added(a, b):
-            total = (a.astype(F32) + b.astype(F32)).astype(BF)
-            half = total.shape[0] // 2
-            return total[half:], total[:half]
-
-        self.send(*self.sequence.run(added, self.kept, self.coming))
-
-    def steps(self):
-        while self.exchanges:
-            self.step()
-
-
-class Gathered:
-    def __init__(self, own, size):
-        self.size, self.held = size, [own]
-        offset = size // 2
-        while offset > 1:
-            self.held = self.held + [exchange(part, "tensor", size, offset) for part in self.held]
-            offset //= 2
-        self.near = [exchange(own, "tensor", size, 1)]
-
-    def relay(self, *done):
-        self.near += [exchange(after(part, *done), "tensor", self.size, 1) for part in self.held[1:]]
-
-    def parts(self):
-        return self.held + self.near
-
-
-class SummedRows:
-    def __init__(self, sequence, operand, weight, size, rows):
-        self.sequence, self.weight, self.size, self.rows = sequence, weight, size, rows
-        self.operand = operand
-
-    def high(self):
-        half = self.size // 2 * self.rows
-        if isinstance(self.operand, tuple):
-            self.operand, upper = self.operand
-            call = lambda v, w: mm_nt(v, w).astype(BF)
-        else:
-            upper = self.operand
-            call = lambda v, w: mm_nt(v[half:], w).astype(BF)
-        sent = self.sequence.run(call, upper, self.weight)
-        self.near = exchange(sent, "tensor", self.size, 1)
-
-    def rest(self):
-        size, rows, offset, places = self.size, self.rows, 2, self.size // 4
-        far, self.kept = self.sequence.run(
-            lambda v, w, n: near_added(v, w, n, places * rows), self.operand, self.weight, self.near
-        )
-        self.coming = exchange(far, "tensor", size, offset)
-        while places > 1:
-            total = self.kept + self.coming.astype(F32)
-            offset, places = 2 * offset, places // 2
-            self.kept = total[: places * rows]
-            self.coming = exchange(total[places * rows :].astype(BF), "tensor", size, offset)
-
-
-def near_added(operand, weight, near, tile):
+def halves_added(kept, coming):
+    total = (kept.astype(F32) + coming.astype(F32)).astype(BF)
+    half = total.shape[0] // 2
+    return total[half:], total[:half]
+
+
+def near_added(operand, weight, near):
+    rows, depth = operand.shape[0] // 2, operand.shape[1]
     width = weight.shape[0]
-
-    def kernel(v, w, n, far, kept):
+    tile = rows // 2
+    outs = [jax.ShapeDtypeStruct((tile, width), BF), jax.ShapeDtypeStruct((tile, width), F32)]
+    settings = dict(
+        out_shape=outs,
+        compiler_params=pltpu.CompilerParams(vmem_limit_bytes=56 * 2**20),
+        cost_estimate=pl.CostEstimate(
+            flops=likely_flops(2 * rows * weight.size), bytes_accessed=2 * weight.size, transcendentals=0
+        ),
+        name="near_added",
+    )
+    if depth >= width:
+        wide = min(256, width)
+
+        def by_columns(v, w, added, far, kept):
+            total = mm_nt(v[...], w[...])
+            far[...] = (total[tile:] + added[tile:, :].astype(F32)).astype(BF)
+            kept[...] = total[:tile] + added[:tile, :].astype(F32)
+
+        def columns(height):
+            return pl.BlockSpec((height, wide), lambda j: (0, j))
+
+        return pl.pallas_call(
+            by_columns,
+            grid=(width // wide,),
+            in_specs=[
+                pl.BlockSpec((rows, depth), lambda j: (0, 0), pipeline_mode=pl.Buffered(1)),
+                pl.BlockSpec((wide, depth), lambda j: (j, 0)),
+                columns(rows),
+            ],
+            out_specs=[columns(tile)] * 2,
+            **settings,
+        )(operand, weight, near)
+
+    def by_rows(v, w, n, far, kept):
         step = pl.program_id(0)
         total = mm_nt(v[...], w[...]) + n[...].astype(F32)
 
@@ -183,7 +155,7 @@
 
     fixed = pl.BlockSpec((tile, width), lambda i: (0, 0))
     return pl.pallas_call(
-        kernel,
+        by_rows,
         grid=(2,),
         in_specs=[
             rowed(operand),
@@ -191,12 +163,7 @@
             rowed(near),
         ],
         out_specs=[fixed, fixed],
-        out_shape=[jax.ShapeDtypeStruct((tile, width), BF), jax.ShapeDtypeStruct((tile, width), F32)],
-        compiler_params=pltpu.CompilerParams(vmem_limit_bytes=56 * 2**20),
-        cost_estimate=pl.CostEstimate(
-            flops=likely_flops(4 * tile * weight.size), bytes_accessed=2 * weight.size, transcendentals=0
-        ),
-        name="near_added",
+        **settings,
     )(operand, weight, near)
 
 
@@ -280,10 +247,12 @@
 
 def grad_kernel(lefts, rights, moving, wide, name, fixed=(0, 1), owner=None):
     part, parts = fixed
+    part, span = part if isinstance(part, tuple) else (part, 1)
     mover, other = (lefts, rights) if moving == "left" else (rights, lefts)
     rows = sum(v.shape[0] for v in mover)
     steps = mover[0].shape[1] // wide
-    held = other[0].shape[1] // parts
+    held = other[0].shape[1] // parts * span
+    begin = other[0].shape[1] // parts * part
     shape = (wide, held) if moving == "left" else (held, wide)
     half = steps // 2
     count, others = len(mover), len(other)
@@ -315,7 +284,7 @@
                 size = source.shape[0]
                 made.append(
                     pltpu.make_async_copy(
-                        source.at[:, pl.ds(part * held, held)],
+                        source.at[:, pl.ds(begin, held)],
                         kept.at[pl.ds(row, size), :],
                         ready.at[p],
                     )
@@ -476,8 +445,8 @@
 
 
 def backward_kernel(order, offsets, pre, before, *rest):
-    pieces = (len(rest) - 2) // 2
-    dgated, dpieces, dpre, carry = rest[:pieces], rest[pieces : 2 * pieces], rest[-2], rest[-1]
+    pieces = (len(rest) - 1) // 2
+    dgated, dpieces, carry = rest[:pieces], rest[pieces : 2 * pieces], rest[-1]
     step_id = pl.program_id(0)
     block = pl.num_programs(0) - 1 - step_id
     rows = pre.shape[1]
@@ -539,7 +508,6 @@
             for k in range(3):
                 value = jnp.concatenate([outs[0][k], outs[1][k]], axis=0).astype(BF)
                 at = pl.ds(k * channels + c * LANES, LANES)
-                dpre[0, pl.ds(base, 2 * SUB), at] = value
                 dpieces[p][0, pl.ds(local, 2 * SUB), at] = value
         return 0
 
@@ -597,12 +565,57 @@
 
 
 def total_over_mesh(values, n_dp, n_tensor):
-    for axis, size in (("tensor", n_tensor), ("dp", n_dp)):
-        offset = 1
-        while offset < size:
-            values = values + exchange(values, axis, size, offset)
-            offset *= 2
+    for axis, size, offsets in (
+        ("tensor", n_tensor, (1, 2)),
+        ("tensor", n_tensor, (4, 8)),
+        ("dp", n_dp, (1,)),
+        ("dp", n_dp, (2, 4)),
+        ("dp", n_dp, (8,)),
+    ):
+        offsets = [o for o in offsets if o < size]
+        if len(offsets) == 2:
+            one, two = offsets
+            parts = [exchange(values, axis, size, o) for o in (one, two, one + two)]
+            values = (values + parts[0]) + (parts[1] + parts[2])
+        elif offsets:
+            values = values + exchange(values, axis, size, offsets[0])
     return values
+
+
+def new_weights(steps, weights, updates):
+    tiles = weights[3].shape[0] // 176
+    counts = [v.shape[0] if v.ndim == 3 else 0 for v in weights]
+
+    def kernel(factor, *refs):
+        olds, changes, news, copies = refs[:4], refs[4:11], refs[11:15], refs[15:]
+        n = 0
+        for old, new, copy, count in zip(olds, news, copies, counts):
+            for k in range(max(count, 1)):
+                at = (k,) if count else Ellipsis
+                value = old[at] - factor[n] * changes[n][...]
+                new[at] = value
+                copy[at] = value.astype(BF)
+                n += 1
+
+    def spec(v):
+        if v.ndim == 3:
+            return pl.BlockSpec((v.shape[0], v.shape[1] // tiles, v.shape[2]), lambda i, f: (0, i, 0))
+        return pl.BlockSpec((v.shape[0] // tiles, v.shape[1]), lambda i, f: (i, 0))
+
+    outs = pl.pallas_call(
+        kernel,
+        grid_spec=pltpu.PrefetchScalarGridSpec(
+            num_scalar_prefetch=1,
+            grid=(tiles,),
+            in_specs=[spec(v) for v in weights] + [spec(v) for v in updates],
+            out_specs=[spec(v) for v in weights] * 2,
+        ),
+        out_shape=[jax.ShapeDtypeStruct(v.shape, F32) for v in weights]
+        + [jax.ShapeDtypeStruct(v.shape, BF) for v in weights],
+        compiler_params=pltpu.CompilerParams(vmem_limit_bytes=60 * 2**20),
+        name="new_weights",
+    )(steps, *weights, *updates)
+    return outs[:4], outs[4:]
 
 
 def per_device(
@@ -638,14 +651,12 @@
     tensor_id = lax.axis_index("tensor")
     near_first = halving(n_dp)
     owner = owners(dp_id, near_first)
-    z_first = near_first[1:2] + near_first[:1] + near_first[2:]
-    owner_z = owners(dp_id, z_first)
     row_places = offsets_by_place(halving(n_tensor))
     place_of = jnp.array([row_places.index(o) for o in range(n_tensor)], jnp.int32)
     order = place_of[jnp.arange(n_tensor) ^ tensor_id]
     offsets = (jnp.cumsum(doc_lengths[0]) - doc_lengths[0]).astype(jnp.int32)
-    sequence = Sequence()
-    run = sequence.run
+    q = Sequence()
+    run = q.run
 
     def cut(i):
         return slice(i * piece, (i + 1) * piece)
@@ -680,38 +691,68 @@
     far = {j: exchange(own_mix_in, "dp", n_dp, j) for j in early}
     near = {0: exchange(own_mix_in, "dp", n_dp, 1)}
     far_a = distant(halves[0])
-    first = lax.optimization_barrier((far_a, near, far))
-    far_a, near, far = first
+    first = lax.optimization_barrier((far_a, near, far, own_mix_in, halves[1]))
+    far_a, near, far, own_mix_in, own_b = first
     own_ffn_in = jnp.concatenate([padded(ffn_in[k].astype(BF)) for k in range(2)], axis=1)
-    far.update({j: exchange(after(own_mix_in, far_a[0]), "dp", n_dp, j) for j in late})
+    far.update({j: exchange(own_mix_in, "dp", n_dp, j) for j in late})
     near.update({j: exchange(far[j], "dp", n_dp, 1) for j in early})
-    own_b = after(halves[1], far_a[0])
     far_b = distant(own_b)
-    weight_sq = jnp.stack([jnp.sum(w * w) for w in [after(weights[0], far_a[0])] + weights[1:]])
-    second = lax.optimization_barrier((far_a, far_b, near, far, weight_sq, own_ffn_in))
-    far_a, far_b, near, far, weight_sq, own_ffn_in = second
+    near_a = [exchange(far_a[0], "tensor", n_tensor, 1)]
+    near_b = [exchange(after(own_b, near_a[0]), "tensor", n_tensor, 1)]
+    second = lax.optimization_barrier(
+        (far_a, far_b, near, far, own_ffn_in, near_a, near_b, mix_out.astype(BF).T, own_mix_in)
+    )
+    far_a, far_b, near, far, own_ffn_in, near_a, near_b, own_mix_out, own_mix_in = second
     near.update({j: exchange(far[j], "dp", n_dp, 1) for j in late})
-    near_a = [exchange(part, "tensor", n_tensor, 1) for part in far_a]
-    near_b = [exchange(part, "tensor", n_tensor, 1) for part in far_b]
-    known = [(dp_id, after(own_mix_in, far_a[0]))] + [(dp_id ^ j, far[j]) for j in far_offsets]
+    near_a += [exchange(part, "tensor", n_tensor, 1) for part in far_a[1:]]
+    near_b += [exchange(after(part, near_a[-1]), "tensor", n_tensor, 1) for part in far_b[1:]]
+    known = [(dp_id, own_mix_in)] + [(dp_id ^ j, far[j]) for j in far_offsets]
     known += [(dp_id ^ j ^ 1, near[j]) for j in [0] + early]
     w_mix_in = jnp.zeros((width, 3 * channels), BF)
     for place, block in known:
         w_mix_in = lax.dynamic_update_slice(w_mix_in, block, (place * depth, 0))
-    own_mix_out = after(mix_out.astype(BF).T, *near_a, *near_b)
     far_mo = [own_mix_out] + [exchange(own_mix_out, "dp", n_dp, j) for j in far_offsets]
     third = lax.optimization_barrier(
-        (near_a, near_b, w_mix_in, own_ffn_in, [near[j] for j in late], far_mo)
-    )
-    near_a, near_b, w_mix_in, own_ffn_in, last, far_mo = third
+        (near_a, near_b, w_mix_in, own_ffn_in, [near[j] for j in late], far_mo, cotangent)
+    )
+    near_a, near_b, w_mix_in, own_ffn_in, last, far_mo, cot_all = third
+    q.last = near_b[0]
+
+    def far_rows(own):
+        return distant(own)[1:]
+
+    def to_core(parts):
+        return [exchange(part, "tensor", n_tensor, 1) for part in parts]
+
+    def to_far(rows_sent):
+        return exchange(rows_sent, "tensor", n_tensor, 2)
+
+    def landed(kept, coming):
+        places, offset = n_tensor // 4, 2
+        while places > 1:
+            total = kept + coming.astype(F32)
+            offset, places = 2 * offset, places // 2
+            kept = total[: places * piece]
+            coming = exchange(total[places * piece :].astype(BF), "tensor", n_tensor, offset)
+        return kept, coming
+
+    def upper(operand, weight):
+        half = operand.shape[0] // 2
+        return run(lambda v, w: mm_nt(v[half:], w).astype(BF), operand, weight)
+
+    def lower(operand, weight, near):
+        return run(near_added, operand, weight, near)
+
+    def add_halves(kept, coming):
+        return run(halves_added, kept, coming)
+
     w_ffn_in = lax.all_gather(own_ffn_in, "dp", axis=0, tiled=True)
-    w_ffn_out = lax.all_gather(padded(ffn_out.astype(BF).T), "dp", axis=0, tiled=True)
-    cots = [Gathered(after(cotangent[cut(0)], near_b[0]), n_tensor)]
+    cot_own = [cot_all[cut(i)] for i in pieces]
+    cot_far = far_rows(cot_own[0])
+    near_mo = exchange(jnp.concatenate(far_mo, axis=0), "dp", n_dp, 1)
     for j, block in zip(late, last):
         w_mix_in = lax.dynamic_update_slice(w_mix_in, block, ((dp_id ^ j ^ 1) * depth, 0))
-    sequence.last = near_b[0]
     whole_one = [v for pair in zip(far_a + near_a, far_b + near_b) for v in pair]
-    near_mo = [exchange(block, "dp", n_dp, 1) for block in far_mo]
     (pre,) = run(
         lambda w, *parts: row_tiles(
             pre_kernel,
@@ -725,78 +766,90 @@
         w_mix_in,
         *whole_one,
     )
-    pre = pre.reshape(n_tensor, rows, 3 * channels)
+    q.close(pre=pre.reshape(n_tensor, rows, 3 * channels), cot0=cot_far, cot_own1=cot_own[1])
+
+    cot_far = far_rows(q.cot_own1)
+    cot0_near = to_core([cot_own[0]] + q.cot0)
     scanned = recurrence_call(
         forward_kernel,
         order,
         offsets,
-        [after(pre, sequence.last)],
+        [q.pre],
         [jax.ShapeDtypeStruct((n_tensor, rows, channels), F32)]
         + [jax.ShapeDtypeStruct((n_tensor, piece, channels), BF)] * CHUNKS,
         channels,
         "recurrence_forward",
     )
-    before, gated = scanned[0], scanned[1:]
-    sequence.last = before
-
-    w_mix_out = run(
-        lambda *blocks: spread(blocks, owner_far + owner_near), far_mo[0], *far_mo[1:], *near_mo
-    )
-
-    sums = [
-        SummedRows(sequence, gated[i].reshape(-1, channels), w_mix_out, n_tensor, piece) for i in pieces
-    ]
-    (cots[0].held[1],) = sequence.pin(cots[0].held[1])
-    for i in pieces:
-        sums[i].high()
-    for i in pieces:
-        sums[i].rest()
-    comings = sequence.pin(*[v.coming for v in sums])
+    q.last = scanned[0]
+    mo_blocks = far_mo + [near_mo[p * depth : (p + 1) * depth] for p in range(len(far_mo))]
+    w_mix_out = run(lambda *blocks: spread(blocks, owner_far + owner_near), *mo_blocks)
+    gated = [v.reshape(-1, channels) for v in scanned[1:]]
+    q.close(
+        up0=upper(gated[0], w_mix_out),
+        w_mo=w_mix_out,
+        gated=gated,
+        before=scanned[0],
+        cot0_near=cot0_near,
+    )
+    cot_parts = [[cot_own[0]] + q.cot0 + q.cot0_near]
+
+    (near0,) = to_core([q.up0])
+    q.close(up1=upper(q.gated[1], q.w_mo), near0=near0)
+
+    (near1,) = to_core([q.up1])
+    far0, kept0 = lower(q.gated[0], q.w_mo, q.near0)
+    q.close(far0=far0, kept0=kept0, near1=near1, cot1=cot_far)
+
+    coming0 = to_far(q.far0)
+    cot1_near = to_core([cot_own[1]] + q.cot1)
+    far1, kept1 = lower(q.gated[1], q.w_mo, q.near1)
+    q.close(far1=far1, kept1=kept1, coming0=coming0, cot1_near=cot1_near)
+    cot_parts.append([cot_own[1]] + q.cot1 + q.cot1_near)
+
+    coming1 = to_far(q.far1)
 
     def middle_of(kept, coming, own):
         middle = own.astype(F32) + kept + coming.astype(F32)
         unit_rows, scaling = unit(middle)
         return (unit_rows * gains[1]).astype(BF), middle, scaling
 
-    middle, scale_two, whole_two = [], [], []
-    for i in pieces:
-        normed_i, middle_i, scale_i = run(middle_of, sums[i].kept, comings[i], tokens[cut(i)])
-        middle.append(middle_i)
-        scale_two.append(scale_i)
-        if i > 0:
-            normed_i = after(normed_i, whole_two[i - 1].held[1])
-        whole_two.append(Gathered(normed_i, n_tensor))
-    hidden, slope, act = [], [], []
+    normed0, middle0, scale0 = run(middle_of, *landed(q.kept0, q.coming0), tokens[cut(0)])
+    q.close(coming1=coming1, normed0=normed0, middle0=middle0, scale0=scale0, w_ffn_in=w_ffn_in)
+    w_ffn_out = lax.all_gather(
+        after(padded(ffn_out.astype(BF).T), q.w_ffn_in), "dp", axis=0, tiled=True
+    )
+    normed_far = far_rows(q.normed0)
+    normed1, middle1, scale1 = run(middle_of, *landed(q.kept1, q.coming1), tokens[cut(1)])
+    weight_sq = run(lambda *ws: jnp.stack([jnp.sum(w * w) for w in ws]), *weights)
+    q.close(
+        normed1=normed1, middle1=middle1, scale1=scale1, normed0_far=normed_far, weight_sq=weight_sq
+    )
+    weight_sq = q.weight_sq
+    middle, scale_two = [q.middle0, q.middle1], [q.scale0, q.scale1]
+
     many = n_tensor * piece
     flops = 2 * many * width * units
-    whole_two[0].relay()
-    one = jax.ShapeDtypeStruct((many // 2, units), BF)
-    for i in pieces:
-        if i > 0:
-            whole_two[i].relay(sequence.last)
-        halves = [
-            run(
-                lambda w, *parts: row_tiles(
-                    gate_up_kernel, parts, w, [], [one] * 3, flops, "gate_up"
-                ),
-                w_ffn_in,
-                *parts,
-            )
-            for parts in (whole_two[i].held, whole_two[i].near)
-        ]
-        if i > 0:
-            cots[i].relay(sequence.last)
-        elif CHUNKS > 1:
-            cots[0].relay(sequence.last)
-            cots.append(
-                Gathered(after(cotangent[cut(1)], whole_two[1].held[1], sequence.last), n_tensor)
-            )
-        hidden.append((halves[0][0], halves[1][0]))
-        slope.append((halves[0][1], halves[1][1]))
-        act.append((halves[0][2], halves[1][2]))
-
-    def listed(chunks):
-        return [part for gathered in chunks for part in gathered.parts()]
+    one = jax.ShapeDtypeStruct((many, units), BF)
+
+    def gate_up(parts):
+        return run(
+            lambda w, *parts: row_tiles(
+                gate_up_kernel, parts, w, [], [one] * 3, 2 * flops, "gate_up"
+            ),
+            q.w_ffn_in,
+            *parts,
+        )
+
+    normed_far = far_rows(q.normed1)
+    normed0 = [q.normed0] + q.normed0_far
+    whole_two = normed0 + to_core(normed0)
+    out0 = gate_up(whole_two)
+    q.close(out0=out0, normed1_far=normed_far)
+    normed1 = [q.normed1] + q.normed1_far
+    parts1 = normed1 + to_core(normed1)
+    out1 = gate_up(parts1)
+    whole_two = whole_two + parts1
+    hidden = [q.out0[0], out1[0]]
 
     def grad(lefts, rights, *settings, **more):
         def call(*values):
@@ -804,49 +857,46 @@
 
         return run(call, *lefts, *rights)
 
-    def flat(pairs):
-        return [v for pair in pairs for v in pair]
-
-    grad_fo = grad(flat(hidden), listed(cots), "right", min(256, depth), "grad_out")
-    grad_fo = lax.psum_scatter(grad_fo, "dp", scatter_dimension=1, tiled=True)
-
-    def gate_up_back(i, half):
+    wide = min(256, depth)
+    grad_fo = grad(hidden, cot_parts[0] + cot_parts[1], "right", wide, "grad_out")
+    q.close(grad_fo=grad_fo, out1=out1)
+    hidden = [q.out0[0], q.out1[0]]
+
+    def gate_up_back(i):
+        out = (q.out0, q.out1)[i]
         (d,) = run(
             lambda w, v, a, *parts: row_tiles(
                 gate_up_back_kernel,
                 parts,
                 w,
                 [v, a],
-                [jax.ShapeDtypeStruct((many // 2, 2 * units), BF)],
-                flops // 2,
+                [jax.ShapeDtypeStruct((many, 2 * units), BF)],
+                flops,
                 "gate_up_back",
             ),
             w_ffn_out,
-            slope[i][half],
-            act[i][half],
-            *(cots[i].near if half else cots[i].held),
+            out[1],
+            out[2],
+            *cot_parts[i],
         )
         return d
 
-    sums = [SummedRows(sequence, None, w_ffn_in, n_tensor, piece) for i in pieces]
-    downs = [SummedRows(sequence, h, w_ffn_out, n_tensor, piece) for h in hidden]
-    upper = []
-    for i in pieces:
-        upper.append(gate_up_back(i, 1))
-        sums[i].operand = (None, upper[i])
-        sums[i].high()
-    d_two = []
-    for i in pieces:
-        lower = gate_up_back(i, 0)
-        d_two.append((lower, upper[i]))
-        sums[i].operand = lower
-        sums[i].rest()
-    for i in pieces:
-        downs[i].high()
-    (grad_fo,) = sequence.pin(grad_fo)
-    grad_fi = grad(listed(whole_two), flat(d_two), "left", min(256, depth), "grad_in")
-    grad_fi = lax.psum_scatter(grad_fi, "dp", scatter_dimension=0, tiled=True)
-    comings = sequence.pin(*[v.coming for v in sums])
+    d0 = gate_up_back(0)
+    q.close(up0=upper(d0, q.w_ffn_in), d0=d0, grad_fo=q.grad_fo)
+
+    sum_fo = lax.psum_scatter(q.grad_fo, "dp", scatter_dimension=1, tiled=True)
+    (near0,) = to_core([q.up0])
+    d1 = gate_up_back(1)
+    up1 = upper(d1, q.w_ffn_in)
+    far0, kept0 = lower(q.d0, q.w_ffn_in, near0)
+    q.close(far0=far0, kept0=kept0, up1=up1, d1=d1, w_ffn_out=w_ffn_out)
+
+    coming0 = to_far(q.far0)
+    (near1,) = to_core([q.up1])
+    down0 = upper(hidden[0], q.w_ffn_out)
+    down1 = upper(hidden[1], q.w_ffn_out)
+    far1, kept1 = lower(q.d1, q.w_ffn_in, near1)
+    q.close(far1=far1, kept1=kept1, coming0=coming0, down0=down0, down1=down1)
 
     def middle_back(kept, coming, mid, scaling, cot):
         unit_rows = mid * scaling
@@ -854,27 +904,32 @@
         d_mid = cot.astype(F32) + d_norm
         return d_mid.astype(BF), d_mid, gain
 
-    d_middle, gain_two, lows, whole_d = [], 0.0, [], []
-    for i in pieces:
-        low, d_mid, gain_i = run(
-            middle_back, sums[i].kept, comings[i], middle[i], scale_two[i], cotangent[cut(i)]
-        )
-        d_middle.append(d_mid)
-        gain_two = gain_two + gain_i
-        lows.append(low)
-    whole_d.append(Gathered(lows[0], n_tensor))
-    for i in pieces:
-        downs[i].rest()
-    for i in range(1, CHUNKS):
-        whole_d.append(
-            Gathered(after(lows[i], whole_d[i - 1].held[1], sequence.last), n_tensor)
-        )
-    for gathered in whole_d:
-        gathered.relay(sequence.last)
-
-    d_gated = []
-    for i in pieces:
-        (d_i,) = run(
+    def grad_in(part):
+        return grad(whole_two, [q.d0, q.d1], "left", wide, "grad_in", fixed=(part, 2))
+
+    def sum_in(value):
+        return lax.psum_scatter(value, "dp", scatter_dimension=0, tiled=True)
+
+    coming1 = to_far(q.far1)
+    down_near = to_core([q.down0, q.down1])
+    back0 = run(
+        middle_back, *landed(q.kept0, q.coming0), middle[0], scale_two[0], cotangent[cut(0)]
+    )
+    grad_fg = grad_in(0)
+    q.close(
+        coming1=coming1, back0=back0, grad_fg=grad_fg, down_near=down_near, sum_fo=sum_fo
+    )
+
+    low_far = far_rows(q.back0[0])
+    sum_fg = sum_in(q.grad_fg)
+    back1 = run(
+        middle_back, *landed(q.kept1, q.coming1), middle[1], scale_two[1], cotangent[cut(1)]
+    )
+    grad_fu = grad_in(1)
+    q.close(back1=back1, grad_fu=grad_fu, low0_far=low_far)
+
+    def d_gated_of(parts):
+        (d,) = run(
             lambda w, *parts: row_tiles(
                 pre_kernel,
                 parts,
@@ -884,49 +939,106 @@
                 2 * many * width * channels,
                 "d_gated",
             ),
-            w_mix_out,
-            *whole_d[i].parts(),
+            q.w_mo,
+            *parts,
         )
-        d_gated.append(d_i.reshape(n_tensor, piece, channels))
+        return d.reshape(n_tensor, piece, channels)
+
+    low_far = far_rows(q.back1[0])
+    low0 = [q.back0[0]] + q.low0_far
+    whole_d0 = low0 + to_core(low0)
+    low1_near = to_core([q.back1[0]])
+    down_far0, down_kept0 = lower(hidden[0], q.w_ffn_out, q.down_near[0])
+    down_far1, down_kept1 = lower(hidden[1], q.w_ffn_out, q.down_near[1])
+    d_gated0 = d_gated_of(whole_d0)
+    q.close(
+        d_gated0=d_gated0,
+        low1_far=low_far,
+        low1_near=low1_near,
+        whole_d0=whole_d0,
+        down_far=[down_far0, down_far1],
+        down_kept=[down_kept0, down_kept1],
+    )
+
+    down_coming0 = to_far(q.down_far[0])
+    whole_d1 = [q.back1[0]] + q.low1_far + q.low1_near + to_core(q.low1_far)
+    d_gated1 = d_gated_of(whole_d1)
     scanned = recurrence_call(
         backward_kernel,
         order[::-1],
         offsets,
-        [pre, before, *d_gated[:-1], after(d_gated[-1], sequence.last)],
-        [jax.ShapeDtypeStruct((n_tensor, piece, 3 * channels), BF)] * CHUNKS
-        + [jax.ShapeDtypeStruct((n_tensor, rows, 3 * channels), BF)],
+        [q.pre, q.before, q.d_gated0, d_gated1],
+        [jax.ShapeDtypeStruct((n_tensor, piece, 3 * channels), BF)] * CHUNKS,
         channels,
         "recurrence_backward",
     )
-    d_pieces, d_pre = scanned[:-1], scanned[-1]
-    sequence.last = d_pre
-    d_flat = d_pre.reshape(n_tensor * rows, 3 * channels)
-    sums_one = [
-        SummedRows(sequence, d.reshape(-1, 3 * channels), w_mix_in, n_tensor, piece) for d in d_pieces
-    ]
-    grad_mi = []
+    q.last = scanned[-1]
+    q.close(scanned=scanned, whole_d1=whole_d1, down_coming0=down_coming0, sum_fg=sum_fg)
+    d_pieces = [v.reshape(-1, 3 * channels) for v in q.scanned]
+    whole_one = far_a + near_a + far_b + near_b
 
     def grad_mix_in(k):
-        halves = grad(
-            whole_one, [d_flat], "left", depth, "grad_mix_in", fixed=(k, 3), owner=owner
+        return grad(
+            whole_one, d_pieces, "left", depth, "grad_mix_in", fixed=(k, 3), owner=owner
         )
-        grad_mi.append(SummedGrad(sequence, halves, n_dp, near_first))
-
-    def grad_mix_out():
-        halves = grad(
-            [g.reshape(-1, channels) for g in gated],
-            listed(whole_d),
-            "right",
-            depth,
-            "grad_mix_out",
-            owner=owner,
-        )
-        return SummedGrad(sequence, halves, n_dp, near_first)
-
+
+    def over_y(halves):
+        return exchange(halves[0], "dp", n_dp, 1)
+
+    def over_z(halves, offset):
+        return exchange(halves[0], "dp", n_dp, offset)
+
+    def finished(kept, coming, offset):
+        while kept.shape[0] > 1:
+            sent, kept = halves_added(kept, coming)
+            offset *= 2
+            coming = exchange(sent, "dp", n_dp, offset)
+        return kept, coming
+
+    sum_fu = sum_in(q.grad_fu)
+    down_coming1 = to_far(q.down_far[1])
+    grad0 = grad_mix_in(0)
+    q.close(grad0=grad0)
+
+    y0 = over_y(q.grad0)
+    up0 = upper(d_pieces[0], w_mix_in)
+    grad1 = grad_mix_in(1)
+    q.close(grad1=grad1, up0=up0, y0=y0, down_coming1=down_coming1)
+
+    half0 = add_halves(q.grad0[1], q.y0)
+    y1 = over_y(q.grad1)
+    z0 = over_z(half0, 2)
+    (near0,) = to_core([q.up0])
+    up1 = upper(d_pieces[1], w_mix_in)
+    grad2 = grad_mix_in(2)
+    q.close(grad2=grad2, up1=up1, y1=y1, z0=z0, kept_y0=half0[1], near0=near0)
+
+    y2 = over_y(q.grad2)
+    half1 = add_halves(q.grad1[1], q.y1)
+    z1 = over_z(half1, 2)
+    half0 = add_halves(q.kept_y0, q.z0)
+    w0 = over_z(half0, 4)
+    (near1,) = to_core([q.up1])
+    far0, kept0 = lower(d_pieces[0], w_mix_in, q.near0)
+    q.close(far0=far0, kept0=kept0, kept_y1=half1[1], kept_z0=half0[1])
+
+    coming0 = to_far(q.far0)
+    grad3 = grad(
+        q.gated, q.whole_d0 + q.whole_d1, "right", depth, "grad_mix_out", owner=owner
+    )
+    far1, kept1 = lower(d_pieces[1], w_mix_in, near1)
+    q.close(
+        far1=far1, kept1=kept1, coming0=coming0, grad3=grad3, y2=y2, z1=z1, w0=w0
+    )
+
+    firsts = [mix_in_m[0], mix_in_m[1], mix_in_m[2], mix_out_m, ffn_in_m[0], ffn_in_m[1], ffn_out_m]
+    seconds = [mix_in_v[0], mix_in_v[1], mix_in_v[2], mix_out_v, ffn_in_v[0], ffn_in_v[1], ffn_out_v]
     moments = [None] * 7
 
-    def lamb(at, grad):
+    def lamb(at, kept, coming=None):
         tall, wide = weights[at].shape
+        if coming is not None:
+            kept, coming = finished(kept, coming, 4)
 
         def call(kept, *coming):
             if coming:
@@ -938,27 +1050,29 @@
             )
             return update, first, second, jnp.sum(update * update)
 
-        if isinstance(grad, SummedGrad):
-            grad.steps()
-            update, first, second, square = run(call, grad.kept, grad.coming)
-        else:
-            update, first, second, square = run(call, grad)
+        update, first, second, square = run(call, kept, *([] if coming is None else [coming]))
         moments[at] = (first, second, update, square)
 
-    firsts = [mix_in_m[0], mix_in_m[1], mix_in_m[2], mix_out_m, ffn_in_m[0], ffn_in_m[1], ffn_out_m]
-    seconds = [mix_in_v[0], mix_in_v[1], mix_in_v[2], mix_out_v, ffn_in_v[0], ffn_in_v[1], ffn_out_v]
-    grad_mix_in(0)
-    for i in pieces:
-        sums_one[i].high()
-    grad_mix_in(1)
-    sums_one[0].rest()
-    grad_mi[0].step()
-    grad_mix_in(2)
-    for i in range(1, CHUNKS):
-        sums_one[i].rest()
-    grad_mi[1].step()
-    grad_mi[0].step()
-    grad_mo = grad_mix_out()
+    def input_back(kept, coming, own, scaling, d_mid):
+        unit_rows = own.astype(F32) * scaling
+        d_norm, gain = norm_backward(kept + coming.astype(F32), unit_rows, scaling, gains[0])
+        return d_mid + d_norm, gain
+
+    coming1 = to_far(q.far1)
+    half2 = add_halves(q.grad2[1], q.y2)
+    y3 = over_y(q.grad3)
+    z2 = over_z(half2, 2)
+    half1 = add_halves(q.kept_y1, q.z1)
+    w1 = over_z(half1, 4)
+    input_grad0, gain_one0 = run(
+        input_back,
+        *landed(q.kept0, q.coming0),
+        tokens[cut(0)],
+        scale_one[cut(0)],
+        q.back0[1],
+    )
+    lamb(0, q.kept_z0, q.w0)
+    lamb(6, q.sum_fo)
     mixed = run(
         lambda *parts: jnp.concatenate(
             [
@@ -968,37 +1082,49 @@
             axis=0,
         ).astype(BF),
         *middle,
-        *[v.kept for v in downs],
-        *[v.coming for v in downs],
-    )
-    lamb(6, grad_fo)
-    grad_mi[1].step()
-
-    def input_back(kept, coming, own, scaling, d_mid):
-        unit_rows = own.astype(F32) * scaling
-        d_norm, gain = norm_backward(kept + coming.astype(F32), unit_rows, scaling, gains[0])
-        return d_mid + d_norm, gain
-
-    input_grad, gain_one = [], 0.0
-    for i in pieces:
-        at = cut(i)
-        grad_i, gain_i = run(
-            input_back, sums_one[i].kept, sums_one[i].coming, tokens[at], scale_one[at], d_middle[i]
-        )
-        gain_one = gain_one + gain_i
-        input_grad.append(grad_i)
-        if i == 0:
-            lamb(0, grad_mi[0])
-            grad_mo.step()
-            grad_mi[2].step()
-    input_grad = jnp.concatenate(input_grad, axis=0)
-    gain_grads = jnp.stack([gain_one, gain_two])
-    grad_mo.step()
-    lamb(1, grad_mi[1])
-    lamb(4, grad_fi[:, :units])
-    lamb(5, grad_fi[:, units:])
-    lamb(2, grad_mi[2])
-    lamb(3, grad_mo)
+        *[
+            v
+            for pair in zip(
+                *[
+                    landed(k, c)
+                    for k, c in zip(q.down_kept, [q.down_coming0, q.down_coming1])
+                ]
+            )
+            for v in pair
+        ],
+    )
+    q.close(
+        coming1=coming1,
+        y3=y3,
+        z2=z2,
+        kept_y2=half2[1],
+        w1=w1,
+        kept_z1=half1[1],
+        sum_fu=sum_fu,
+    )
+
+    half3 = add_halves(q.grad3[1], q.y3)
+    z3 = over_z(half3, 2)
+    half2 = add_halves(q.kept_y2, q.z2)
+    w2 = over_z(half2, 4)
+    input_grad1, gain_one1 = run(
+        input_back,
+        *landed(q.kept1, q.coming1),
+        tokens[cut(1)],
+        scale_one[cut(1)],
+        q.back1[1],
+    )
+    lamb(1, q.kept_z1, q.w1)
+    q.close(z3=z3, kept_y3=half3[1], w2=w2, kept_z2=half2[1])
+
+    half3 = add_halves(q.kept_y3, q.z3)
+    w3 = over_z(half3, 4)
+    lamb(4, q.sum_fg)
+    lamb(5, q.sum_fu)
+    lamb(2, q.kept_z2, q.w2)
+    lamb(3, half3[1], w3)
+    input_grad = jnp.concatenate([input_grad0, input_grad1], axis=0)
+    gain_grads = jnp.stack([gain_one0 + gain_one1, q.back0[2] + q.back1[2]])
     squares = jnp.concatenate([weight_sq, jnp.stack([m[3] for m in moments])])
     packed = jnp.concatenate([gain_grads.reshape(-1), jnp.pad(squares, (0, SUB * LANES - 14))])
     packed = total_over_mesh(packed.reshape(-1, LANES), n_dp, n_tensor).reshape(-1)
@@ -1008,7 +1134,9 @@
     weight_sq = jnp.concatenate([squares[0], jnp.sum(gains * gains, axis=1)])
     update_sq = jnp.concatenate([squares[1], jnp.sum(gn_update * gn_update, axis=1)])
     trust = jnp.sqrt(weight_sq) / jnp.sqrt(update_sq + NORM_EPSILON)
-    nexts = [w - LEARN_RATE * trust[i] * moments[i][2] for i, w in enumerate(weights)]
+    nexts, copies = new_weights(
+        LEARN_RATE * trust[0:7], (mix_in, mix_out, ffn_in, ffn_out), [m[2] for m in moments]
+    )
     gains_next = gains - LEARN_RATE * trust[7:9][:, None] * gn_update
     layer_norms = jnp.stack([jnp.sqrt(weight_sq), jnp.sqrt(update_sq)])
 
@@ -1017,13 +1145,13 @@
 
     return (
         (mixed, input_grad)
-        + grouped(nexts)
+        + tuple(nexts)
         + (gains_next,)
         + grouped([m[0] for m in moments])
         + (gn_first,)
         + grouped([m[1] for m in moments])
         + (gn_second,)
-        + grouped([n.astype(BF) for n in nexts])
+        + tuple(copies)
         + (layer_norms,)
     )
 

time: 1050 us -> 975 us (0.929)
  waiting for transfers between devices: 293 us -> 255 us
  Pallas kernels: 438 us -> 425 us
  local copies, waits for them, and re-layouts: 65.2 us -> 53.2 us
    ppermute x71 -> x70, waiting for transfers between devices: 293 us -> 249 us  [exchange(): return lax.ppermute(value, axis, [(i, i ^ offset) for i in range(size)])]
    pallas_call x11 -> x7, Pallas kernels: 167 us -> 140 us  [row_tiles(): pl.pallas_call(body, grid=(count,), in_specs=[pl.BlockSpec(memory_space=p...]
    pallas_call x2 -> x3, Pallas kernels: 72.4 us -> 80.1 us  [grad_kernel(): pl.pallas_call(kernel, grid=(steps,), in_specs=in_specs, out_specs=pl.Blo...]
    pallas_call x8 -> x9, Pallas kernels: 96.1 us -> 103 us  [the longest x6 60.7 us: near_added(): pl.pallas_call(by_rows, grid=(2,), in_specs=[rowed(operand), pl.BlockSpec...]
    ppermute x71 -> x70, starting transfers between devices: 64.7 us -> 58.2 us  [exchange(): return lax.ppermute(value, axis, [(i, i ^ offset) for i in range(size)])]
  transfers between devices with their start and end apart: 75 -> 75, of which waited for: 22 -> 35; matrix products, arithmetic and copies ran while one was open for 17% -> 17% of each run, Pallas kernels for 42% -> 41%
where the time goes in v3:
time: 975 us; the launch traced here: 968 us
  Pallas kernels  425 us (44%)
  waiting for transfers between devices  255 us (26%)
  other arithmetic  91.4 us (9%)
  matrix products  69.2 us (7%)
  starting transfers between devices  58.4 us (6%)
  local copies, waits for them, and re-layouts  53.2 us (5%)
  between operations  15.4 us (2%)
    ppermute x70, waiting for transfers between devices, exchange(): return lax.ppermute(value, axis, [(i, i ^ offset) for i in range(size)])  249 us
    pallas_call x7, Pallas kernels, row_tiles(): pl.pallas_call(body, grid=(count,), in_specs=[pl.BlockSpec(memory_space=p...  140 us
    pallas_call x3, Pallas kernels, grad_kernel(): pl.pallas_call(kernel, grid=(steps,), in_specs=in_specs, out_specs=pl.Blo...  80.1 us
    dot_general x8, matrix products, mm_nt(): lax.dot_general(a, b, (((1,), (1,)), ((), ())), preferred_element_type=F32)  69.2 us
    pallas_call x6, Pallas kernels, near_added(): pl.pallas_call(by_rows, grid=(2,), in_specs=[rowed(operand), pl.BlockSpec...  60.7 us
    pallas_call x4, Pallas kernels, grad_kernel(): pl.pallas_call(kernel_by_place, grid_spec=pltpu.PrefetchScalarGridSpec(nu...  60 us
    ppermute x70, starting transfers between devices, exchange(): return lax.ppermute(value, axis, [(i, i ^ offset) for i in range(size)])  58.2 us
    pallas_call x2, Pallas kernels, recurrence_call(): pl.pallas_call(kernel, grid_spec=pltpu.PrefetchScalarGridSpec(num_scalar_...  41.9 us
  transfers between devices with their start and end apart: 75, of which 35 were waited for; matrix products, arithmetic and copies ran while one was open for 17% of the time, Pallas kernels for 41%

profile of v3, /device:TPU:0, one launch (start us, length us, event | category | flops | bytes accessed | tf_op | source)
XLA Modules:
  0.0 967.8 jit_solution(10980706363551539571)
XLA Ops:
  21.0 13.4 %collective-permute-done.1 = bf16[256,1536]{1,0:T(8,128)(2,1)S(1)} collective-permute-done((bf16[256,1536]{1,0:T(8,128)(2,1)S(1)}, bf16[256,1536]{1,0:T(8,128)(2,1)S(1)}, u32[]{:S(2)}, u32[]{:S(2)}) %collective-permute-start.1) | collective-permute-done | bytes 786464 | tf_op jit(solution)/shard_map/ppermute | solution.py:31
  36.5 18.1 %collective-permute-done.3 = bf16[256,1536]{1,0:T(8,128)(2,1)S(1)} collective-permute-done((bf16[256,1536]{1,0:T(8,128)(2,1)S(1)}, bf16[256,1536]{1,0:T(8,128)(2,1)S(1)}, u32[]{:S(2)}, u32[]{:S(2)}) %collective-permute-start.3) | collective-permute-done | bytes 786464 | tf_op jit(solution)/shard_map/ppermute | solution.py:31
  65.4 15.5 %collective-permute-done.5 = bf16[256,1536]{1,0:T(8,128)(2,1)} collective-permute-done((bf16[256,1536]{1,0:T(8,128)(2,1)}, bf16[256,1536]{1,0:T(8,128)(2,1)}, u32[]{:S(2)}, u32[]{:S(2)}) %collective-permute-start.5) | collective-permute-done | bytes 786464 | tf_op jit(solution)/shard_map/ppermute | solution.py:31
  81.0 16.3 %collective-permute-done.6 = bf16[256,1536]{1,0:T(8,128)(2,1)} collective-permute-done((bf16[256,1536]{1,0:T(8,128)(2,1)}, bf16[256,1536]{1,0:T(8,128)(2,1)}, u32[]{:S(2)}, u32[]{:S(2)}) %collective-permute-start.6) | collective-permute-done | bytes 786464 | tf_op jit(solution)/shard_map/ppermute | solution.py:31
  128.8 27.8 %pre.1 = f32[3072,1536]{1,0:T(8,128)} custom-call(bf16[384,2048]{1,0:T(8,128)(2,1)} %copy-done.57, bf16[384,2048]{1,0:T(8,128)(2,1)} %get-tuple-element.288.refs_1_.refs_4_, bf16[384,2048]{1,0:T(8,128)(2,1)} %copy-done.108, bf16[384,2048]{1,0:T(8,128)(2,1)} %collective-permute-done.4.refs_3_.refs_5_, bf16[384,2048]{1,0:T(8,128)(2,1)} %copy-done.110, ...), custom_call_target="tpu_custom_call" | custom-call | flops 34923765760 | bytes 12582912 | tf_op jit(solution)/shard_map/pre/pallas_call | solution.py:231
  161.7 18.9 %recurrence_forward.1 = (f32[4,768,512]{2,1,0:T(8,128)}, bf16[4,384,512]{2,1,0:T(8,128)(2,1)S(1)}, bf16[4,384,512]{2,1,0:T(8,128)(2,1)S(1)}) custom-call(s32[4]{0:T(128)S(1)} %gather_fusion, s32[4]{0:T(128)S(1)} %bitcast_subtract_fusion.offsets, f32[4,768,1536]{2,1,0:T(8,128)} %bitcast.218), custom_call_target="tpu_custom_call" | custom-call | flops 23592960000 | bytes 37748736 | tf_op jit(solution)/shard_map/recurrence_forward/pallas_call | solution.py:524
  201.0 28.3 %collective-permute-done.22.refs_5_.refs_1_ = bf16[384,2048]{1,0:T(8,128)(2,1)S(1)} collective-permute-done((bf16[384,2048]{1,0:T(8,128)(2,1)}, bf16[384,2048]{1,0:T(8,128)(2,1)S(1)}, u32[]{:S(2)}, u32[]{:S(2)}) %collective-permute-start.22) | collective-permute-done | bytes 1572896 | tf_op jit(solution)/shard_map/ppermute | solution.py:31
  238.4 28.1 %collective-permute-done.23 = bf16[384,2048]{1,0:T(8,128)(2,1)} collective-permute-done((bf16[384,2048]{1,0:T(8,128)(2,1)}, bf16[384,2048]{1,0:T(8,128)(2,1)}, u32[]{:S(2)}, u32[]{:S(2)}) %collective-permute-start.23) | collective-permute-done | bytes 1572896 | tf_op jit(solution)/shard_map/ppermute | solution.py:31
  276.6 25.0 %collective-permute-done.26 = bf16[384,2048]{1,0:T(8,128)(2,1)} collective-permute-done((bf16[384,2048]{1,0:T(8,128)(2,1)}, bf16[384,2048]{1,0:T(8,128)(2,1)}, u32[]{:S(2)}, u32[]{:S(2)}) %collective-permute-start.26) | collective-permute-done | bytes 1572896 | tf_op jit(solution)/shard_map/ppermute | solution.py:31
  316.1 19.7 %collective-permute-done.27.refs_1_ = bf16[384,2048]{1,0:T(8,128)(2,1)} collective-permute-done((bf16[384,2048]{1,0:T(8,128)(2,1)}, bf16[384,2048]{1,0:T(8,128)(2,1)}, u32[]{:S(2)}, u32[]{:S(2)}) %collective-permute-start.27) | collective-permute-done | bytes 1572896 | tf_op jit(solution)/shard_map/ppermute | solution.py:31
  339.6 29.9 %gate_up.2 = (bf16[1536,1408]{1,0:T(8,128)(2,1)}, bf16[1536,1408]{1,0:T(8,128)(2,1)}, bf16[1536,1408]{1,0:T(8,128)(2,1)}) custom-call(bf16[384,2048]{1,0:T(8,128)(2,1)} %multiply_convert_fusion.1.refs_0_, bf16[384,2048]{1,0:T(8,128)(2,1)} %collective-permute-done.27.refs_1_, bf16[384,2048]{1,0:T(8,128)(2,1)} %collective-permute-done.28.refs_2_, ...), custom_call_target="tpu_custom_call" | custom-call | flops 32346783744 | bytes 23068672 | tf_op jit(solution)/shard_map/gate_up/pallas_call | solution.py:231
  378.5 30.4 %gate_up.3 = (bf16[1536,1408]{1,0:T(8,128)(2,1)}, bf16[1536,1408]{1,0:T(8,128)(2,1)}, bf16[1536,1408]{1,0:T(8,128)(2,1)}) custom-call(bf16[384,2048]{1,0:T(8,128)(2,1)} %copy-done.59, bf16[384,2048]{1,0:T(8,128)(2,1)} %copy-done.116, bf16[384,2048]{1,0:T(8,128)(2,1)} %copy-done.117, bf16[384,2048]{1,0:T(8,128)(2,1)} %copy-done.119, ...), custom_call_target="tpu_custom_call" | custom-call | flops 32346783744 | bytes 23068672 | tf_op jit(solution)/shard_map/gate_up/pallas_call | solution.py:231
  408.9 25.7 %grad_out.1 = bf16[1408,2048]{1,0:T(8,128)(2,1)} custom-call(bf16[384,2048]{1,0:T(8,128)(2,1)} %copy-done.58, bf16[384,2048]{1,0:T(8,128)(2,1)} %collective-permute-done.16.refs_1_, bf16[384,2048]{1,0:T(8,128)(2,1)} %collective-permute-done.18.refs_2_, bf16[384,2048]{1,0:T(8,128)(2,1)} %copy-done.112, bf16[384,2048]{1,0:T(8,128)(2,1)} %get-tuple-element.332.refs_4_.refs_0_, ...), custom_call_target="tpu_custom_call" | custom-call | flops 32346783744 | bytes 5767168 | tf_op jit(solution)/shard_map/grad_out/pallas_call | solution.py:349
  434.6 17.2 %gate_up_back.2.v.refs_8_ = bf16[1536,2816]{1,0:T(8,128)(2,1)} custom-call(bf16[384,2048]{1,0:T(8,128)(2,1)} %copy-done.58, bf16[384,2048]{1,0:T(8,128)(2,1)} %collective-permute-done.16.refs_1_, bf16[384,2048]{1,0:T(8,128)(2,1)} %collective-permute-done.18.refs_2_, bf16[384,2048]{1,0:T(8,128)(2,1)} %copy-done.112, ...), custom_call_target="tpu_custom_call" | custom-call | flops 18173392896 | bytes 11534336 | tf_op jit(solution)/shard_map/gate_up_back/pallas_call | solution.py:231
  451.8 14.4 %fusion.10 = bf16[768,2048]{1,0:T(8,128)(2,1)} fusion(bf16[2048,2816]{1,0:T(8,128)(2,1)} %all-gather.3.cloned.1.call-done.refs_4_.w, bf16[1536,2816]{1,0:T(8,128)(2,1)} %gate_up_back.2.v.refs_8_), kind=kOutput, calls=%fused_computation.22 | convolution fusion | flops 8859942912 | bytes 19005440 | tf_op jit(solution)/shard_map/dot_general | solution.py:43
  466.6 17.2 %gate_up_back.3.v.refs_9_ = bf16[1536,2816]{1,0:T(8,128)(2,1)} custom-call(bf16[384,2048]{1,0:T(8,128)(2,1)} %get-tuple-element.332.refs_4_.refs_0_, bf16[384,2048]{1,0:T(8,128)(2,1)} %copy-done.118, bf16[384,2048]{1,0:T(8,128)(2,1)} %collective-permute-done.24.refs_6_.refs_2_, bf16[384,2048]{1,0:T(8,128)(2,1)} %collective-permute-done.25.refs_7_.refs_3_, ...), custom_call_target="tpu_custom_call" | custom-call | flops 18173392896 | bytes 11534336 | tf_op jit(solution)/shard_map/gate_up_back/pallas_call | solution.py:231
  483.9 14.9 %fusion.13 = bf16[768,2048]{1,0:T(8,128)(2,1)} fusion(bf16[2048,2816]{1,0:T(8,128)(2,1)} %all-gather.3.cloned.1.call-done.refs_4_.w, bf16[1536,2816]{1,0:T(8,128)(2,1)} %gate_up_back.3.v.refs_9_), kind=kOutput, calls=%fused_computation.23 | convolution fusion | flops 8859942912 | bytes 19005440 | tf_op jit(solution)/shard_map/dot_general | solution.py:43
  500.5 15.5 %near_added.10 = (bf16[384,2048]{1,0:T(8,128)(2,1)}, f32[384,2048]{1,0:T(8,128)}) custom-call(bf16[1536,2816]{1,0:T(8,128)(2,1)} %gate_up_back.2.v.refs_8_, bf16[2048,2816]{1,0:T(8,128)(2,1)} %all-gather.3.cloned.1.call-done.refs_4_.w, bf16[768,2048]{1,0:T(8,128)(2,1)} %copy-done.106), custom_call_target="tpu_custom_call" | custom-call | flops 18173392896 | bytes 11534336 | tf_op jit(solution)/shard_map/near_added/pallas_call | solution.py:129
  535.2 15.8 %near_added.11 = (bf16[384,2048]{1,0:T(8,128)(2,1)}, f32[384,2048]{1,0:T(8,128)}) custom-call(bf16[1536,2816]{1,0:T(8,128)(2,1)} %gate_up_back.3.v.refs_9_, bf16[2048,2816]{1,0:T(8,128)(2,1)} %all-gather.3.cloned.1.call-done.refs_4_.w, bf16[768,2048]{1,0:T(8,128)(2,1)} %collective-permute-done.34.added), custom_call_target="tpu_custom_call" | custom-call | flops 18173392896 | bytes 11534336 | tf_op jit(solution)/shard_map/near_added/pallas_call | solution.py:129
  558.6 27.3 %grad_in.2 = bf16[2048,1408]{1,0:T(8,128)(2,1)} custom-call(bf16[384,2048]{1,0:T(8,128)(2,1)} %multiply_convert_fusion.1.refs_0_, bf16[384,2048]{1,0:T(8,128)(2,1)} %collective-permute-done.27.refs_1_, bf16[384,2048]{1,0:T(8,128)(2,1)} %collective-permute-done.28.refs_2_, bf16[384,2048]{1,0:T(8,128)(2,1)} %collective-permute-done.29.refs_3_, ...), custom_call_target="tpu_custom_call" | custom-call | flops 32346783744 | bytes 5767168 | tf_op jit(solution)/shard_map/grad_in/pallas_call | solution.py:349
  606.3 27.1 %grad_in.3 = bf16[2048,1408]{1,0:T(8,128)(2,1)} custom-call(bf16[384,2048]{1,0:T(8,128)(2,1)} %multiply_convert_fusion.1.refs_0_, bf16[384,2048]{1,0:T(8,128)(2,1)} %collective-permute-done.27.refs_1_, bf16[384,2048]{1,0:T(8,128)(2,1)} %collective-permute-done.28.refs_2_, bf16[384,2048]{1,0:T(8,128)(2,1)} %collective-permute-done.29.refs_3_, ...), custom_call_target="tpu_custom_call" | custom-call | flops 32346783744 | bytes 5767168 | tf_op jit(solution)/shard_map/grad_in/pallas_call | solution.py:349
  635.4 11.4 %near_added.12 = (bf16[384,2048]{1,0:T(8,128)(2,1)}, f32[384,2048]{1,0:T(8,128)}) custom-call(bf16[1536,1408]{1,0:T(8,128)(2,1)} %get-tuple-element.413.refs_8_.v, bf16[2048,1408]{1,0:T(8,128)(2,1)} %all-gather.5.cloned.1.call-done.refs_4_.w, bf16[768,2048]{1,0:T(8,128)(2,1)} %collective-permute-done.37.n), custom_call_target="tpu_custom_call" | custom-call | flops 11086696448 | bytes 5767168 | tf_op jit(solution)/shard_map/near_added/pallas_call | solution.py:157
  646.8 11.3 %near_added.13 = (bf16[384,2048]{1,0:T(8,128)(2,1)}, f32[384,2048]{1,0:T(8,128)}) custom-call(bf16[1536,1408]{1,0:T(8,128)(2,1)} %get-tuple-element.416.refs_9_.v, bf16[2048,1408]{1,0:T(8,128)(2,1)} %all-gather.5.cloned.1.call-done.refs_4_.w, bf16[768,2048]{1,0:T(8,128)(2,1)} %collective-permute-done.38.n), custom_call_target="tpu_custom_call" | custom-call | flops 11086696448 | bytes 5767168 | tf_op jit(solution)/shard_map/near_added/pallas_call | solution.py:157
  683.2 23.0 %recurrence_backward.1 = (bf16[4,384,1536]{2,1,0:T(8,128)(2,1)}, bf16[4,384,1536]{2,1,0:T(8,128)(2,1)}) custom-call(s32[4]{0:T(128)S(1)} %rev.3.order, s32[4]{0:T(128)S(1)} %copy-done.4, f32[4,768,1536]{2,1,0:T(8,128)} %bitcast.219, f32[4,768,512]{2,1,0:T(8,128)} %get-tuple-element.403.before, f32[4,384,512]{2,1,0:T(8,128)S(1)} %bitcast.186, ...), custom_call_target="tpu_custom_call" | custom-call | flops 23592960000 | bytes 37748736 | tf_op jit(solution)/shard_map/recurrence_backward/pallas_call | solution.py:524
  709.9 14.8 %grad_mix_in.3 = (bf16[4,256,512]{2,1,0:T(8,128)(2,1)}, bf16[4,256,512]{2,1,0:T(8,128)(2,1)}) custom-call(s32[8]{0:T(128)} %stack.130.owners_ref, bf16[384,2048]{1,0:T(8,128)(2,1)} %copy-done.57, bf16[384,2048]{1,0:T(8,128)(2,1)} %copy-done.108, bf16[384,2048]{1,0:T(8,128)(2,1)} %copy-done.110, bf16[384,2048]{1,0:T(8,128)(2,1)} %copy-done.111, ...), custom_call_target="tpu_custom_call" | custom-call | flops 14307921920 | bytes 2097152 | tf_op jit(solution)/shard_map/grad_mix_in/pallas_call | solution.py:373
  735.4 15.3 %grad_mix_in.4 = (bf16[4,256,512]{2,1,0:T(8,128)(2,1)}, bf16[4,256,512]{2,1,0:T(8,128)(2,1)}) custom-call(s32[8]{0:T(128)} %stack.130.owners_ref, bf16[384,2048]{1,0:T(8,128)(2,1)} %copy-done.57, bf16[384,2048]{1,0:T(8,128)(2,1)} %copy-done.108, bf16[384,2048]{1,0:T(8,128)(2,1)} %copy-done.110, bf16[384,2048]{1,0:T(8,128)(2,1)} %copy-done.111, ...), custom_call_target="tpu_custom_call" | custom-call | flops 14307921920 | bytes 2097152 | tf_op jit(solution)/shard_map/grad_mix_in/pallas_call | solution.py:373
  771.5 15.1 %grad_mix_in.5 = (bf16[4,256,512]{2,1,0:T(8,128)(2,1)}, bf16[4,256,512]{2,1,0:T(8,128)(2,1)}) custom-call(s32[8]{0:T(128)} %stack.130.owners_ref, bf16[384,2048]{1,0:T(8,128)(2,1)} %copy-done.57, bf16[384,2048]{1,0:T(8,128)(2,1)} %copy-done.108, bf16[384,2048]{1,0:T(8,128)(2,1)} %copy-done.110, bf16[384,2048]{1,0:T(8,128)(2,1)} %copy-done.111, ...), custom_call_target="tpu_custom_call" | custom-call | flops 14307921920 | bytes 2097152 | tf_op jit(solution)/shard_map/grad_mix_in/pallas_call | solution.py:373
  800.1 11.6 %near_added.14 = (bf16[384,2048]{1,0:T(8,128)(2,1)}, f32[384,2048]{1,0:T(8,128)}) custom-call(bf16[1536,1536]{1,0:T(8,128)(2,1)} %bitcast.229, bf16[2048,1536]{1,0:T(8,128)(2,1)} %constant_dynamic-update-slice_fusion.4.refs_8_.w, bf16[768,2048]{1,0:T(8,128)(2,1)} %collective-permute-done.50.n), custom_call_target="tpu_custom_call" | custom-call | flops 11730940928 | bytes 6291456 | tf_op jit(solution)/shard_map/near_added/pallas_call | solution.py:157
  819.1 14.7 %grad_mix_out.1 = (bf16[4,512,256]{2,1,0:T(8,128)(2,1)}, bf16[4,512,256]{2,1,0:T(8,128)(2,1)}) custom-call(s32[8]{0:T(128)} %stack.130.owners_ref, bf16[384,2048]{1,0:T(8,128)(2,1)} %get-tuple-element.464.refs_0_, bf16[384,2048]{1,0:T(8,128)(2,1)} %collective-permute-done.39.refs_1_, bf16[384,2048]{1,0:T(8,128)(2,1)} %collective-permute-done.40.refs_2_, ...), custom_call_target="tpu_custom_call" | custom-call | flops 14307921920 | bytes 2097152 | tf_op jit(solution)/shard_map/grad_mix_out/pallas_call | solution.py:373
  833.9 11.8 %near_added.15 = (bf16[384,2048]{1,0:T(8,128)(2,1)}, f32[384,2048]{1,0:T(8,128)}) custom-call(bf16[1536,1536]{1,0:T(8,128)(2,1)} %bitcast.224, bf16[2048,1536]{1,0:T(8,128)(2,1)} %constant_dynamic-update-slice_fusion.4.refs_8_.w, bf16[768,2048]{1,0:T(8,128)(2,1)} %collective-permute-done.51.n), custom_call_target="tpu_custom_call" | custom-call | flops 11730940928 | bytes 6291456 | tf_op jit(solution)/shard_map/near_added/pallas_call | solution.py:157
  876.2 15.1 %collective-permute-done.57 = bf16[4,512,256]{2,1,0:T(8,128)(2,1)} collective-permute-done((bf16[4,512,256]{2,1,0:T(8,128)(2,1)}, bf16[4,512,256]{2,1,0:T(8,128)(2,1)}, u32[]{:S(2)}, u32[]{:S(2)}) %collective-permute-start.57) | collective-permute-done | bytes 1048608 | tf_op jit(solution)/shard_map/ppermute | solution.py:31
  948.8 10.8 %new_weights.1 = (f32[3,256,512]{2,1,0:T(8,128)}, f32[512,256]{1,0:T(8,128)}, f32[2,256,1408]{2,1,0:T(8,128)}, f32[1408,256]{1,0:T(8,128)}, bf16[3,256,512]{2,1,...) custom-call(f32[7]{0:T(128)} %slice_multiply_fusion.7.factor, ...), custom_call_target="tpu_custom_call" | custom-call | tf_op jit(solution)/shard_map/new_weights/pallas_call | solution.py:605
  (517 shorter events, 350.7 us)
Async XLA Ops:
  7.2 294.4 %all-gather.3.cloned.1.call-start = ((), (), s32[]{:S(2)}) async-start(), calls=%async_computation.3 | async-start | bytes 12976128 | tf_op jit(solution)/shard_map/all_gather | solution.py:749
  12.4 42.2 %collective-permute-start = (bf16[384,2048]{1,0:T(8,128)(2,1)S(1)}, bf16[384,2048]{1,0:T(8,128)(2,1)S(1)}, u32[]{:S(2)}, u32[]{:S(2)}) collective-permute-start(bf16[384,2048]{1,0:T(8,128)(2,1)S(1)} %get-tuple-element.444.refs_0_), channel_id=1, source_target_pairs={{0,2},{1,3},{2,0},{3,1},{4,6},{5,7},{6,4},{7,5},{8,10},{9,11},{10,... | collective-permute-start | bytes 4718600 | tf_op jit(solution)/shard_map/ppermute | solution.py:31
  18.5 36.1 %collective-permute-start.3 = (bf16[256,1536]{1,0:T(8,128)(2,1)S(1)}, bf16[256,1536]{1,0:T(8,128)(2,1)S(1)}, u32[]{:S(2)}, u32[]{:S(2)}) collective-permute-start(bf16[256,1536]{1,0:T(8,128)(2,1)S(1)} %pad_maximum_fusion.8), channel_id=1, source_target_pairs={{0,24},{4,28},{8,16},{12,20},{16,8},{20,12},{24,0},{28,4},{1,25},{... | collective-permute-start | bytes 2359304 | tf_op jit(solution)/shard_map/ppermute | solution.py:31
  54.7 44.9 %collective-permute-start.4 = (bf16[384,2048]{1,0:T(8,128)(2,1)}, bf16[384,2048]{1,0:T(8,128)(2,1)}, u32[]{:S(2)}, u32[]{:S(2)}) collective-permute-start(bf16[384,2048]{1,0:T(8,128)(2,1)} %get-tuple-element.288.refs_1_.refs_4_), channel_id=1, source_target_pairs={{0,2},{1,3},{2,0},{3,1},{4,6},{5,7},{6,4},{7,5},{8,10},{9,11},{10,... | collective-permute-start | bytes 4718600 | tf_op jit(solution)/shard_map/ppermute | solution.py:31
  59.3 40.3 %collective-permute-start.9 = (bf16[384,2048]{1,0:T(8,128)(2,1)}, bf16[384,2048]{1,0:T(8,128)(2,1)}, u32[]{:S(2)}, u32[]{:S(2)}) collective-permute-start(bf16[384,2048]{1,0:T(8,128)(2,1)} %get-tuple-element.288.refs_1_.refs_4_), channel_id=1, source_target_pairs={{0,1},{1,0},{2,3},{3,2},{4,5},{5,4},{6,7},{7,6},{8,9},{9,8},{10,11... | collective-permute-start | bytes 4718600 | tf_op jit(solution)/shard_map/ppermute | solution.py:31
  60.8 36.5 %collective-permute-start.6 = (bf16[256,1536]{1,0:T(8,128)(2,1)}, bf16[256,1536]{1,0:T(8,128)(2,1)}, u32[]{:S(2)}, u32[]{:S(2)}) collective-permute-start(bf16[256,1536]{1,0:T(8,128)(2,1)} %copy-done.78), channel_id=1, source_target_pairs={{0,4},{4,0},{8,12},{12,8},{16,20},{20,16},{24,28},{28,24},{1,5},{5... | collective-permute-start | bytes 2359304 | tf_op jit(solution)/shard_map/ppermute | solution.py:31
  62.3 37.3 %collective-permute-start.7 = (bf16[256,1536]{1,0:T(8,128)(2,1)}, bf16[256,1536]{1,0:T(8,128)(2,1)}, u32[]{:S(2)}, u32[]{:S(2)}) collective-permute-start(bf16[256,1536]{1,0:T(8,128)(2,1)} %copy-done.37), channel_id=1, source_target_pairs={{0,16},{4,20},{8,24},{12,28},{16,0},{20,4},{24,8},{28,12},{1,17},{... | collective-permute-start | bytes 2359304 | tf_op jit(solution)/shard_map/ppermute | solution.py:31
  124.4 310.2 %all-gather.5.cloned.1.call-start = ((), (), s32[]{:S(2)}) async-start(), calls=%async_computation.4 | async-start | bytes 6488064 | tf_op jit(solution)/shard_map/all_gather | solution.py:818
  127.3 56.4 %collective-permute-start.18 = (bf16[384,2048]{1,0:T(8,128)(2,1)S(1)}, bf16[384,2048]{1,0:T(8,128)(2,1)}, u32[]{:S(2)}, u32[]{:S(2)}) collective-permute-start(bf16[384,2048]{1,0:T(8,128)(2,1)S(1)} %get-tuple-element.579.refs_0_), channel_id=1, source_target_pairs={{0,1},{1,0},{2,3},{3,2},{4,5},{5,4},{6,7},{7,6},{8,9},{9,8},{10,11... | collective-permute-start | bytes 4718600 | tf_op jit(solution)/shard_map/ppermute | solution.py:31
  128.3 52.7 %collective-permute-start.17 = (bf16[1024,512]{1,0:T(8,128)(2,1)S(1)}, bf16[1024,512]{1,0:T(8,128)(2,1)S(1)}, u32[]{:S(2)}, u32[]{:S(2)}) collective-permute-start(bf16[1024,512]{1,0:T(8,128)(2,1)S(1)} %pad_maximum_fusion.7), channel_id=1, source_target_pairs={{0,4},{4,0},{8,12},{12,8},{16,20},{20,16},{24,28},{28,24},{1,5},{5... | collective-permute-start | bytes 3145736 | tf_op jit(solution)/shard_map/ppermute | solution.py:31
  191.0 38.3 %collective-permute-start.21 = (bf16[768,2048]{1,0:T(8,128)(2,1)S(1)}, bf16[768,2048]{1,0:T(8,128)(2,1)S(1)}, u32[]{:S(2)}, u32[]{:S(2)}) collective-permute-start(bf16[768,2048]{1,0:T(8,128)(2,1)S(1)} %convolution_convert_fusion), channel_id=1, source_target_pairs={{0,1},{1,0},{2,3},{3,2},{4,5},{5,4},{6,7},{7,6},{8,9},{9,8},{10,11... | collective-permute-start | bytes 9437192 | tf_op jit(solution)/shard_map/ppermute | solution.py:31
  192.7 36.6 %collective-permute-start.22 = (bf16[384,2048]{1,0:T(8,128)(2,1)}, bf16[384,2048]{1,0:T(8,128)(2,1)S(1)}, u32[]{:S(2)}, u32[]{:S(2)}) collective-permute-start(bf16[384,2048]{1,0:T(8,128)(2,1)} %get-tuple-element.332.refs_4_.refs_0_), channel_id=1, source_target_pairs={{0,2},{1,3},{2,0},{3,1},{4,6},{5,7},{6,4},{7,5},{8,10},{9,11},{10,... | collective-permute-start | bytes 4718600 | tf_op jit(solution)/shard_map/ppermute | solution.py:31
  193.3 45.1 %collective-permute-start.24 = (bf16[384,2048]{1,0:T(8,128)(2,1)}, bf16[384,2048]{1,0:T(8,128)(2,1)}, u32[]{:S(2)}, u32[]{:S(2)}) collective-permute-start(bf16[384,2048]{1,0:T(8,128)(2,1)} %get-tuple-element.332.refs_4_.refs_0_), channel_id=1, source_target_pairs={{0,1},{1,0},{2,3},{3,2},{4,5},{5,4},{6,7},{7,6},{8,9},{9,8},{10,11... | collective-permute-start | bytes 4718600 | tf_op jit(solution)/shard_map/ppermute | solution.py:31
  230.5 36.0 %collective-permute-start.23 = (bf16[384,2048]{1,0:T(8,128)(2,1)}, bf16[384,2048]{1,0:T(8,128)(2,1)}, u32[]{:S(2)}, u32[]{:S(2)}) collective-permute-start(bf16[384,2048]{1,0:T(8,128)(2,1)} %get-tuple-element.333), channel_id=1, source_target_pairs={{0,2},{1,3},{2,0},{3,1},{4,6},{5,7},{6,4},{7,5},{8,10},{9,11},{10,... | collective-permute-start | bytes 4718600 | tf_op jit(solution)/shard_map/ppermute | solution.py:31
  337.0 258.3 %reduce-scatter.4.cloned.1.call-start = ((), (), s32[]{:S(2)}) async-start(), calls=%async_computation.5 | async-start | bytes 6488064 | tf_op jit(solution)/shard_map/reduce_scatter | solution.py:887
  337.0 36.9 %collective-permute-start.30 = (bf16[384,2048]{1,0:T(8,128)(2,1)S(1)}, bf16[384,2048]{1,0:T(8,128)(2,1)S(1)}, u32[]{:S(2)}, u32[]{:S(2)}) collective-permute-start(bf16[384,2048]{1,0:T(8,128)(2,1)S(1)} %multiply_convert_fusion.refs_0_.refs_4_), channel_id=1, source_target_pairs={{0,2},{1,3},{2,0},{3,1},{4,6},{5,7},{6,4},{7,5},{8,10},{9,11},{10,... | collective-permute-start | bytes 4718600 | tf_op jit(solution)/shard_map/ppermute | solution.py:31
  337.7 36.2 %collective-permute-start.31 = (bf16[384,2048]{1,0:T(8,128)(2,1)S(1)}, bf16[384,2048]{1,0:T(8,128)(2,1)S(1)}, u32[]{:S(2)}, u32[]{:S(2)}) collective-permute-start(bf16[384,2048]{1,0:T(8,128)(2,1)S(1)} %multiply_convert_fusion.refs_0_.refs_4_), channel_id=1, source_target_pairs={{0,1},{1,0},{2,3},{3,2},{4,5},{5,4},{6,7},{7,6},{8,9},{9,8},{10,11... | collective-permute-start | bytes 4718600 | tf_op jit(solution)/shard_map/ppermute | solution.py:31
  483.8 226.0 %reduce-scatter.6.cloned.1.call-start = ((), (), s32[]{:S(2)}) async-start(), calls=%async_computation.6 | async-start | bytes 6488064 | tf_op jit(solution)/shard_map/reduce_scatter | solution.py:911
  516.2 36.9 %collective-permute-start.35 = (bf16[384,2048]{1,0:T(8,128)(2,1)}, bf16[384,2048]{1,0:T(8,128)(2,1)S(1)}, u32[]{:S(2)}, u32[]{:S(2)}) collective-permute-start(bf16[384,2048]{1,0:T(8,128)(2,1)} %get-tuple-element.385), channel_id=1, source_target_pairs={{0,2},{1,3},{2,0},{3,1},{4,6},{5,7},{6,4},{7,5},{8,10},{9,11},{10,... | collective-permute-start | bytes 4718600 | tf_op jit(solution)/shard_map/ppermute | solution.py:31
  553.1 36.3 %collective-permute-start.36 = (bf16[384,2048]{1,0:T(8,128)(2,1)}, bf16[384,2048]{1,0:T(8,128)(2,1)}, u32[]{:S(2)}, u32[]{:S(2)}) collective-permute-start(bf16[384,2048]{1,0:T(8,128)(2,1)} %get-tuple-element.393), channel_id=1, source_target_pairs={{0,2},{1,3},{2,0},{3,1},{4,6},{5,7},{6,4},{7,5},{8,10},{9,11},{10,... | collective-permute-start | bytes 4718600 | tf_op jit(solution)/shard_map/ppermute | solution.py:31
  595.3 280.9 %reduce-scatter.8.cloned.1.call-start = ((), (), s32[]{:S(2)}) async-start(), calls=%async_computation.7 | async-start | bytes 6488064 | tf_op jit(solution)/shard_map/reduce_scatter | solution.py:911
  596.0 37.5 %collective-permute-start.39 = (bf16[384,2048]{1,0:T(8,128)(2,1)}, bf16[384,2048]{1,0:T(8,128)(2,1)}, u32[]{:S(2)}, u32[]{:S(2)}) collective-permute-start(bf16[384,2048]{1,0:T(8,128)(2,1)} %get-tuple-element.464.refs_0_), channel_id=1, source_target_pairs={{0,2},{1,3},{2,0},{3,1},{4,6},{5,7},{6,4},{7,5},{8,10},{9,11},{10,... | collective-permute-start | bytes 4718600 | tf_op jit(solution)/shard_map/ppermute | solution.py:31
  597.5 60.6 %collective-permute-start.40 = (bf16[384,2048]{1,0:T(8,128)(2,1)}, bf16[384,2048]{1,0:T(8,128)(2,1)}, u32[]{:S(2)}, u32[]{:S(2)}) collective-permute-start(bf16[384,2048]{1,0:T(8,128)(2,1)} %get-tuple-element.464.refs_0_), channel_id=1, source_target_pairs={{0,1},{1,0},{2,3},{3,2},{4,5},{5,4},{6,7},{7,6},{8,9},{9,8},{10,11... | collective-permute-start | bytes 4718600 | tf_op jit(solution)/shard_map/ppermute | solution.py:31
  633.5 36.4 %collective-permute-start.42 = (bf16[384,2048]{1,0:T(8,128)(2,1)S(1)}, bf16[384,2048]{1,0:T(8,128)(2,1)S(1)}, u32[]{:S(2)}, u32[]{:S(2)}) collective-permute-start(bf16[384,2048]{1,0:T(8,128)(2,1)S(1)} %copy-done.55), channel_id=1, source_target_pairs={{0,2},{1,3},{2,0},{3,1},{4,6},{5,7},{6,4},{7,5},{8,10},{9,11},{10,... | collective-permute-start | bytes 4718600 | tf_op jit(solution)/shard_map/ppermute | solution.py:31
  672.3 37.5 %collective-permute-start.45 = (bf16[384,2048]{1,0:T(8,128)(2,1)}, bf16[384,2048]{1,0:T(8,128)(2,1)}, u32[]{:S(2)}, u32[]{:S(2)}) collective-permute-start(bf16[384,2048]{1,0:T(8,128)(2,1)} %get-tuple-element.428), channel_id=1, source_target_pairs={{0,2},{1,3},{2,0},{3,1},{4,6},{5,7},{6,4},{7,5},{8,10},{9,11},{10,... | collective-permute-start | bytes 4718600 | tf_op jit(solution)/shard_map/ppermute | solution.py:31
  673.6 77.1 %collective-permute-start.47 = (bf16[384,2048]{1,0:T(8,128)(2,1)}, bf16[384,2048]{1,0:T(8,128)(2,1)S(1)}, u32[]{:S(2)}, u32[]{:S(2)}) collective-permute-start(bf16[384,2048]{1,0:T(8,128)(2,1)} %get-tuple-element.439), channel_id=1, source_target_pairs={{0,2},{1,3},{2,0},{3,1},{4,6},{5,7},{6,4},{7,5},{8,10},{9,11},{10,... | collective-permute-start | bytes 4718600 | tf_op jit(solution)/shard_map/ppermute | solution.py:31
  759.0 38.3 %collective-permute-start.48 = (bf16[4,256,512]{2,1,0:T(8,128)(2,1)}, bf16[4,256,512]{2,1,0:T(8,128)(2,1)}, u32[]{:S(2)}, u32[]{:S(2)}) collective-permute-start(bf16[4,256,512]{2,1,0:T(8,128)(2,1)} %get-tuple-element.440), channel_id=1, source_target_pairs={{0,4},{4,0},{8,12},{12,8},{16,20},{20,16},{24,28},{28,24},{1,5},{5... | collective-permute-start | bytes 3145736 | tf_op jit(solution)/shard_map/ppermute | solution.py:31
  797.3 36.6 %collective-permute-start.51 = (bf16[768,2048]{1,0:T(8,128)(2,1)}, bf16[768,2048]{1,0:T(8,128)(2,1)}, u32[]{:S(2)}, u32[]{:S(2)}) collective-permute-start(bf16[768,2048]{1,0:T(8,128)(2,1)} %convolution_convert_fusion.2), channel_id=1, source_target_pairs={{0,1},{1,0},{2,3},{3,2},{4,5},{5,4},{6,7},{7,6},{8,9},{9,8},{10,11... | collective-permute-start | bytes 9437192 | tf_op jit(solution)/shard_map/ppermute | solution.py:31
  811.7 40.1 %collective-permute-start.52 = (bf16[384,2048]{1,0:T(8,128)(2,1)}, bf16[384,2048]{1,0:T(8,128)(2,1)S(1)}, u32[]{:S(2)}, u32[]{:S(2)}) collective-permute-start(bf16[384,2048]{1,0:T(8,128)(2,1)} %get-tuple-element.472), channel_id=1, source_target_pairs={{0,2},{1,3},{2,0},{3,1},{4,6},{5,7},{6,4},{7,5},{8,10},{9,11},{10,... | collective-permute-start | bytes 4718600 | tf_op jit(solution)/shard_map/ppermute | solution.py:31
  813.5 38.4 %collective-permute-start.53 = (bf16[4,256,512]{2,1,0:T(8,128)(2,1)}, bf16[4,256,512]{2,1,0:T(8,128)(2,1)S(1)}, u32[]{:S(2)}, u32[]{:S(2)}) collective-permute-start(bf16[4,256,512]{2,1,0:T(8,128)(2,1)} %get-tuple-element.450), channel_id=1, source_target_pairs={{0,4},{4,0},{8,12},{12,8},{16,20},{20,16},{24,28},{28,24},{1,5},{5... | collective-permute-start | bytes 3145736 | tf_op jit(solution)/shard_map/ppermute | solution.py:31
  814.1 37.8 %collective-permute-start.54 = (bf16[2,256,512]{2,1,0:T(8,128)(2,1)S(1)}, bf16[2,256,512]{2,1,0:T(8,128)(2,1)S(1)}, u32[]{:S(2)}, u32[]{:S(2)}) collective-permute-start(bf16[2,256,512]{2,1,0:T(8,128)(2,1)S(1)} %get-tuple-element.602), channel_id=1, source_target_pairs={{0,8},{4,12},{8,0},{12,4},{16,24},{20,28},{24,16},{28,20},{1,9},{5... | collective-permute-start | bytes 1572872 | tf_op jit(solution)/shard_map/ppermute | solution.py:31
  852.6 38.7 %collective-permute-start.56 = (bf16[384,2048]{1,0:T(8,128)(2,1)}, bf16[384,2048]{1,0:T(8,128)(2,1)}, u32[]{:S(2)}, u32[]{:S(2)}) collective-permute-start(bf16[384,2048]{1,0:T(8,128)(2,1)} %get-tuple-element.480), channel_id=1, source_target_pairs={{0,2},{1,3},{2,0},{3,1},{4,6},{5,7},{6,4},{7,5},{8,10},{9,11},{10,... | collective-permute-start | bytes 4718600 | tf_op jit(solution)/shard_map/ppermute | solution.py:31
  (164 other events, 2281.3 us)
Sparse Core Ops, SparseCore 0:
  124.5 168.2 all-gather.2
  337.1 94.0 all-gather.4
  484.0 111.2 reduce-scatter.3
  598.8 109.7 reduce-scatter.5
  712.1 138.4 reduce-scatter.7

commit v4 on v3

--- a/solution.py
+++ b/solution.py
@@ -195,8 +195,30 @@
         out[:, up_at] = (d * act[:, at].astype(F32)).astype(BF)
 
 
-def pre_kernel(x, w, out):
-    out[...] = jnp.dot(x[...], w[...], preferred_element_type=F32)
+def d_gated_kernel(x, w, out):
+    out[...] = jnp.dot(x[...], w[...], preferred_element_type=F32).astype(BF)
+
+
+def pre_kernel(x, w, rate, act_in, act_gate, slope_in, slope_gate):
+    channels = rate.shape[1]
+
+    def silu(v):
+        s = sigmoid(v)
+        a = v * s
+        return a, s + a * (1.0 - s)
+
+    def product(k):
+        return jnp.dot(
+            x[...], w[:, k * channels : (k + 1) * channels], preferred_element_type=F32
+        )
+
+    act, slope = silu(product(0))
+    act_in[...] = act
+    slope_in[...] = slope.astype(BF)
+    rate[...] = LOWER_BOUND + (1.0 - LOWER_BOUND) * sigmoid(product(1))
+    act, slope = silu(product(2))
+    act_gate[...] = act.astype(BF)
+    slope_gate[...] = slope.astype(BF)
 
 
 def row_tiles(kernel, parts, weight, others, outs, flops, name):
@@ -395,11 +417,10 @@
     return jnp.where(start, 0.0, 1.0).astype(F32)
 
 
-def forward_kernel(order, offsets, pre, before, *rest):
+def forward_kernel(order, offsets, free, act_in, act_gate, before, *rest):
     gated, carry = rest[:-1], rest[-1]
     block = pl.program_id(0)
-    rows = pre.shape[1]
-    channels = before.shape[2]
+    rows, channels = free.shape[1:]
     piece = rows // len(gated)
 
     @pl.when(block == 0)
@@ -415,15 +436,12 @@
         for c in range(channels // LANES):
             lanes = pl.ds(c * LANES, LANES)
             state = carry[:, lanes]
+            gates = act_gate[0, pl.ds(base, 2 * SUB), lanes].astype(F32)
             outs = []
             for g in range(2):
                 here = pl.ds(base + g * SUB, SUB)
-                vin, vforget, vgate = (
-                    pre[0, here, pl.ds(k * channels + c * LANES, LANES)] for k in range(3)
-                )
-                rate = keeps[g] * (LOWER_BOUND + (1.0 - LOWER_BOUND) * sigmoid(vforget))
-                drive = (1.0 - rate) * (vin * sigmoid(vin))
-                a, b = rate, drive
+                rate = keeps[g] * free[0, here, lanes]
+                a, b = rate, (1.0 - rate) * act_in[0, here, lanes]
                 for s in (1, 2, 4):
                     inside = row_id >= s
                     a_up = jnp.where(inside, pltpu.roll(a, s, 0), 1.0)
@@ -435,7 +453,7 @@
                 last_a = jnp.broadcast_to(a[SUB - 1 : SUB], (SUB, LANES))
                 last_b = jnp.broadcast_to(b[SUB - 1 : SUB], (SUB, LANES))
                 state = last_b + last_a * state
-                outs.append(whole * (vgate * sigmoid(vgate)))
+                outs.append(whole * gates[g * SUB : (g + 1) * SUB])
             carry[:, lanes] = state
             gated[p][0, pl.ds(local, 2 * SUB), lanes] = jnp.concatenate(outs, axis=0).astype(BF)
         return 0
@@ -444,13 +462,14 @@
         lax.fori_loop(0, piece // (2 * SUB), functools.partial(step, p=p), 0)
 
 
-def backward_kernel(order, offsets, pre, before, *rest):
+def backward_kernel(
+    order, offsets, free, act_in, act_gate, slope_in, slope_gate, before, *rest
+):
     pieces = (len(rest) - 1) // 2
     dgated, dpieces, carry = rest[:pieces], rest[pieces : 2 * pieces], rest[-1]
     step_id = pl.program_id(0)
     block = pl.num_programs(0) - 1 - step_id
-    rows = pre.shape[1]
-    channels = before.shape[2]
+    rows, channels = free.shape[1:]
     piece = rows // pieces
     groups = piece // (2 * SUB)
 
@@ -466,23 +485,27 @@
         keeps = [keep_of(block * rows + base + g * SUB, offsets) for g in range(2)]
         for c in range(channels // LANES):
             lanes = pl.ds(c * LANES, LANES)
+            both = pl.ds(base, 2 * SUB)
             flow = carry[:, lanes]
+            halves = [
+                v.astype(F32)
+                for v in (
+                    act_gate[0, both, lanes],
+                    slope_in[0, both, lanes],
+                    slope_gate[0, both, lanes],
+                    dgated[p][0, pl.ds(local, 2 * SUB), lanes],
+                )
+            ]
             outs = [None, None]
             for g in (1, 0):
                 here = pl.ds(base + g * SUB, SUB)
-                vin, vforget, vgate = (
-                    pre[0, here, pl.ds(k * channels + c * LANES, LANES)] for k in range(3)
-                )
-                keep, prev = keeps[g], before[0, here, lanes]
-                dg = dgated[p][0, pl.ds(local + g * SUB, SUB), lanes]
-                s_forget = sigmoid(vforget)
-                rate = keep * (LOWER_BOUND + (1.0 - LOWER_BOUND) * s_forget)
-                s_in = sigmoid(vin)
-                act_in = vin * s_in
+                gate, in_slope, gate_slope, dg = [v[g * SUB : (g + 1) * SUB] for v in halves]
+                open_rate, act, prev = free[0, here, lanes], act_in[0, here, lanes], before[0, here, lanes]
+                keep = keeps[g]
+                rate = keep * open_rate
                 rest_in = 1.0 - rate
-                state = rate * prev + rest_in * act_in
-                s_gate = sigmoid(vgate)
-                x = dg * (vgate * s_gate)
+                state = rate * prev + rest_in * act
+                x = dg * gate
                 a, b = rate, rate * x
                 for s in (1, 2, 4):
                     inside = row_id < SUB - s
@@ -495,14 +518,14 @@
                 first_a = jnp.broadcast_to(a[0:1], (SUB, LANES))
                 first_b = jnp.broadcast_to(b[0:1], (SUB, LANES))
                 flow = first_b + first_a * flow
-                d_in = carried * rest_in * (s_in * (1.0 + vin * (1.0 - s_in)))
+                d_in = carried * rest_in * in_slope
                 d_forget = (
                     carried
-                    * (prev - act_in)
+                    * (prev - act)
                     * keep
-                    * ((1.0 - LOWER_BOUND) * s_forget * (1.0 - s_forget))
+                    * ((open_rate - LOWER_BOUND) * (1.0 - open_rate) * (1.0 / (1.0 - LOWER_BOUND)))
                 )
-                d_gate = dg * state * (s_gate * (1.0 + vgate * (1.0 - s_gate)))
+                d_gate = dg * state * gate_slope
                 outs[g] = (d_in, d_forget, d_gate)
             carry[:, lanes] = flow
             for k in range(3):
@@ -583,7 +606,7 @@
 
 
 def new_weights(steps, weights, updates):
-    tiles = weights[3].shape[0] // 176
+    tiles = weights[3].shape[0] // 352
     counts = [v.shape[0] if v.ndim == 3 else 0 for v in weights]
 
     def kernel(factor, *refs):
@@ -753,28 +776,28 @@
     for j, block in zip(late, last):
         w_mix_in = lax.dynamic_update_slice(w_mix_in, block, ((dp_id ^ j ^ 1) * depth, 0))
     whole_one = [v for pair in zip(far_a + near_a, far_b + near_b) for v in pair]
-    (pre,) = run(
+    tall = n_tensor * rows
+    pre = run(
         lambda w, *parts: row_tiles(
             pre_kernel,
             parts,
             w,
             [],
-            [jax.ShapeDtypeStruct((n_tensor * rows, 3 * channels), F32)],
-            2 * n_tensor * rows * width * 3 * channels,
+            [jax.ShapeDtypeStruct((tall, channels), t) for t in (F32, F32, BF, BF, BF)],
+            2 * tall * width * 3 * channels,
             "pre",
         ),
         w_mix_in,
         *whole_one,
     )
-    q.close(pre=pre.reshape(n_tensor, rows, 3 * channels), cot0=cot_far, cot_own1=cot_own[1])
-
-    cot_far = far_rows(q.cot_own1)
+    q.close(pre=[v.reshape(n_tensor, rows, channels) for v in pre], cot0=cot_far)
+
     cot0_near = to_core([cot_own[0]] + q.cot0)
     scanned = recurrence_call(
         forward_kernel,
         order,
         offsets,
-        [q.pre],
+        q.pre[:3],
         [jax.ShapeDtypeStruct((n_tensor, rows, channels), F32)]
         + [jax.ShapeDtypeStruct((n_tensor, piece, channels), BF)] * CHUNKS,
         channels,
@@ -798,13 +821,11 @@
 
     (near1,) = to_core([q.up1])
     far0, kept0 = lower(q.gated[0], q.w_mo, q.near0)
-    q.close(far0=far0, kept0=kept0, near1=near1, cot1=cot_far)
+    q.close(far0=far0, kept0=kept0, near1=near1)
 
     coming0 = to_far(q.far0)
-    cot1_near = to_core([cot_own[1]] + q.cot1)
     far1, kept1 = lower(q.gated[1], q.w_mo, q.near1)
-    q.close(far1=far1, kept1=kept1, coming0=coming0, cot1_near=cot1_near)
-    cot_parts.append([cot_own[1]] + q.cot1 + q.cot1_near)
+    q.close(far1=far1, kept1=kept1, coming0=coming0)
 
     coming1 = to_far(q.far1)
 
@@ -814,15 +835,17 @@
         return (unit_rows * gains[1]).astype(BF), middle, scaling
 
     normed0, middle0, scale0 = run(middle_of, *landed(q.kept0, q.coming0), tokens[cut(0)])
-    q.close(coming1=coming1, normed0=normed0, middle0=middle0, scale0=scale0, w_ffn_in=w_ffn_in)
+    q.close(coming1=coming1, normed0=normed0, middle0=middle0, scale0=scale0)
+    normed_far = far_rows(q.normed0)
+    normed_near = to_core([q.normed0])
+    normed1, middle1, scale1 = run(middle_of, *landed(q.kept1, q.coming1), tokens[cut(1)])
+    weight_sq = run(lambda *ws: jnp.stack([jnp.sum(w * w) for w in ws]), *weights)
+    q.close(w_ffn_in=w_ffn_in, weight_sq=weight_sq)
     w_ffn_out = lax.all_gather(
         after(padded(ffn_out.astype(BF).T), q.w_ffn_in), "dp", axis=0, tiled=True
     )
-    normed_far = far_rows(q.normed0)
-    normed1, middle1, scale1 = run(middle_of, *landed(q.kept1, q.coming1), tokens[cut(1)])
-    weight_sq = run(lambda *ws: jnp.stack([jnp.sum(w * w) for w in ws]), *weights)
     q.close(
-        normed1=normed1, middle1=middle1, scale1=scale1, normed0_far=normed_far, weight_sq=weight_sq
+        normed1=normed1, middle1=middle1, scale1=scale1, normed0_far=normed_far, normed0_near=normed_near
     )
     weight_sq = q.weight_sq
     middle, scale_two = [q.middle0, q.middle1], [q.scale0, q.scale1]
@@ -841,15 +864,18 @@
         )
 
     normed_far = far_rows(q.normed1)
-    normed0 = [q.normed0] + q.normed0_far
-    whole_two = normed0 + to_core(normed0)
+    normed_near = to_core([q.normed1])
+    whole_two = [q.normed0] + q.normed0_far + q.normed0_near + to_core(q.normed0_far)
     out0 = gate_up(whole_two)
-    q.close(out0=out0, normed1_far=normed_far)
-    normed1 = [q.normed1] + q.normed1_far
-    parts1 = normed1 + to_core(normed1)
+    q.close(out0=out0, normed1_far=normed_far, normed1_near=normed_near, cot_own1=cot_own[1])
+    cot_far = far_rows(q.cot_own1)
+    parts1 = [q.normed1] + q.normed1_far + q.normed1_near + to_core(q.normed1_far)
     out1 = gate_up(parts1)
     whole_two = whole_two + parts1
-    hidden = [q.out0[0], out1[0]]
+    q.close(out1=out1, cot1=cot_far)
+    hidden = [q.out0[0], q.out1[0]]
+    cot1 = [q.cot_own1] + q.cot1
+    cot_parts.append(cot1 + to_core(cot1))
 
     def grad(lefts, rights, *settings, **more):
         def call(*values):
@@ -858,9 +884,6 @@
         return run(call, *lefts, *rights)
 
     wide = min(256, depth)
-    grad_fo = grad(hidden, cot_parts[0] + cot_parts[1], "right", wide, "grad_out")
-    q.close(grad_fo=grad_fo, out1=out1)
-    hidden = [q.out0[0], q.out1[0]]
 
     def gate_up_back(i):
         out = (q.out0, q.out1)[i]
@@ -881,10 +904,13 @@
         )
         return d
 
+    grad_fo = grad(hidden, cot_parts[0] + cot_parts[1], "right", wide, "grad_out")
+    q.close(grad_fo=grad_fo)
+
+    sum_fo = lax.psum_scatter(q.grad_fo, "dp", scatter_dimension=1, tiled=True)
     d0 = gate_up_back(0)
-    q.close(up0=upper(d0, q.w_ffn_in), d0=d0, grad_fo=q.grad_fo)
-
-    sum_fo = lax.psum_scatter(q.grad_fo, "dp", scatter_dimension=1, tiled=True)
+    q.close(up0=upper(d0, q.w_ffn_in), d0=d0)
+
     (near0,) = to_core([q.up0])
     d1 = gate_up_back(1)
     up1 = upper(d1, q.w_ffn_in)
@@ -931,11 +957,11 @@
     def d_gated_of(parts):
         (d,) = run(
             lambda w, *parts: row_tiles(
-                pre_kernel,
+                d_gated_kernel,
                 parts,
                 w,
                 [],
-                [jax.ShapeDtypeStruct((many, channels), F32)],
+                [jax.ShapeDtypeStruct((many, channels), BF)],
                 2 * many * width * channels,
                 "d_gated",
             ),
@@ -960,20 +986,21 @@
         down_kept=[down_kept0, down_kept1],
     )
 
-    down_coming0 = to_far(q.down_far[0])
+    down_coming = [to_far(q.down_far[0]), to_far(q.down_far[1])]
+
     whole_d1 = [q.back1[0]] + q.low1_far + q.low1_near + to_core(q.low1_far)
     d_gated1 = d_gated_of(whole_d1)
     scanned = recurrence_call(
         backward_kernel,
         order[::-1],
         offsets,
-        [q.pre, q.before, q.d_gated0, d_gated1],
+        q.pre + [q.before, q.d_gated0, d_gated1],
         [jax.ShapeDtypeStruct((n_tensor, piece, 3 * channels), BF)] * CHUNKS,
         channels,
         "recurrence_backward",
     )
     q.last = scanned[-1]
-    q.close(scanned=scanned, whole_d1=whole_d1, down_coming0=down_coming0, sum_fg=sum_fg)
+    q.close(scanned=scanned, whole_d1=whole_d1, sum_fg=sum_fg, grad_fu=q.grad_fu)
     d_pieces = [v.reshape(-1, 3 * channels) for v in q.scanned]
     whole_one = far_a + near_a + far_b + near_b
 
@@ -996,39 +1023,52 @@
         return kept, coming
 
     sum_fu = sum_in(q.grad_fu)
-    down_coming1 = to_far(q.down_far[1])
     grad0 = grad_mix_in(0)
     q.close(grad0=grad0)
 
     y0 = over_y(q.grad0)
     up0 = upper(d_pieces[0], w_mix_in)
     grad1 = grad_mix_in(1)
-    q.close(grad1=grad1, up0=up0, y0=y0, down_coming1=down_coming1)
+    up1 = upper(d_pieces[1], w_mix_in)
+    q.close(grad1=grad1, up0=up0, up1=up1, y0=y0, down_coming=down_coming)
 
     half0 = add_halves(q.grad0[1], q.y0)
     y1 = over_y(q.grad1)
     z0 = over_z(half0, 2)
-    (near0,) = to_core([q.up0])
-    up1 = upper(d_pieces[1], w_mix_in)
+    near0, near1 = to_core([q.up0, q.up1])
     grad2 = grad_mix_in(2)
-    q.close(grad2=grad2, up1=up1, y1=y1, z0=z0, kept_y0=half0[1], near0=near0)
+    far0, kept0 = lower(d_pieces[0], w_mix_in, near0)
+    q.close(
+        grad2=grad2,
+        near1=near1,
+        y1=y1,
+        z0=z0,
+        kept_y0=half0[1],
+        far0=far0,
+        kept0=kept0,
+    )
 
     y2 = over_y(q.grad2)
     half1 = add_halves(q.grad1[1], q.y1)
     z1 = over_z(half1, 2)
     half0 = add_halves(q.kept_y0, q.z0)
     w0 = over_z(half0, 4)
-    (near1,) = to_core([q.up1])
-    far0, kept0 = lower(d_pieces[0], w_mix_in, q.near0)
-    q.close(far0=far0, kept0=kept0, kept_y1=half1[1], kept_z0=half0[1])
-
     coming0 = to_far(q.far0)
     grad3 = grad(
         q.gated, q.whole_d0 + q.whole_d1, "right", depth, "grad_mix_out", owner=owner
     )
-    far1, kept1 = lower(d_pieces[1], w_mix_in, near1)
+    far1, kept1 = lower(d_pieces[1], w_mix_in, q.near1)
     q.close(
-        far1=far1, kept1=kept1, coming0=coming0, grad3=grad3, y2=y2, z1=z1, w0=w0
+        far1=far1,
+        kept1=kept1,
+        sum_fu=sum_fu,
+        coming0=coming0,
+        grad3=grad3,
+        y2=y2,
+        z1=z1,
+        w0=w0,
+        kept_y1=half1[1],
+        kept_z0=half0[1],
     )
 
     firsts = [mix_in_m[0], mix_in_m[1], mix_in_m[2], mix_out_m, ffn_in_m[0], ffn_in_m[1], ffn_out_m]
@@ -1087,7 +1127,7 @@
             for pair in zip(
                 *[
                     landed(k, c)
-                    for k, c in zip(q.down_kept, [q.down_coming0, q.down_coming1])
+                    for k, c in zip(q.down_kept, q.down_coming)
                 ]
             )
             for v in pair
@@ -1100,7 +1140,6 @@
         kept_y2=half2[1],
         w1=w1,
         kept_z1=half1[1],
-        sum_fu=sum_fu,
     )
 
     half3 = add_halves(q.grad3[1], q.y3)
@@ -1122,14 +1161,26 @@
     lamb(4, q.sum_fg)
     lamb(5, q.sum_fu)
     lamb(2, q.kept_z2, q.w2)
-    lamb(3, half3[1], w3)
+    squares = [weight_sq[i] for i in range(7)] + [m[3] if m else jnp.zeros((), F32) for m in moments]
+    packed = run(
+        lambda one, *others: jnp.stack(
+            [one + others[0], others[1] + others[2], jnp.pad(jnp.stack(others[3:]), (0, width - 14))]
+        ),
+        gain_one0,
+        gain_one1,
+        q.back0[2],
+        q.back1[2],
+        *squares,
+    )
+    q.close(packed=packed, w3=w3, kept_z3=half3[1])
+    lamb(3, q.kept_z3, q.w3)
     input_grad = jnp.concatenate([input_grad0, input_grad1], axis=0)
-    gain_grads = jnp.stack([gain_one0 + gain_one1, q.back0[2] + q.back1[2]])
-    squares = jnp.concatenate([weight_sq, jnp.stack([m[3] for m in moments])])
-    packed = jnp.concatenate([gain_grads.reshape(-1), jnp.pad(squares, (0, SUB * LANES - 14))])
-    packed = total_over_mesh(packed.reshape(-1, LANES), n_dp, n_tensor).reshape(-1)
-    gain_grads = packed[: 2 * width].reshape(2, width)
-    squares = packed[2 * width : 2 * width + 14].reshape(2, 7)
+    place = lax.broadcasted_iota(jnp.int32, (3, width), 1)
+    last_row = lax.broadcasted_iota(jnp.int32, (3, width), 0) == 2
+    packed = q.packed + jnp.where(last_row & (place == 10), moments[3][3], 0.0)
+    packed = total_over_mesh(packed, n_dp, n_tensor)
+    gain_grads = packed[:2]
+    squares = packed[2, :14].reshape(2, 7)
     gn_first, gn_second, gn_update = adam_moments(gain_grads, gains, gains_m, gains_v, 0.0)
     weight_sq = jnp.concatenate([squares[0], jnp.sum(gains * gains, axis=1)])
     update_sq = jnp.concatenate([squares[1], jnp.sum(gn_update * gn_update, axis=1)])

time: 975 us -> 942 us (0.966)
  waiting for transfers between devices: 255 us -> 222 us
  other arithmetic: 91.4 us -> 80.5 us
  local copies, waits for them, and re-layouts: 53.2 us -> 63.8 us
  starting transfers between devices: 58.4 us -> 68.6 us
  Pallas kernels: 425 us -> 415 us
    ppermute x70, waiting for transfers between devices: 249 us -> 215 us  [exchange(): return lax.ppermute(value, axis, [(i, i ^ offset) for i in range(size)])]
    ppermute x70, starting transfers between devices: 58.2 us -> 68.4 us  [exchange(): return lax.ppermute(value, axis, [(i, i ^ offset) for i in range(size)])]
    unnamed x245 -> x224, local copies, waits for them, and re-layouts: 19.3 us -> 20.5 us
  transfers between devices with their start and end apart: 75 -> 75, of which waited for: 35 -> 38; matrix products, arithmetic and copies ran while one was open for 17% -> 19% of each run, Pallas kernels for 41% -> 43%
where the time goes in v4:
time: 942 us; the launch traced here: 935 us
  Pallas kernels  415 us (44%)
  waiting for transfers between devices  222 us (24%)
  other arithmetic  80.5 us (9%)
  matrix products  70.1 us (7%)
  starting transfers between devices  68.6 us (7%)
  local copies, waits for them, and re-layouts  63.8 us (7%)
  between operations  15.3 us (2%)
    ppermute x70, waiting for transfers between devices, exchange(): return lax.ppermute(value, axis, [(i, i ^ offset) for i in range(size)])  215 us
    pallas_call x7, Pallas kernels, row_tiles(): pl.pallas_call(body, grid=(count,), in_specs=[pl.BlockSpec(memory_space=p...  143 us
    pallas_call x3, Pallas kernels, grad_kernel(): pl.pallas_call(kernel, grid=(steps,), in_specs=in_specs, out_specs=pl.Blo...  79.9 us
    dot_general x8, matrix products, mm_nt(): lax.dot_general(a, b, (((1,), (1,)), ((), ())), preferred_element_type=F32)  70.1 us
    ppermute x70, starting transfers between devices, exchange(): return lax.ppermute(value, axis, [(i, i ^ offset) for i in range(size)])  68.4 us
    pallas_call x6, Pallas kernels, near_added(): pl.pallas_call(by_rows, grid=(2,), in_specs=[rowed(operand), pl.BlockSpec...  59.9 us
    pallas_call x4, Pallas kernels, grad_kernel(): pl.pallas_call(kernel_by_place, grid_spec=pltpu.PrefetchScalarGridSpec(nu...  58.9 us
    pallas_call x2, Pallas kernels, recurrence_call(): pl.pallas_call(kernel, grid_spec=pltpu.PrefetchScalarGridSpec(num_scalar_...  33.3 us
  transfers between devices with their start and end apart: 75, of which 38 were waited for; matrix products, arithmetic and copies ran while one was open for 19% of the time, Pallas kernels for 43%

profile of v4, /device:TPU:0, one launch (start us, length us, event | category | flops | bytes accessed | tf_op | source)
XLA Modules:
  0.0 935.3 jit_solution(15018951324674795696)
XLA Ops:
  21.0 13.4 %collective-permute-done.1 = bf16[256,1536]{1,0:T(8,128)(2,1)S(1)} collective-permute-done((bf16[256,1536]{1,0:T(8,128)(2,1)S(1)}, bf16[256,1536]{1,0:T(8,128)(2,1)S(1)}, u32[]{:S(2)}, u32[]{:S(2)}) %collective-permute-start.1) | collective-permute-done | bytes 786464 | tf_op jit(solution)/shard_map/ppermute | solution.py:31
  36.5 18.1 %collective-permute-done.3 = bf16[256,1536]{1,0:T(8,128)(2,1)S(1)} collective-permute-done((bf16[256,1536]{1,0:T(8,128)(2,1)S(1)}, bf16[256,1536]{1,0:T(8,128)(2,1)S(1)}, u32[]{:S(2)}, u32[]{:S(2)}) %collective-permute-start.3) | collective-permute-done | bytes 786464 | tf_op jit(solution)/shard_map/ppermute | solution.py:31
  65.4 15.5 %collective-permute-done.5 = bf16[256,1536]{1,0:T(8,128)(2,1)} collective-permute-done((bf16[256,1536]{1,0:T(8,128)(2,1)}, bf16[256,1536]{1,0:T(8,128)(2,1)}, u32[]{:S(2)}, u32[]{:S(2)}) %collective-permute-start.5) | collective-permute-done | bytes 786464 | tf_op jit(solution)/shard_map/ppermute | solution.py:31
  81.0 16.3 %collective-permute-done.6 = bf16[256,1536]{1,0:T(8,128)(2,1)} collective-permute-done((bf16[256,1536]{1,0:T(8,128)(2,1)}, bf16[256,1536]{1,0:T(8,128)(2,1)}, u32[]{:S(2)}, u32[]{:S(2)}) %collective-permute-start.6) | collective-permute-done | bytes 786464 | tf_op jit(solution)/shard_map/ppermute | solution.py:31
  133.8 29.8 %pre.1 = (f32[3072,512]{1,0:T(8,128)}, f32[3072,512]{1,0:T(8,128)}, bf16[3072,512]{1,0:T(8,128)(2,1)}, bf16[3072,512]{1,0:T(8,128)(2,1)}, bf16[3072,512]{1,0:T(8,128)(2,1)}) custom-call(bf16[384,2048]{1,0:T(8,128)(2,1)} %copy-done.54, bf16[384,2048]{1,0:T(8,128)(2,1)} %get-tuple-element.300.refs_1_.refs_4_, bf16[384,2048]{1,0:T(8,128)(2,1)} %copy-done.98, ...), custom_call_target="tpu_custom_call" | custom-call | flops 34923765760 | bytes 12582912 | tf_op jit(solution)/shard_map/pre/pallas_call | solution.py:253
  163.7 13.6 %recurrence_forward.1 = (f32[4,768,512]{2,1,0:T(8,128)}, bf16[4,384,512]{2,1,0:T(8,128)(2,1)S(1)}, bf16[4,384,512]{2,1,0:T(8,128)(2,1)S(1)}) custom-call(s32[4]{0:T(128)S(1)} %gather_fusion, s32[4]{0:T(128)S(1)} %bitcast_subtract_fusion.offsets, f32[4,768,512]{2,1,0:T(8,128)} %bitcast.213, f32[4,768,512]{2,1,0:T(8,128)} %bitcast.215, ...), custom_call_target="tpu_custom_call" | custom-call | flops 23592960000 | bytes 37748736 | tf_op jit(solution)/shard_map/recurrence_forward/pallas_call | solution.py:547
  212.2 28.4 %collective-permute-done.22 = bf16[384,2048]{1,0:T(8,128)(2,1)S(1)} collective-permute-done((bf16[384,2048]{1,0:T(8,128)(2,1)}, bf16[384,2048]{1,0:T(8,128)(2,1)S(1)}, u32[]{:S(2)}, u32[]{:S(2)}) %collective-permute-start.22) | collective-permute-done | bytes 1572896 | tf_op jit(solution)/shard_map/ppermute | solution.py:31
  249.7 26.8 %collective-permute-done.23 = bf16[384,2048]{1,0:T(8,128)(2,1)S(1)} collective-permute-done((bf16[384,2048]{1,0:T(8,128)(2,1)}, bf16[384,2048]{1,0:T(8,128)(2,1)S(1)}, u32[]{:S(2)}, u32[]{:S(2)}) %collective-permute-start.23) | collective-permute-done | bytes 1572896 | tf_op jit(solution)/shard_map/ppermute | solution.py:31
  290.4 21.3 %collective-permute-done.24.refs_1_ = bf16[384,2048]{1,0:T(8,128)(2,1)} collective-permute-done((bf16[384,2048]{1,0:T(8,128)(2,1)}, bf16[384,2048]{1,0:T(8,128)(2,1)}, u32[]{:S(2)}, u32[]{:S(2)}) %collective-permute-start.24) | collective-permute-done | bytes 1572896 | tf_op jit(solution)/shard_map/ppermute | solution.py:31
  315.4 29.9 %gate_up.2 = (bf16[1536,1408]{1,0:T(8,128)(2,1)}, bf16[1536,1408]{1,0:T(8,128)(2,1)}, bf16[1536,1408]{1,0:T(8,128)(2,1)}) custom-call(bf16[384,2048]{1,0:T(8,128)(2,1)} %multiply_convert_fusion.1.refs_0_, bf16[384,2048]{1,0:T(8,128)(2,1)} %collective-permute-done.24.refs_1_, bf16[384,2048]{1,0:T(8,128)(2,1)} %collective-permute-done.25.refs_2_, ...), custom_call_target="tpu_custom_call" | custom-call | flops 32346783744 | bytes 23068672 | tf_op jit(solution)/shard_map/gate_up/pallas_call | solution.py:253
  354.5 30.5 %gate_up.3 = (bf16[1536,1408]{1,0:T(8,128)(2,1)}, bf16[1536,1408]{1,0:T(8,128)(2,1)}, bf16[1536,1408]{1,0:T(8,128)(2,1)}) custom-call(bf16[384,2048]{1,0:T(8,128)(2,1)} %copy-done.56, bf16[384,2048]{1,0:T(8,128)(2,1)} %collective-permute-done.27.refs_1_.refs_5_, bf16[384,2048]{1,0:T(8,128)(2,1)} %collective-permute-done.28.refs_2_.refs_6_, ...), custom_call_target="tpu_custom_call" | custom-call | flops 32346783744 | bytes 23068672 | tf_op jit(solution)/shard_map/gate_up/pallas_call | solution.py:253
  391.1 25.6 %grad_out.1 = bf16[1408,2048]{1,0:T(8,128)(2,1)} custom-call(bf16[384,2048]{1,0:T(8,128)(2,1)} %get-tuple-element.603.refs_0_, bf16[384,2048]{1,0:T(8,128)(2,1)} %collective-permute-done.16.refs_1_, bf16[384,2048]{1,0:T(8,128)(2,1)} %collective-permute-done.18.refs_2_, bf16[384,2048]{1,0:T(8,128)(2,1)} %copy-done.100, ...), custom_call_target="tpu_custom_call" | custom-call | flops 32346783744 | bytes 5767168 | tf_op jit(solution)/shard_map/grad_out/pallas_call | solution.py:371
  416.9 17.5 %gate_up_back.2.v.refs_8_ = bf16[1536,2816]{1,0:T(8,128)(2,1)} custom-call(bf16[384,2048]{1,0:T(8,128)(2,1)} %get-tuple-element.603.refs_0_, bf16[384,2048]{1,0:T(8,128)(2,1)} %collective-permute-done.16.refs_1_, bf16[384,2048]{1,0:T(8,128)(2,1)} %collective-permute-done.18.refs_2_, bf16[384,2048]{1,0:T(8,128)(2,1)} %copy-done.100, ...), custom_call_target="tpu_custom_call" | custom-call | flops 18173392896 | bytes 11534336 | tf_op jit(solution)/shard_map/gate_up_back/pallas_call | solution.py:253
  434.4 13.3 %fusion.10 = bf16[768,2048]{1,0:T(8,128)(2,1)S(1)} fusion(bf16[2048,2816]{1,0:T(8,128)(2,1)} %all-gather.3.cloned.1.call-done.refs_4_.w, bf16[1536,2816]{1,0:T(8,128)(2,1)} %gate_up_back.2.v.refs_8_), kind=kOutput, calls=%fused_computation.22 | convolution fusion | flops 8859942912 | bytes 19005440 | tf_op jit(solution)/shard_map/dot_general | solution.py:43
  448.0 17.6 %gate_up_back.3.v.refs_9_ = bf16[1536,2816]{1,0:T(8,128)(2,1)} custom-call(bf16[384,2048]{1,0:T(8,128)(2,1)} %get-tuple-element.378.refs_4_.refs_0_, bf16[384,2048]{1,0:T(8,128)(2,1)} %copy-done.105, bf16[384,2048]{1,0:T(8,128)(2,1)} %copy-done.106, bf16[384,2048]{1,0:T(8,128)(2,1)} %copy-done.107, ...), custom_call_target="tpu_custom_call" | custom-call | flops 18173392896 | bytes 11534336 | tf_op jit(solution)/shard_map/gate_up_back/pallas_call | solution.py:253
  465.6 14.6 %fusion.13 = bf16[768,2048]{1,0:T(8,128)(2,1)} fusion(bf16[2048,2816]{1,0:T(8,128)(2,1)} %all-gather.3.cloned.1.call-done.refs_4_.w, bf16[1536,2816]{1,0:T(8,128)(2,1)} %gate_up_back.3.v.refs_9_), kind=kOutput, calls=%fused_computation.23 | convolution fusion | flops 8859942912 | bytes 19005440 | tf_op jit(solution)/shard_map/dot_general | solution.py:43
  481.9 15.6 %near_added.10 = (bf16[384,2048]{1,0:T(8,128)(2,1)}, f32[384,2048]{1,0:T(8,128)}) custom-call(bf16[1536,2816]{1,0:T(8,128)(2,1)} %gate_up_back.2.v.refs_8_, bf16[2048,2816]{1,0:T(8,128)(2,1)} %all-gather.3.cloned.1.call-done.refs_4_.w, bf16[768,2048]{1,0:T(8,128)(2,1)} %copy-done.96), custom_call_target="tpu_custom_call" | custom-call | flops 18173392896 | bytes 11534336 | tf_op jit(solution)/shard_map/near_added/pallas_call | solution.py:129
  508.5 9.4 %convolution_convert_fusion.4 = bf16[768,2048]{1,0:T(8,128)(2,1)} fusion(bf16[2048,1408]{1,0:T(8,128)(2,1)} %all-gather.5.cloned.1.call-done.refs_4_.w, bf16[1536,1408]{1,0:T(8,128)(2,1)} %get-tuple-element.435.refs_9_.v), kind=kOutput, calls=%fused_computation.26 | convolution fusion | flops 4430757888 | bytes 11075584 | tf_op jit(solution)/shard_map/dot_general | solution.py:43
  517.9 15.6 %near_added.11 = (bf16[384,2048]{1,0:T(8,128)(2,1)}, f32[384,2048]{1,0:T(8,128)}) custom-call(bf16[1536,2816]{1,0:T(8,128)(2,1)} %gate_up_back.3.v.refs_9_, bf16[2048,2816]{1,0:T(8,128)(2,1)} %all-gather.3.cloned.1.call-done.refs_4_.w, bf16[768,2048]{1,0:T(8,128)(2,1)} %collective-permute-done.34.added), custom_call_target="tpu_custom_call" | custom-call | flops 18173392896 | bytes 11534336 | tf_op jit(solution)/shard_map/near_added/pallas_call | solution.py:129
  541.6 27.0 %grad_in.2 = bf16[2048,1408]{1,0:T(8,128)(2,1)} custom-call(bf16[384,2048]{1,0:T(8,128)(2,1)} %multiply_convert_fusion.1.refs_0_, bf16[384,2048]{1,0:T(8,128)(2,1)} %collective-permute-done.24.refs_1_, bf16[384,2048]{1,0:T(8,128)(2,1)} %collective-permute-done.25.refs_2_, bf16[384,2048]{1,0:T(8,128)(2,1)} %collective-permute-done.26.refs_3_, ...), custom_call_target="tpu_custom_call" | custom-call | flops 32346783744 | bytes 5767168 | tf_op jit(solution)/shard_map/grad_in/pallas_call | solution.py:371
  581.4 27.2 %grad_in.3 = bf16[2048,1408]{1,0:T(8,128)(2,1)} custom-call(bf16[384,2048]{1,0:T(8,128)(2,1)} %multiply_convert_fusion.1.refs_0_, bf16[384,2048]{1,0:T(8,128)(2,1)} %collective-permute-done.24.refs_1_, bf16[384,2048]{1,0:T(8,128)(2,1)} %collective-permute-done.25.refs_2_, bf16[384,2048]{1,0:T(8,128)(2,1)} %collective-permute-done.26.refs_3_, ...), custom_call_target="tpu_custom_call" | custom-call | flops 32346783744 | bytes 5767168 | tf_op jit(solution)/shard_map/grad_in/pallas_call | solution.py:371
  610.7 11.4 %near_added.12 = (bf16[384,2048]{1,0:T(8,128)(2,1)}, f32[384,2048]{1,0:T(8,128)}) custom-call(bf16[1536,1408]{1,0:T(8,128)(2,1)} %get-tuple-element.432.refs_8_.v, bf16[2048,1408]{1,0:T(8,128)(2,1)} %all-gather.5.cloned.1.call-done.refs_4_.w, bf16[768,2048]{1,0:T(8,128)(2,1)} %collective-permute-done.37.n), custom_call_target="tpu_custom_call" | custom-call | flops 11086696448 | bytes 5767168 | tf_op jit(solution)/shard_map/near_added/pallas_call | solution.py:157
  622.1 11.4 %near_added.13 = (bf16[384,2048]{1,0:T(8,128)(2,1)}, f32[384,2048]{1,0:T(8,128)}) custom-call(bf16[1536,1408]{1,0:T(8,128)(2,1)} %get-tuple-element.435.refs_9_.v, bf16[2048,1408]{1,0:T(8,128)(2,1)} %all-gather.5.cloned.1.call-done.refs_4_.w, bf16[768,2048]{1,0:T(8,128)(2,1)} %collective-permute-done.38.n), custom_call_target="tpu_custom_call" | custom-call | flops 11086696448 | bytes 5767168 | tf_op jit(solution)/shard_map/near_added/pallas_call | solution.py:157
  660.6 19.7 %recurrence_backward.1 = (bf16[4,384,1536]{2,1,0:T(8,128)(2,1)}, bf16[4,384,1536]{2,1,0:T(8,128)(2,1)}) custom-call(s32[4]{0:T(128)S(1)} %rev.3.order, s32[4]{0:T(128)S(1)} %copy-done.5, f32[4,768,512]{2,1,0:T(8,128)} %bitcast.214, f32[4,768,512]{2,1,0:T(8,128)} %bitcast.216, bf16[4,768,512]{2,1,0:T(8,128)(2,1)} %bitcast.228, ...), custom_call_target="tpu_custom_call" | custom-call | flops 23592960000 | bytes 37748736 | tf_op jit(solution)/shard_map/recurrence_backward/pallas_call | solution.py:547
  682.8 14.8 %grad_mix_in.3 = (bf16[4,256,512]{2,1,0:T(8,128)(2,1)}, bf16[4,256,512]{2,1,0:T(8,128)(2,1)}) custom-call(s32[8]{0:T(128)} %stack.136.owners_ref, bf16[384,2048]{1,0:T(8,128)(2,1)} %copy-done.54, bf16[384,2048]{1,0:T(8,128)(2,1)} %copy-done.98, bf16[384,2048]{1,0:T(8,128)(2,1)} %copy-done.99, bf16[384,2048]{1,0:T(8,128)(2,1)} %collective-permute-done.10.refs_6_.refs_3_, ...), custom_call_target="tpu_custom_call" | custom-call | flops 14307921920 | bytes 2097152 | tf_op jit(solution)/shard_map/grad_mix_in/pallas_call | solution.py:395
  708.5 14.7 %grad_mix_in.4 = (bf16[4,256,512]{2,1,0:T(8,128)(2,1)}, bf16[4,256,512]{2,1,0:T(8,128)(2,1)}) custom-call(s32[8]{0:T(128)} %stack.136.owners_ref, bf16[384,2048]{1,0:T(8,128)(2,1)} %copy-done.54, bf16[384,2048]{1,0:T(8,128)(2,1)} %copy-done.98, bf16[384,2048]{1,0:T(8,128)(2,1)} %copy-done.99, bf16[384,2048]{1,0:T(8,128)(2,1)} %collective-permute-done.10.refs_6_.refs_3_, ...), custom_call_target="tpu_custom_call" | custom-call | flops 14307921920 | bytes 2097152 | tf_op jit(solution)/shard_map/grad_mix_in/pallas_call | solution.py:395
  723.3 9.4 %convolution_convert_fusion.2 = bf16[768,2048]{1,0:T(8,128)(2,1)} fusion(bf16[2048,1536]{1,0:T(8,128)(2,1)} %constant_dynamic-update-slice_fusion.4.refs_8_.w, bf16[1536,1536]{1,0:T(8,128)(2,1)} %bitcast.219), kind=kOutput, calls=%fused_computation.24 | convolution fusion | flops 4833411072 | bytes 11796480 | tf_op jit(solution)/shard_map/dot_general | solution.py:43
  736.7 14.7 %grad_mix_in.5 = (bf16[4,256,512]{2,1,0:T(8,128)(2,1)}, bf16[4,256,512]{2,1,0:T(8,128)(2,1)}) custom-call(s32[8]{0:T(128)} %stack.136.owners_ref, bf16[384,2048]{1,0:T(8,128)(2,1)} %copy-done.54, bf16[384,2048]{1,0:T(8,128)(2,1)} %copy-done.98, bf16[384,2048]{1,0:T(8,128)(2,1)} %copy-done.99, bf16[384,2048]{1,0:T(8,128)(2,1)} %collective-permute-done.10.refs_6_.refs_3_, ...), custom_call_target="tpu_custom_call" | custom-call | flops 14307921920 | bytes 2097152 | tf_op jit(solution)/shard_map/grad_mix_in/pallas_call | solution.py:395
  754.3 11.6 %near_added.14 = (bf16[384,2048]{1,0:T(8,128)(2,1)}, f32[384,2048]{1,0:T(8,128)}) custom-call(bf16[1536,1536]{1,0:T(8,128)(2,1)} %bitcast.226, bf16[2048,1536]{1,0:T(8,128)(2,1)} %constant_dynamic-update-slice_fusion.4.refs_8_.w, bf16[768,2048]{1,0:T(8,128)(2,1)} %collective-permute-done.51.n), custom_call_target="tpu_custom_call" | custom-call | flops 11730940928 | bytes 6291456 | tf_op jit(solution)/shard_map/near_added/pallas_call | solution.py:157
  784.3 14.8 %grad_mix_out.1 = (bf16[4,512,256]{2,1,0:T(8,128)(2,1)}, bf16[4,512,256]{2,1,0:T(8,128)(2,1)}) custom-call(s32[8]{0:T(128)} %stack.136.owners_ref, bf16[384,2048]{1,0:T(8,128)(2,1)} %get-tuple-element.450.refs_0_, bf16[384,2048]{1,0:T(8,128)(2,1)} %collective-permute-done.39.refs_1_, bf16[384,2048]{1,0:T(8,128)(2,1)} %collective-permute-done.40.refs_2_, ...), custom_call_target="tpu_custom_call" | custom-call | flops 14307921920 | bytes 2097152 | tf_op jit(solution)/shard_map/grad_mix_out/pallas_call | solution.py:395
  799.1 12.0 %near_added.15 = (bf16[384,2048]{1,0:T(8,128)(2,1)}, f32[384,2048]{1,0:T(8,128)}) custom-call(bf16[1536,1536]{1,0:T(8,128)(2,1)} %bitcast.221, bf16[2048,1536]{1,0:T(8,128)(2,1)} %constant_dynamic-update-slice_fusion.4.refs_8_.w, bf16[768,2048]{1,0:T(8,128)(2,1)} %collective-permute-done.48.n), custom_call_target="tpu_custom_call" | custom-call | flops 11730940928 | bytes 6291456 | tf_op jit(solution)/shard_map/near_added/pallas_call | solution.py:157
  842.9 15.3 %collective-permute-done.57 = bf16[4,512,256]{2,1,0:T(8,128)(2,1)S(1)} collective-permute-done((bf16[4,512,256]{2,1,0:T(8,128)(2,1)S(1)}, bf16[4,512,256]{2,1,0:T(8,128)(2,1)S(1)}, u32[]{:S(2)}, u32[]{:S(2)}) %collective-permute-start.57) | collective-permute-done | bytes 1048608 | tf_op jit(solution)/shard_map/ppermute | solution.py:31
  (497 shorter events, 343.2 us)
Async XLA Ops:
  7.2 283.2 %all-gather.3.cloned.1.call-start = ((), (), s32[]{:S(2)}) async-start(), calls=%async_computation.3 | async-start | bytes 12976128 | tf_op jit(solution)/shard_map/all_gather | solution.py:772
  12.4 42.2 %collective-permute-start = (bf16[384,2048]{1,0:T(8,128)(2,1)S(1)}, bf16[384,2048]{1,0:T(8,128)(2,1)S(1)}, u32[]{:S(2)}, u32[]{:S(2)}) collective-permute-start(bf16[384,2048]{1,0:T(8,128)(2,1)S(1)} %get-tuple-element.472.refs_0_), channel_id=1, source_target_pairs={{0,2},{1,3},{2,0},{3,1},{4,6},{5,7},{6,4},{7,5},{8,10},{9,11},{10,... | collective-permute-start | bytes 4718600 | tf_op jit(solution)/shard_map/ppermute | solution.py:31
  18.5 36.1 %collective-permute-start.3 = (bf16[256,1536]{1,0:T(8,128)(2,1)S(1)}, bf16[256,1536]{1,0:T(8,128)(2,1)S(1)}, u32[]{:S(2)}, u32[]{:S(2)}) collective-permute-start(bf16[256,1536]{1,0:T(8,128)(2,1)S(1)} %pad_maximum_fusion.8), channel_id=1, source_target_pairs={{0,24},{4,28},{8,16},{12,20},{16,8},{20,12},{24,0},{28,4},{1,25},{... | collective-permute-start | bytes 2359304 | tf_op jit(solution)/shard_map/ppermute | solution.py:31
  54.7 44.9 %collective-permute-start.4 = (bf16[384,2048]{1,0:T(8,128)(2,1)}, bf16[384,2048]{1,0:T(8,128)(2,1)}, u32[]{:S(2)}, u32[]{:S(2)}) collective-permute-start(bf16[384,2048]{1,0:T(8,128)(2,1)} %get-tuple-element.300.refs_1_.refs_4_), channel_id=1, source_target_pairs={{0,2},{1,3},{2,0},{3,1},{4,6},{5,7},{6,4},{7,5},{8,10},{9,11},{10,... | collective-permute-start | bytes 4718600 | tf_op jit(solution)/shard_map/ppermute | solution.py:31
  59.3 40.3 %collective-permute-start.9 = (bf16[384,2048]{1,0:T(8,128)(2,1)}, bf16[384,2048]{1,0:T(8,128)(2,1)}, u32[]{:S(2)}, u32[]{:S(2)}) collective-permute-start(bf16[384,2048]{1,0:T(8,128)(2,1)} %get-tuple-element.300.refs_1_.refs_4_), channel_id=1, source_target_pairs={{0,1},{1,0},{2,3},{3,2},{4,5},{5,4},{6,7},{7,6},{8,9},{9,8},{10,11... | collective-permute-start | bytes 4718600 | tf_op jit(solution)/shard_map/ppermute | solution.py:31
  60.8 36.5 %collective-permute-start.6 = (bf16[256,1536]{1,0:T(8,128)(2,1)}, bf16[256,1536]{1,0:T(8,128)(2,1)}, u32[]{:S(2)}, u32[]{:S(2)}) collective-permute-start(bf16[256,1536]{1,0:T(8,128)(2,1)} %copy-done.71), channel_id=1, source_target_pairs={{0,4},{4,0},{8,12},{12,8},{16,20},{20,16},{24,28},{28,24},{1,5},{5... | collective-permute-start | bytes 2359304 | tf_op jit(solution)/shard_map/ppermute | solution.py:31
  62.3 37.3 %collective-permute-start.7 = (bf16[256,1536]{1,0:T(8,128)(2,1)}, bf16[256,1536]{1,0:T(8,128)(2,1)}, u32[]{:S(2)}, u32[]{:S(2)}) collective-permute-start(bf16[256,1536]{1,0:T(8,128)(2,1)} %copy-done.36), channel_id=1, source_target_pairs={{0,16},{4,20},{8,24},{12,28},{16,0},{20,4},{24,8},{28,12},{1,17},{... | collective-permute-start | bytes 2359304 | tf_op jit(solution)/shard_map/ppermute | solution.py:31
  123.5 293.3 %all-gather.5.cloned.1.call-start = ((), (), s32[]{:S(2)}) async-start(), calls=%async_computation.4 | async-start | bytes 6488064 | tf_op jit(solution)/shard_map/all_gather | solution.py:844
  129.0 57.5 %collective-permute-start.18 = (bf16[384,2048]{1,0:T(8,128)(2,1)}, bf16[384,2048]{1,0:T(8,128)(2,1)}, u32[]{:S(2)}, u32[]{:S(2)}) collective-permute-start(bf16[384,2048]{1,0:T(8,128)(2,1)} %get-tuple-element.603.refs_0_), channel_id=1, source_target_pairs={{0,1},{1,0},{2,3},{3,2},{4,5},{5,4},{6,7},{7,6},{8,9},{9,8},{10,11... | collective-permute-start | bytes 4718600 | tf_op jit(solution)/shard_map/ppermute | solution.py:31
  133.4 47.4 %collective-permute-start.17 = (bf16[1024,512]{1,0:T(8,128)(2,1)}, bf16[1024,512]{1,0:T(8,128)(2,1)}, u32[]{:S(2)}, u32[]{:S(2)}) collective-permute-start(bf16[1024,512]{1,0:T(8,128)(2,1)} %pad_maximum_fusion.7), channel_id=1, source_target_pairs={{0,4},{4,0},{8,12},{12,8},{16,20},{20,16},{24,28},{28,24},{1,5},{5... | collective-permute-start | bytes 3145736 | tf_op jit(solution)/shard_map/ppermute | solution.py:31
  203.9 36.6 %collective-permute-start.22 = (bf16[384,2048]{1,0:T(8,128)(2,1)}, bf16[384,2048]{1,0:T(8,128)(2,1)S(1)}, u32[]{:S(2)}, u32[]{:S(2)}) collective-permute-start(bf16[384,2048]{1,0:T(8,128)(2,1)} %get-tuple-element.351), channel_id=1, source_target_pairs={{0,2},{1,3},{2,0},{3,1},{4,6},{5,7},{6,4},{7,5},{8,10},{9,11},{10,... | collective-permute-start | bytes 4718600 | tf_op jit(solution)/shard_map/ppermute | solution.py:31
  240.5 35.9 %collective-permute-start.23 = (bf16[384,2048]{1,0:T(8,128)(2,1)}, bf16[384,2048]{1,0:T(8,128)(2,1)S(1)}, u32[]{:S(2)}, u32[]{:S(2)}) collective-permute-start(bf16[384,2048]{1,0:T(8,128)(2,1)} %get-tuple-element.356), channel_id=1, source_target_pairs={{0,2},{1,3},{2,0},{3,1},{4,6},{5,7},{6,4},{7,5},{8,10},{9,11},{10,... | collective-permute-start | bytes 4718600 | tf_op jit(solution)/shard_map/ppermute | solution.py:31
  312.8 36.9 %collective-permute-start.27 = (bf16[384,2048]{1,0:T(8,128)(2,1)S(1)}, bf16[384,2048]{1,0:T(8,128)(2,1)}, u32[]{:S(2)}, u32[]{:S(2)}) collective-permute-start(bf16[384,2048]{1,0:T(8,128)(2,1)S(1)} %multiply_convert_fusion.refs_0_.refs_4_), channel_id=1, source_target_pairs={{0,2},{1,3},{2,0},{3,1},{4,6},{5,7},{6,4},{7,5},{8,10},{9,11},{10,... | collective-permute-start | bytes 4718600 | tf_op jit(solution)/shard_map/ppermute | solution.py:31
  314.2 35.5 %collective-permute-start.28 = (bf16[384,2048]{1,0:T(8,128)(2,1)S(1)}, bf16[384,2048]{1,0:T(8,128)(2,1)}, u32[]{:S(2)}, u32[]{:S(2)}) collective-permute-start(bf16[384,2048]{1,0:T(8,128)(2,1)S(1)} %multiply_convert_fusion.refs_0_.refs_4_), channel_id=1, source_target_pairs={{0,1},{1,0},{2,3},{3,2},{4,5},{5,4},{6,7},{7,6},{8,9},{9,8},{10,11... | collective-permute-start | bytes 4718600 | tf_op jit(solution)/shard_map/ppermute | solution.py:31
  314.5 254.2 %reduce-scatter.4.cloned.1.call-start = ((), (), s32[]{:S(2)}) async-start(), calls=%async_computation.5 | async-start | bytes 6488064 | tf_op jit(solution)/shard_map/reduce_scatter | solution.py:910
  349.7 36.8 %collective-permute-start.30 = (bf16[384,2048]{1,0:T(8,128)(2,1)S(1)}, bf16[384,2048]{1,0:T(8,128)(2,1)S(1)}, u32[]{:S(2)}, u32[]{:S(2)}) collective-permute-start(bf16[384,2048]{1,0:T(8,128)(2,1)S(1)} %copy-done.55), channel_id=1, source_target_pairs={{0,2},{1,3},{2,0},{3,1},{4,6},{5,7},{6,4},{7,5},{8,10},{9,11},{10,... | collective-permute-start | bytes 4718600 | tf_op jit(solution)/shard_map/ppermute | solution.py:31
  351.2 35.3 %collective-permute-start.31 = (bf16[384,2048]{1,0:T(8,128)(2,1)S(1)}, bf16[384,2048]{1,0:T(8,128)(2,1)S(1)}, u32[]{:S(2)}, u32[]{:S(2)}) collective-permute-start(bf16[384,2048]{1,0:T(8,128)(2,1)S(1)} %copy-done.55), channel_id=1, source_target_pairs={{0,1},{1,0},{2,3},{3,2},{4,5},{5,4},{6,7},{7,6},{8,9},{9,8},{10,11... | collective-permute-start | bytes 4718600 | tf_op jit(solution)/shard_map/ppermute | solution.py:31
  416.8 266.0 %reduce-scatter.6.cloned.1.call-start = ((), (), s32[]{:S(2)}) async-start(), calls=%async_computation.6 | async-start | bytes 6488064 | tf_op jit(solution)/shard_map/reduce_scatter | solution.py:937
  497.9 36.7 %collective-permute-start.35 = (bf16[384,2048]{1,0:T(8,128)(2,1)}, bf16[384,2048]{1,0:T(8,128)(2,1)S(1)}, u32[]{:S(2)}, u32[]{:S(2)}) collective-permute-start(bf16[384,2048]{1,0:T(8,128)(2,1)} %get-tuple-element.403), channel_id=1, source_target_pairs={{0,2},{1,3},{2,0},{3,1},{4,6},{5,7},{6,4},{7,5},{8,10},{9,11},{10,... | collective-permute-start | bytes 4718600 | tf_op jit(solution)/shard_map/ppermute | solution.py:31
  534.6 35.9 %collective-permute-start.36 = (bf16[384,2048]{1,0:T(8,128)(2,1)}, bf16[384,2048]{1,0:T(8,128)(2,1)}, u32[]{:S(2)}, u32[]{:S(2)}) collective-permute-start(bf16[384,2048]{1,0:T(8,128)(2,1)} %get-tuple-element.411), channel_id=1, source_target_pairs={{0,2},{1,3},{2,0},{3,1},{4,6},{5,7},{6,4},{7,5},{8,10},{9,11},{10,... | collective-permute-start | bytes 4718600 | tf_op jit(solution)/shard_map/ppermute | solution.py:31
  570.5 38.2 %collective-permute-start.39 = (bf16[384,2048]{1,0:T(8,128)(2,1)}, bf16[384,2048]{1,0:T(8,128)(2,1)}, u32[]{:S(2)}, u32[]{:S(2)}) collective-permute-start(bf16[384,2048]{1,0:T(8,128)(2,1)} %get-tuple-element.450.refs_0_), channel_id=1, source_target_pairs={{0,2},{1,3},{2,0},{3,1},{4,6},{5,7},{6,4},{7,5},{8,10},{9,11},{10,... | collective-permute-start | bytes 4718600 | tf_op jit(solution)/shard_map/ppermute | solution.py:31
  572.0 61.5 %collective-permute-start.40 = (bf16[384,2048]{1,0:T(8,128)(2,1)}, bf16[384,2048]{1,0:T(8,128)(2,1)}, u32[]{:S(2)}, u32[]{:S(2)}) collective-permute-start(bf16[384,2048]{1,0:T(8,128)(2,1)} %get-tuple-element.450.refs_0_), channel_id=1, source_target_pairs={{0,1},{1,0},{2,3},{3,2},{4,5},{5,4},{6,7},{7,6},{8,9},{9,8},{10,11... | collective-permute-start | bytes 4718600 | tf_op jit(solution)/shard_map/ppermute | solution.py:31
  572.0 247.9 %reduce-scatter.8.cloned.1.call-start = ((), (), s32[]{:S(2)}) async-start(), calls=%async_computation.7 | async-start | bytes 6488064 | tf_op jit(solution)/shard_map/reduce_scatter | solution.py:937
  608.7 36.7 %collective-permute-start.42 = (bf16[384,2048]{1,0:T(8,128)(2,1)S(1)}, bf16[384,2048]{1,0:T(8,128)(2,1)}, u32[]{:S(2)}, u32[]{:S(2)}) collective-permute-start(bf16[384,2048]{1,0:T(8,128)(2,1)S(1)} %copy-done.52), channel_id=1, source_target_pairs={{0,2},{1,3},{2,0},{3,1},{4,6},{5,7},{6,4},{7,5},{8,10},{9,11},{10,... | collective-permute-start | bytes 4718600 | tf_op jit(solution)/shard_map/ppermute | solution.py:31
  647.4 85.3 %collective-permute-start.46 = (bf16[384,2048]{1,0:T(8,128)(2,1)}, bf16[384,2048]{1,0:T(8,128)(2,1)S(1)}, u32[]{:S(2)}, u32[]{:S(2)}) collective-permute-start(bf16[384,2048]{1,0:T(8,128)(2,1)} %get-tuple-element.467), channel_id=1, source_target_pairs={{0,2},{1,3},{2,0},{3,1},{4,6},{5,7},{6,4},{7,5},{8,10},{9,11},{10,... | collective-permute-start | bytes 4718600 | tf_op jit(solution)/shard_map/ppermute | solution.py:31
  647.9 84.7 %collective-permute-start.47 = (bf16[384,2048]{1,0:T(8,128)(2,1)}, bf16[384,2048]{1,0:T(8,128)(2,1)S(1)}, u32[]{:S(2)}, u32[]{:S(2)}) collective-permute-start(bf16[384,2048]{1,0:T(8,128)(2,1)} %get-tuple-element.468), channel_id=1, source_target_pairs={{0,2},{1,3},{2,0},{3,1},{4,6},{5,7},{6,4},{7,5},{8,10},{9,11},{10,... | collective-permute-start | bytes 4718600 | tf_op jit(solution)/shard_map/ppermute | solution.py:31
  697.6 35.6 %collective-permute-start.45 = (bf16[4,256,512]{2,1,0:T(8,128)(2,1)}, bf16[4,256,512]{2,1,0:T(8,128)(2,1)S(1)}, u32[]{:S(2)}, u32[]{:S(2)}) collective-permute-start(bf16[4,256,512]{2,1,0:T(8,128)(2,1)} %get-tuple-element.461), channel_id=1, source_target_pairs={{0,4},{4,0},{8,12},{12,8},{16,20},{20,16},{24,28},{28,24},{1,5},{5... | collective-permute-start | bytes 3145736 | tf_op jit(solution)/shard_map/ppermute | solution.py:31
  733.3 39.2 %collective-permute-start.49 = (bf16[4,256,512]{2,1,0:T(8,128)(2,1)}, bf16[4,256,512]{2,1,0:T(8,128)(2,1)}, u32[]{:S(2)}, u32[]{:S(2)}) collective-permute-start(bf16[4,256,512]{2,1,0:T(8,128)(2,1)} %get-tuple-element.469), channel_id=1, source_target_pairs={{0,4},{4,0},{8,12},{12,8},{16,20},{20,16},{24,28},{28,24},{1,5},{5... | collective-permute-start | bytes 3145736 | tf_op jit(solution)/shard_map/ppermute | solution.py:31
  733.6 38.8 %collective-permute-start.48 = (bf16[768,2048]{1,0:T(8,128)(2,1)}, bf16[768,2048]{1,0:T(8,128)(2,1)}, u32[]{:S(2)}, u32[]{:S(2)}) collective-permute-start(bf16[768,2048]{1,0:T(8,128)(2,1)} %convolution_convert_fusion.2), channel_id=1, source_target_pairs={{0,1},{1,0},{2,3},{3,2},{4,5},{5,4},{6,7},{7,6},{8,9},{9,8},{10,11... | collective-permute-start | bytes 9437192 | tf_op jit(solution)/shard_map/ppermute | solution.py:31
  772.4 41.9 %collective-permute-start.53 = (bf16[4,256,512]{2,1,0:T(8,128)(2,1)S(1)}, bf16[4,256,512]{2,1,0:T(8,128)(2,1)}, u32[]{:S(2)}, u32[]{:S(2)}) collective-permute-start(bf16[4,256,512]{2,1,0:T(8,128)(2,1)S(1)} %copy-done.109), channel_id=1, source_target_pairs={{0,4},{4,0},{8,12},{12,8},{16,20},{20,16},{24,28},{28,24},{1,5},{5... | collective-permute-start | bytes 3145736 | tf_op jit(solution)/shard_map/ppermute | solution.py:31
  776.4 37.8 %collective-permute-start.54 = (bf16[2,256,512]{2,1,0:T(8,128)(2,1)S(1)}, bf16[2,256,512]{2,1,0:T(8,128)(2,1)S(1)}, u32[]{:S(2)}, u32[]{:S(2)}) collective-permute-start(bf16[2,256,512]{2,1,0:T(8,128)(2,1)S(1)} %get-tuple-element.626), channel_id=1, source_target_pairs={{0,8},{4,12},{8,0},{12,4},{16,24},{20,28},{24,16},{28,20},{1,9},{5... | collective-permute-start | bytes 1572872 | tf_op jit(solution)/shard_map/ppermute | solution.py:31
  819.9 38.3 %collective-permute-start.56 = (bf16[384,2048]{1,0:T(8,128)(2,1)}, bf16[384,2048]{1,0:T(8,128)(2,1)S(1)}, u32[]{:S(2)}, u32[]{:S(2)}) collective-permute-start(bf16[384,2048]{1,0:T(8,128)(2,1)} %get-tuple-element.501), channel_id=1, source_target_pairs={{0,2},{1,3},{2,0},{3,1},{4,6},{5,7},{6,4},{7,5},{8,10},{9,11},{10,... | collective-permute-start | bytes 4718600 | tf_op jit(solution)/shard_map/ppermute | solution.py:31
  (154 other events, 2208.4 us)
Sparse Core Ops, SparseCore 0:
  123.6 166.7 all-gather.2
  314.6 93.1 all-gather.4
  416.9 111.4 reduce-scatter.3
  572.1 110.6 reduce-scatter.5
  686.3 133.5 reduce-scatter.7

commit v5 on v4

--- a/solution.py
+++ b/solution.py
@@ -690,10 +690,11 @@
     weights = [mix_in[0], mix_in[1], mix_in[2], mix_out, ffn_in[0], ffn_in[1], ffn_out]
 
     own_mix_in = jnp.concatenate([mix_in[k] for k in range(3)], axis=1).astype(BF)
+    own_mix_in, own_tokens = lax.optimization_barrier((own_mix_in, tokens))
     halves, scales_one = [], []
     for i in range(2):
-        half = tokens[i * (rows // 2) : (i + 1) * (rows // 2)]
-        unit_i, scale_i = unit(after(half, own_mix_in).astype(F32))
+        half = own_tokens[i * (rows // 2) : (i + 1) * (rows // 2)]
+        unit_i, scale_i = unit(half.astype(F32))
         halves.append((unit_i * gains[0]).astype(BF))
         scales_one.append(scale_i)
     scale_one = jnp.concatenate(scales_one, axis=0)

time: 942 us -> 940 us (level)
    unnamed x224 -> x236, local copies, waits for them, and re-layouts: 20.5 us -> 22.6 us
  transfers between devices with their start and end apart: 75 -> 75, of which waited for: 38 -> 39; matrix products, arithmetic and copies ran while one was open for 19% -> 19% of each run, Pallas kernels for 43% -> 44%
where the time goes in v5:
time: 940 us; the launch traced here: 933 us
  Pallas kernels  415 us (44%)
  waiting for transfers between devices  227 us (24%)
  other arithmetic  84.6 us (9%)
  matrix products  70 us (7%)
  starting transfers between devices  60.8 us (6%)
  local copies, waits for them, and re-layouts  60.5 us (6%)
  between operations  15.3 us (2%)
    ppermute x70, waiting for transfers between devices, exchange(): return lax.ppermute(value, axis, [(i, i ^ offset) for i in range(size)])  210 us
    pallas_call x7, Pallas kernels, row_tiles(): pl.pallas_call(body, grid=(count,), in_specs=[pl.BlockSpec(memory_space=p...  143 us
    pallas_call x3, Pallas kernels, grad_kernel(): pl.pallas_call(kernel, grid=(steps,), in_specs=in_specs, out_specs=pl.Blo...  79.9 us
    dot_general x8, matrix products, mm_nt(): lax.dot_general(a, b, (((1,), (1,)), ((), ())), preferred_element_type=F32)  70 us
    ppermute x70, starting transfers between devices, exchange(): return lax.ppermute(value, axis, [(i, i ^ offset) for i in range(size)])  60.6 us
    pallas_call x6, Pallas kernels, near_added(): pl.pallas_call(by_rows, grid=(2,), in_specs=[rowed(operand), pl.BlockSpec...  59.7 us
    pallas_call x4, Pallas kernels, grad_kernel(): pl.pallas_call(kernel_by_place, grid_spec=pltpu.PrefetchScalarGridSpec(nu...  59.1 us
    pallas_call x2, Pallas kernels, recurrence_call(): pl.pallas_call(kernel, grid_spec=pltpu.PrefetchScalarGridSpec(num_scalar_...  33.2 us
  transfers between devices with their start and end apart: 75, of which 39 were waited for; matrix products, arithmetic and copies ran while one was open for 19% of the time, Pallas kernels for 44%

profile of v5, /device:TPU:0, one launch (start us, length us, event | category | flops | bytes accessed | tf_op | source)
XLA Modules:
  0.0 933.1 jit_solution(9875884776552210092)
XLA Ops:
  20.7 13.4 %collective-permute-done.1 = bf16[256,1536]{1,0:T(8,128)(2,1)S(1)} collective-permute-done((bf16[256,1536]{1,0:T(8,128)(2,1)S(1)}, bf16[256,1536]{1,0:T(8,128)(2,1)S(1)}, u32[]{:S(2)}, u32[]{:S(2)}) %collective-permute-start.1) | collective-permute-done | bytes 786464 | tf_op jit(solution)/shard_map/ppermute | solution.py:31
  36.2 18.1 %collective-permute-done.3 = bf16[256,1536]{1,0:T(8,128)(2,1)S(1)} collective-permute-done((bf16[256,1536]{1,0:T(8,128)(2,1)S(1)}, bf16[256,1536]{1,0:T(8,128)(2,1)S(1)}, u32[]{:S(2)}, u32[]{:S(2)}) %collective-permute-start.3) | collective-permute-done | bytes 786464 | tf_op jit(solution)/shard_map/ppermute | solution.py:31
  67.3 13.7 %collective-permute-done.5 = bf16[256,1536]{1,0:T(8,128)(2,1)} collective-permute-done((bf16[256,1536]{1,0:T(8,128)(2,1)}, bf16[256,1536]{1,0:T(8,128)(2,1)}, u32[]{:S(2)}, u32[]{:S(2)}) %collective-permute-start.5) | collective-permute-done | bytes 786464 | tf_op jit(solution)/shard_map/ppermute | solution.py:31
  81.1 16.3 %collective-permute-done.6 = bf16[256,1536]{1,0:T(8,128)(2,1)} collective-permute-done((bf16[256,1536]{1,0:T(8,128)(2,1)}, bf16[256,1536]{1,0:T(8,128)(2,1)}, u32[]{:S(2)}, u32[]{:S(2)}) %collective-permute-start.6) | collective-permute-done | bytes 786464 | tf_op jit(solution)/shard_map/ppermute | solution.py:31
  132.5 30.3 %pre.1 = (f32[3072,512]{1,0:T(8,128)}, f32[3072,512]{1,0:T(8,128)}, bf16[3072,512]{1,0:T(8,128)(2,1)}, bf16[3072,512]{1,0:T(8,128)(2,1)}, bf16[3072,512]{1,0:T(8,128)(2,1)}) custom-call(bf16[384,2048]{1,0:T(8,128)(2,1)} %copy-done.53, bf16[384,2048]{1,0:T(8,128)(2,1)} %get-tuple-element.300.refs_1_.refs_4_, bf16[384,2048]{1,0:T(8,128)(2,1)} %copy-done.105, ...), custom_call_target="tpu_custom_call" | custom-call | flops 34923765760 | bytes 12582912 | tf_op jit(solution)/shard_map/pre/pallas_call | solution.py:253
  164.7 13.5 %recurrence_forward.1 = (f32[4,768,512]{2,1,0:T(8,128)}, bf16[4,384,512]{2,1,0:T(8,128)(2,1)S(1)}, bf16[4,384,512]{2,1,0:T(8,128)(2,1)S(1)}) custom-call(s32[4]{0:T(128)S(1)} %gather_fusion, s32[4]{0:T(128)S(1)} %bitcast_subtract_fusion.offsets, f32[4,768,512]{2,1,0:T(8,128)} %bitcast.213, f32[4,768,512]{2,1,0:T(8,128)} %bitcast.215, ...), custom_call_target="tpu_custom_call" | custom-call | flops 23592960000 | bytes 37748736 | tf_op jit(solution)/shard_map/recurrence_forward/pallas_call | solution.py:547
  206.6 29.4 %collective-permute-done.22 = bf16[384,2048]{1,0:T(8,128)(2,1)} collective-permute-done((bf16[384,2048]{1,0:T(8,128)(2,1)}, bf16[384,2048]{1,0:T(8,128)(2,1)}, u32[]{:S(2)}, u32[]{:S(2)}) %collective-permute-start.22) | collective-permute-done | bytes 1572896 | tf_op jit(solution)/shard_map/ppermute | solution.py:31
  244.4 27.6 %collective-permute-done.23 = bf16[384,2048]{1,0:T(8,128)(2,1)S(1)} collective-permute-done((bf16[384,2048]{1,0:T(8,128)(2,1)}, bf16[384,2048]{1,0:T(8,128)(2,1)S(1)}, u32[]{:S(2)}, u32[]{:S(2)}) %collective-permute-start.23) | collective-permute-done | bytes 1572896 | tf_op jit(solution)/shard_map/ppermute | solution.py:31
  282.7 10.1 %all-gather.3.cloned.1.call-done.refs_4_.w = bf16[2048,2816]{1,0:T(8,128)(2,1)} async-done(((bf16[256,2816]{1,0:T(8,128)(2,1)}), bf16[2048,2816]{1,0:T(8,128)(2,1)}) %all-gather.3.cloned.1.call-update) | async-done | bytes 11534352 | tf_op jit(solution)/shard_map/all_gather | solution.py:773
  292.8 14.6 %collective-permute-done.24.refs_1_ = bf16[384,2048]{1,0:T(8,128)(2,1)} collective-permute-done((bf16[384,2048]{1,0:T(8,128)(2,1)}, bf16[384,2048]{1,0:T(8,128)(2,1)}, u32[]{:S(2)}, u32[]{:S(2)}) %collective-permute-start.24) | collective-permute-done | bytes 1572896 | tf_op jit(solution)/shard_map/ppermute | solution.py:31
  311.1 29.9 %gate_up.2 = (bf16[1536,1408]{1,0:T(8,128)(2,1)}, bf16[1536,1408]{1,0:T(8,128)(2,1)}, bf16[1536,1408]{1,0:T(8,128)(2,1)}) custom-call(bf16[384,2048]{1,0:T(8,128)(2,1)} %multiply_convert_fusion.1.refs_0_, bf16[384,2048]{1,0:T(8,128)(2,1)} %collective-permute-done.24.refs_1_, bf16[384,2048]{1,0:T(8,128)(2,1)} %collective-permute-done.25.refs_2_, ...), custom_call_target="tpu_custom_call" | custom-call | flops 32346783744 | bytes 23068672 | tf_op jit(solution)/shard_map/gate_up/pallas_call | solution.py:253
  350.2 30.5 %gate_up.3 = (bf16[1536,1408]{1,0:T(8,128)(2,1)}, bf16[1536,1408]{1,0:T(8,128)(2,1)}, bf16[1536,1408]{1,0:T(8,128)(2,1)}) custom-call(bf16[384,2048]{1,0:T(8,128)(2,1)} %copy-done.55, bf16[384,2048]{1,0:T(8,128)(2,1)} %collective-permute-done.27.refs_1_.refs_5_, bf16[384,2048]{1,0:T(8,128)(2,1)} %collective-permute-done.28.refs_2_.refs_6_, ...), custom_call_target="tpu_custom_call" | custom-call | flops 32346783744 | bytes 23068672 | tf_op jit(solution)/shard_map/gate_up/pallas_call | solution.py:253
  386.8 25.7 %grad_out.1 = bf16[1408,2048]{1,0:T(8,128)(2,1)} custom-call(bf16[384,2048]{1,0:T(8,128)(2,1)} %get-tuple-element.607.refs_0_, bf16[384,2048]{1,0:T(8,128)(2,1)} %collective-permute-done.16.refs_1_, bf16[384,2048]{1,0:T(8,128)(2,1)} %collective-permute-done.18.refs_2_, bf16[384,2048]{1,0:T(8,128)(2,1)} %copy-done.107, ...), custom_call_target="tpu_custom_call" | custom-call | flops 32346783744 | bytes 5767168 | tf_op jit(solution)/shard_map/grad_out/pallas_call | solution.py:371
  412.6 17.8 %gate_up_back.2.v.refs_8_ = bf16[1536,2816]{1,0:T(8,128)(2,1)} custom-call(bf16[384,2048]{1,0:T(8,128)(2,1)} %get-tuple-element.607.refs_0_, bf16[384,2048]{1,0:T(8,128)(2,1)} %collective-permute-done.16.refs_1_, bf16[384,2048]{1,0:T(8,128)(2,1)} %collective-permute-done.18.refs_2_, bf16[384,2048]{1,0:T(8,128)(2,1)} %copy-done.107, ...), custom_call_target="tpu_custom_call" | custom-call | flops 18173392896 | bytes 11534336 | tf_op jit(solution)/shard_map/gate_up_back/pallas_call | solution.py:253
  430.4 13.3 %fusion.10 = bf16[768,2048]{1,0:T(8,128)(2,1)S(1)} fusion(bf16[2048,2816]{1,0:T(8,128)(2,1)} %all-gather.3.cloned.1.call-done.refs_4_.w, bf16[1536,2816]{1,0:T(8,128)(2,1)} %gate_up_back.2.v.refs_8_), kind=kOutput, calls=%fused_computation.22 | convolution fusion | flops 8859942912 | bytes 19005440 | tf_op jit(solution)/shard_map/dot_general | solution.py:43
  444.0 17.5 %gate_up_back.3.v.refs_9_ = bf16[1536,2816]{1,0:T(8,128)(2,1)} custom-call(bf16[384,2048]{1,0:T(8,128)(2,1)} %get-tuple-element.378.refs_4_.refs_0_, bf16[384,2048]{1,0:T(8,128)(2,1)} %copy-done.112, bf16[384,2048]{1,0:T(8,128)(2,1)} %copy-done.113, bf16[384,2048]{1,0:T(8,128)(2,1)} %copy-done.114, ...), custom_call_target="tpu_custom_call" | custom-call | flops 18173392896 | bytes 11534336 | tf_op jit(solution)/shard_map/gate_up_back/pallas_call | solution.py:253
  461.5 14.6 %fusion.13 = bf16[768,2048]{1,0:T(8,128)(2,1)} fusion(bf16[2048,2816]{1,0:T(8,128)(2,1)} %all-gather.3.cloned.1.call-done.refs_4_.w, bf16[1536,2816]{1,0:T(8,128)(2,1)} %gate_up_back.3.v.refs_9_), kind=kOutput, calls=%fused_computation.23 | convolution fusion | flops 8859942912 | bytes 19005440 | tf_op jit(solution)/shard_map/dot_general | solution.py:43
  477.8 15.6 %near_added.10 = (bf16[384,2048]{1,0:T(8,128)(2,1)}, f32[384,2048]{1,0:T(8,128)}) custom-call(bf16[1536,2816]{1,0:T(8,128)(2,1)} %gate_up_back.2.v.refs_8_, bf16[2048,2816]{1,0:T(8,128)(2,1)} %all-gather.3.cloned.1.call-done.refs_4_.w, bf16[768,2048]{1,0:T(8,128)(2,1)} %copy-done.103), custom_call_target="tpu_custom_call" | custom-call | flops 18173392896 | bytes 11534336 | tf_op jit(solution)/shard_map/near_added/pallas_call | solution.py:129
  503.8 9.4 %convolution_convert_fusion.4 = bf16[768,2048]{1,0:T(8,128)(2,1)} fusion(bf16[2048,1408]{1,0:T(8,128)(2,1)} %all-gather.5.cloned.1.call-done.refs_4_.w, bf16[1536,1408]{1,0:T(8,128)(2,1)} %get-tuple-element.435.refs_9_.v), kind=kOutput, calls=%fused_computation.26 | convolution fusion | flops 4430757888 | bytes 11075584 | tf_op jit(solution)/shard_map/dot_general | solution.py:43
  513.2 15.7 %near_added.11 = (bf16[384,2048]{1,0:T(8,128)(2,1)}, f32[384,2048]{1,0:T(8,128)}) custom-call(bf16[1536,2816]{1,0:T(8,128)(2,1)} %gate_up_back.3.v.refs_9_, bf16[2048,2816]{1,0:T(8,128)(2,1)} %all-gather.3.cloned.1.call-done.refs_4_.w, bf16[768,2048]{1,0:T(8,128)(2,1)} %collective-permute-done.34.added), custom_call_target="tpu_custom_call" | custom-call | flops 18173392896 | bytes 11534336 | tf_op jit(solution)/shard_map/near_added/pallas_call | solution.py:129
  537.0 27.0 %grad_in.2 = bf16[2048,1408]{1,0:T(8,128)(2,1)} custom-call(bf16[384,2048]{1,0:T(8,128)(2,1)} %multiply_convert_fusion.1.refs_0_, bf16[384,2048]{1,0:T(8,128)(2,1)} %collective-permute-done.24.refs_1_, bf16[384,2048]{1,0:T(8,128)(2,1)} %collective-permute-done.25.refs_2_, bf16[384,2048]{1,0:T(8,128)(2,1)} %collective-permute-done.26.refs_3_, ...), custom_call_target="tpu_custom_call" | custom-call | flops 32346783744 | bytes 5767168 | tf_op jit(solution)/shard_map/grad_in/pallas_call | solution.py:371
  577.4 27.2 %grad_in.3 = bf16[2048,1408]{1,0:T(8,128)(2,1)} custom-call(bf16[384,2048]{1,0:T(8,128)(2,1)} %multiply_convert_fusion.1.refs_0_, bf16[384,2048]{1,0:T(8,128)(2,1)} %collective-permute-done.24.refs_1_, bf16[384,2048]{1,0:T(8,128)(2,1)} %collective-permute-done.25.refs_2_, bf16[384,2048]{1,0:T(8,128)(2,1)} %collective-permute-done.26.refs_3_, ...), custom_call_target="tpu_custom_call" | custom-call | flops 32346783744 | bytes 5767168 | tf_op jit(solution)/shard_map/grad_in/pallas_call | solution.py:371
  606.5 11.4 %near_added.12 = (bf16[384,2048]{1,0:T(8,128)(2,1)}, f32[384,2048]{1,0:T(8,128)}) custom-call(bf16[1536,1408]{1,0:T(8,128)(2,1)} %get-tuple-element.432.refs_8_.v, bf16[2048,1408]{1,0:T(8,128)(2,1)} %all-gather.5.cloned.1.call-done.refs_4_.w, bf16[768,2048]{1,0:T(8,128)(2,1)} %collective-permute-done.37.n), custom_call_target="tpu_custom_call" | custom-call | flops 11086696448 | bytes 5767168 | tf_op jit(solution)/shard_map/near_added/pallas_call | solution.py:157
  617.9 11.3 %near_added.13 = (bf16[384,2048]{1,0:T(8,128)(2,1)}, f32[384,2048]{1,0:T(8,128)}) custom-call(bf16[1536,1408]{1,0:T(8,128)(2,1)} %get-tuple-element.435.refs_9_.v, bf16[2048,1408]{1,0:T(8,128)(2,1)} %all-gather.5.cloned.1.call-done.refs_4_.w, bf16[768,2048]{1,0:T(8,128)(2,1)} %collective-permute-done.38.n), custom_call_target="tpu_custom_call" | custom-call | flops 11086696448 | bytes 5767168 | tf_op jit(solution)/shard_map/near_added/pallas_call | solution.py:157
  655.7 19.7 %recurrence_backward.1 = (bf16[4,384,1536]{2,1,0:T(8,128)(2,1)}, bf16[4,384,1536]{2,1,0:T(8,128)(2,1)}) custom-call(s32[4]{0:T(128)S(1)} %rev.3.order, s32[4]{0:T(128)S(1)} %copy-done.5, f32[4,768,512]{2,1,0:T(8,128)} %bitcast.214, f32[4,768,512]{2,1,0:T(8,128)} %bitcast.216, bf16[4,768,512]{2,1,0:T(8,128)(2,1)} %bitcast.228, ...), custom_call_target="tpu_custom_call" | custom-call | flops 23592960000 | bytes 37748736 | tf_op jit(solution)/shard_map/recurrence_backward/pallas_call | solution.py:547
  680.1 14.7 %grad_mix_in.3 = (bf16[4,256,512]{2,1,0:T(8,128)(2,1)}, bf16[4,256,512]{2,1,0:T(8,128)(2,1)}) custom-call(s32[8]{0:T(128)} %stack.136.owners_ref, bf16[384,2048]{1,0:T(8,128)(2,1)} %copy-done.53, bf16[384,2048]{1,0:T(8,128)(2,1)} %copy-done.105, bf16[384,2048]{1,0:T(8,128)(2,1)} %copy-done.106, bf16[384,2048]{1,0:T(8,128)(2,1)} %collective-permute-done.10.refs_6_.refs_3_, ...), custom_call_target="tpu_custom_call" | custom-call | flops 14307921920 | bytes 2097152 | tf_op jit(solution)/shard_map/grad_mix_in/pallas_call | solution.py:395
  705.7 14.8 %grad_mix_in.4 = (bf16[4,256,512]{2,1,0:T(8,128)(2,1)}, bf16[4,256,512]{2,1,0:T(8,128)(2,1)}) custom-call(s32[8]{0:T(128)} %stack.136.owners_ref, bf16[384,2048]{1,0:T(8,128)(2,1)} %copy-done.53, bf16[384,2048]{1,0:T(8,128)(2,1)} %copy-done.105, bf16[384,2048]{1,0:T(8,128)(2,1)} %copy-done.106, bf16[384,2048]{1,0:T(8,128)(2,1)} %collective-permute-done.10.refs_6_.refs_3_, ...), custom_call_target="tpu_custom_call" | custom-call | flops 14307921920 | bytes 2097152 | tf_op jit(solution)/shard_map/grad_mix_in/pallas_call | solution.py:395
  733.9 14.7 %grad_mix_in.5 = (bf16[4,256,512]{2,1,0:T(8,128)(2,1)}, bf16[4,256,512]{2,1,0:T(8,128)(2,1)}) custom-call(s32[8]{0:T(128)} %stack.136.owners_ref, bf16[384,2048]{1,0:T(8,128)(2,1)} %copy-done.53, bf16[384,2048]{1,0:T(8,128)(2,1)} %copy-done.105, bf16[384,2048]{1,0:T(8,128)(2,1)} %copy-done.106, bf16[384,2048]{1,0:T(8,128)(2,1)} %collective-permute-done.10.refs_6_.refs_3_, ...), custom_call_target="tpu_custom_call" | custom-call | flops 14307921920 | bytes 2097152 | tf_op jit(solution)/shard_map/grad_mix_in/pallas_call | solution.py:395
  751.5 11.6 %near_added.14 = (bf16[384,2048]{1,0:T(8,128)(2,1)}, f32[384,2048]{1,0:T(8,128)}) custom-call(bf16[1536,1536]{1,0:T(8,128)(2,1)} %bitcast.226, bf16[2048,1536]{1,0:T(8,128)(2,1)} %constant_dynamic-update-slice_fusion.4.refs_8_.w, bf16[768,2048]{1,0:T(8,128)(2,1)} %collective-permute-done.51.n), custom_call_target="tpu_custom_call" | custom-call | flops 11730940928 | bytes 6291456 | tf_op jit(solution)/shard_map/near_added/pallas_call | solution.py:157
  781.2 14.8 %grad_mix_out.1 = (bf16[4,512,256]{2,1,0:T(8,128)(2,1)}, bf16[4,512,256]{2,1,0:T(8,128)(2,1)}) custom-call(s32[8]{0:T(128)} %stack.136.owners_ref, bf16[384,2048]{1,0:T(8,128)(2,1)} %get-tuple-element.450.refs_0_, bf16[384,2048]{1,0:T(8,128)(2,1)} %collective-permute-done.39.refs_1_, bf16[384,2048]{1,0:T(8,128)(2,1)} %collective-permute-done.40.refs_2_, ...), custom_call_target="tpu_custom_call" | custom-call | flops 14307921920 | bytes 2097152 | tf_op jit(solution)/shard_map/grad_mix_out/pallas_call | solution.py:395
  796.1 11.9 %near_added.15 = (bf16[384,2048]{1,0:T(8,128)(2,1)}, f32[384,2048]{1,0:T(8,128)}) custom-call(bf16[1536,1536]{1,0:T(8,128)(2,1)} %bitcast.221, bf16[2048,1536]{1,0:T(8,128)(2,1)} %constant_dynamic-update-slice_fusion.4.refs_8_.w, bf16[768,2048]{1,0:T(8,128)(2,1)} %collective-permute-done.48.n), custom_call_target="tpu_custom_call" | custom-call | flops 11730940928 | bytes 6291456 | tf_op jit(solution)/shard_map/near_added/pallas_call | solution.py:157
  841.2 15.3 %collective-permute-done.57 = bf16[4,512,256]{2,1,0:T(8,128)(2,1)S(1)} collective-permute-done((bf16[4,512,256]{2,1,0:T(8,128)(2,1)}, bf16[4,512,256]{2,1,0:T(8,128)(2,1)S(1)}, u32[]{:S(2)}, u32[]{:S(2)}) %collective-permute-start.57) | collective-permute-done | bytes 1048608 | tf_op jit(solution)/shard_map/ppermute | solution.py:31
  (507 shorter events, 346.2 us)
Async XLA Ops:
  7.2 285.6 %all-gather.3.cloned.1.call-start = ((), (), s32[]{:S(2)}) async-start(), calls=%async_computation.3 | async-start | bytes 12976128 | tf_op jit(solution)/shard_map/all_gather | solution.py:773
  12.1 42.2 %collective-permute-start = (bf16[384,2048]{1,0:T(8,128)(2,1)S(1)}, bf16[384,2048]{1,0:T(8,128)(2,1)S(1)}, u32[]{:S(2)}, u32[]{:S(2)}) collective-permute-start(bf16[384,2048]{1,0:T(8,128)(2,1)S(1)} %get-tuple-element.472.refs_0_), channel_id=1, source_target_pairs={{0,2},{1,3},{2,0},{3,1},{4,6},{5,7},{6,4},{7,5},{8,10},{9,11},{10,... | collective-permute-start | bytes 4718600 | tf_op jit(solution)/shard_map/ppermute | solution.py:31
  18.2 36.1 %collective-permute-start.3 = (bf16[256,1536]{1,0:T(8,128)(2,1)S(1)}, bf16[256,1536]{1,0:T(8,128)(2,1)S(1)}, u32[]{:S(2)}, u32[]{:S(2)}) collective-permute-start(bf16[256,1536]{1,0:T(8,128)(2,1)S(1)} %pad_maximum_fusion.8), channel_id=1, source_target_pairs={{0,24},{4,28},{8,16},{12,20},{16,8},{20,12},{24,0},{28,4},{1,25},{... | collective-permute-start | bytes 2359304 | tf_op jit(solution)/shard_map/ppermute | solution.py:31
  54.5 45.3 %collective-permute-start.4 = (bf16[384,2048]{1,0:T(8,128)(2,1)}, bf16[384,2048]{1,0:T(8,128)(2,1)}, u32[]{:S(2)}, u32[]{:S(2)}) collective-permute-start(bf16[384,2048]{1,0:T(8,128)(2,1)} %get-tuple-element.300.refs_1_.refs_4_), channel_id=1, source_target_pairs={{0,2},{1,3},{2,0},{3,1},{4,6},{5,7},{6,4},{7,5},{8,10},{9,11},{10,... | collective-permute-start | bytes 4718600 | tf_op jit(solution)/shard_map/ppermute | solution.py:31
  59.0 40.7 %collective-permute-start.9 = (bf16[384,2048]{1,0:T(8,128)(2,1)}, bf16[384,2048]{1,0:T(8,128)(2,1)}, u32[]{:S(2)}, u32[]{:S(2)}) collective-permute-start(bf16[384,2048]{1,0:T(8,128)(2,1)} %get-tuple-element.300.refs_1_.refs_4_), channel_id=1, source_target_pairs={{0,1},{1,0},{2,3},{3,2},{4,5},{5,4},{6,7},{7,6},{8,9},{9,8},{10,11... | collective-permute-start | bytes 4718600 | tf_op jit(solution)/shard_map/ppermute | solution.py:31
  60.9 36.5 %collective-permute-start.6 = (bf16[256,1536]{1,0:T(8,128)(2,1)}, bf16[256,1536]{1,0:T(8,128)(2,1)}, u32[]{:S(2)}, u32[]{:S(2)}) collective-permute-start(bf16[256,1536]{1,0:T(8,128)(2,1)} %copy-done.76), channel_id=1, source_target_pairs={{0,4},{4,0},{8,12},{12,8},{16,20},{20,16},{24,28},{28,24},{1,5},{5... | collective-permute-start | bytes 2359304 | tf_op jit(solution)/shard_map/ppermute | solution.py:31
  62.4 37.3 %collective-permute-start.7 = (bf16[256,1536]{1,0:T(8,128)(2,1)}, bf16[256,1536]{1,0:T(8,128)(2,1)}, u32[]{:S(2)}, u32[]{:S(2)}) collective-permute-start(bf16[256,1536]{1,0:T(8,128)(2,1)} %copy-done.35), channel_id=1, source_target_pairs={{0,16},{4,20},{8,24},{12,28},{16,0},{20,4},{24,8},{28,12},{1,17},{... | collective-permute-start | bytes 2359304 | tf_op jit(solution)/shard_map/ppermute | solution.py:31
  124.4 288.2 %all-gather.5.cloned.1.call-start = ((), (), s32[]{:S(2)}) async-start(), calls=%async_computation.4 | async-start | bytes 6488064 | tf_op jit(solution)/shard_map/all_gather | solution.py:845
  130.0 51.6 %collective-permute-start.18 = (bf16[384,2048]{1,0:T(8,128)(2,1)}, bf16[384,2048]{1,0:T(8,128)(2,1)}, u32[]{:S(2)}, u32[]{:S(2)}) collective-permute-start(bf16[384,2048]{1,0:T(8,128)(2,1)} %get-tuple-element.607.refs_0_), channel_id=1, source_target_pairs={{0,1},{1,0},{2,3},{3,2},{4,5},{5,4},{6,7},{7,6},{8,9},{9,8},{10,11... | collective-permute-start | bytes 4718600 | tf_op jit(solution)/shard_map/ppermute | solution.py:31
  132.0 47.6 %collective-permute-start.17 = (bf16[1024,512]{1,0:T(8,128)(2,1)}, bf16[1024,512]{1,0:T(8,128)(2,1)S(1)}, u32[]{:S(2)}, u32[]{:S(2)}) collective-permute-start(bf16[1024,512]{1,0:T(8,128)(2,1)} %pad_maximum_fusion.7), channel_id=1, source_target_pairs={{0,4},{4,0},{8,12},{12,8},{16,20},{20,16},{24,28},{28,24},{1,5},{5... | collective-permute-start | bytes 3145736 | tf_op jit(solution)/shard_map/ppermute | solution.py:31
  198.9 37.0 %collective-permute-start.22 = (bf16[384,2048]{1,0:T(8,128)(2,1)}, bf16[384,2048]{1,0:T(8,128)(2,1)}, u32[]{:S(2)}, u32[]{:S(2)}) collective-permute-start(bf16[384,2048]{1,0:T(8,128)(2,1)} %get-tuple-element.351), channel_id=1, source_target_pairs={{0,2},{1,3},{2,0},{3,1},{4,6},{5,7},{6,4},{7,5},{8,10},{9,11},{10,... | collective-permute-start | bytes 4718600 | tf_op jit(solution)/shard_map/ppermute | solution.py:31
  235.9 36.1 %collective-permute-start.23 = (bf16[384,2048]{1,0:T(8,128)(2,1)}, bf16[384,2048]{1,0:T(8,128)(2,1)S(1)}, u32[]{:S(2)}, u32[]{:S(2)}) collective-permute-start(bf16[384,2048]{1,0:T(8,128)(2,1)} %get-tuple-element.356), channel_id=1, source_target_pairs={{0,2},{1,3},{2,0},{3,1},{4,6},{5,7},{6,4},{7,5},{8,10},{9,11},{10,... | collective-permute-start | bytes 4718600 | tf_op jit(solution)/shard_map/ppermute | solution.py:31
  308.5 36.9 %collective-permute-start.27 = (bf16[384,2048]{1,0:T(8,128)(2,1)S(1)}, bf16[384,2048]{1,0:T(8,128)(2,1)}, u32[]{:S(2)}, u32[]{:S(2)}) collective-permute-start(bf16[384,2048]{1,0:T(8,128)(2,1)S(1)} %multiply_convert_fusion.refs_0_.refs_4_), channel_id=1, source_target_pairs={{0,2},{1,3},{2,0},{3,1},{4,6},{5,7},{6,4},{7,5},{8,10},{9,11},{10,... | collective-permute-start | bytes 4718600 | tf_op jit(solution)/shard_map/ppermute | solution.py:31
  309.2 36.2 %collective-permute-start.28 = (bf16[384,2048]{1,0:T(8,128)(2,1)S(1)}, bf16[384,2048]{1,0:T(8,128)(2,1)}, u32[]{:S(2)}, u32[]{:S(2)}) collective-permute-start(bf16[384,2048]{1,0:T(8,128)(2,1)S(1)} %multiply_convert_fusion.refs_0_.refs_4_), channel_id=1, source_target_pairs={{0,1},{1,0},{2,3},{3,2},{4,5},{5,4},{6,7},{7,6},{8,9},{9,8},{10,11... | collective-permute-start | bytes 4718600 | tf_op jit(solution)/shard_map/ppermute | solution.py:31
  309.5 254.5 %reduce-scatter.4.cloned.1.call-start = ((), (), s32[]{:S(2)}) async-start(), calls=%async_computation.5 | async-start | bytes 6488064 | tf_op jit(solution)/shard_map/reduce_scatter | solution.py:911
  345.4 36.8 %collective-permute-start.30 = (bf16[384,2048]{1,0:T(8,128)(2,1)S(1)}, bf16[384,2048]{1,0:T(8,128)(2,1)S(1)}, u32[]{:S(2)}, u32[]{:S(2)}) collective-permute-start(bf16[384,2048]{1,0:T(8,128)(2,1)S(1)} %copy-done.54), channel_id=1, source_target_pairs={{0,2},{1,3},{2,0},{3,1},{4,6},{5,7},{6,4},{7,5},{8,10},{9,11},{10,... | collective-permute-start | bytes 4718600 | tf_op jit(solution)/shard_map/ppermute | solution.py:31
  346.2 36.0 %collective-permute-start.31 = (bf16[384,2048]{1,0:T(8,128)(2,1)S(1)}, bf16[384,2048]{1,0:T(8,128)(2,1)S(1)}, u32[]{:S(2)}, u32[]{:S(2)}) collective-permute-start(bf16[384,2048]{1,0:T(8,128)(2,1)S(1)} %copy-done.54), channel_id=1, source_target_pairs={{0,1},{1,0},{2,3},{3,2},{4,5},{5,4},{6,7},{7,6},{8,9},{9,8},{10,11... | collective-permute-start | bytes 4718600 | tf_op jit(solution)/shard_map/ppermute | solution.py:31
  412.6 267.5 %reduce-scatter.6.cloned.1.call-start = ((), (), s32[]{:S(2)}) async-start(), calls=%async_computation.6 | async-start | bytes 6488064 | tf_op jit(solution)/shard_map/reduce_scatter | solution.py:938
  493.9 36.7 %collective-permute-start.35 = (bf16[384,2048]{1,0:T(8,128)(2,1)}, bf16[384,2048]{1,0:T(8,128)(2,1)S(1)}, u32[]{:S(2)}, u32[]{:S(2)}) collective-permute-start(bf16[384,2048]{1,0:T(8,128)(2,1)} %get-tuple-element.403), channel_id=1, source_target_pairs={{0,2},{1,3},{2,0},{3,1},{4,6},{5,7},{6,4},{7,5},{8,10},{9,11},{10,... | collective-permute-start | bytes 4718600 | tf_op jit(solution)/shard_map/ppermute | solution.py:31
  530.5 35.9 %collective-permute-start.36 = (bf16[384,2048]{1,0:T(8,128)(2,1)}, bf16[384,2048]{1,0:T(8,128)(2,1)}, u32[]{:S(2)}, u32[]{:S(2)}) collective-permute-start(bf16[384,2048]{1,0:T(8,128)(2,1)} %get-tuple-element.411), channel_id=1, source_target_pairs={{0,2},{1,3},{2,0},{3,1},{4,6},{5,7},{6,4},{7,5},{8,10},{9,11},{10,... | collective-permute-start | bytes 4718600 | tf_op jit(solution)/shard_map/ppermute | solution.py:31
  566.5 38.2 %collective-permute-start.39 = (bf16[384,2048]{1,0:T(8,128)(2,1)}, bf16[384,2048]{1,0:T(8,128)(2,1)}, u32[]{:S(2)}, u32[]{:S(2)}) collective-permute-start(bf16[384,2048]{1,0:T(8,128)(2,1)} %get-tuple-element.450.refs_0_), channel_id=1, source_target_pairs={{0,2},{1,3},{2,0},{3,1},{4,6},{5,7},{6,4},{7,5},{8,10},{9,11},{10,... | collective-permute-start | bytes 4718600 | tf_op jit(solution)/shard_map/ppermute | solution.py:31
  567.4 61.9 %collective-permute-start.40 = (bf16[384,2048]{1,0:T(8,128)(2,1)}, bf16[384,2048]{1,0:T(8,128)(2,1)}, u32[]{:S(2)}, u32[]{:S(2)}) collective-permute-start(bf16[384,2048]{1,0:T(8,128)(2,1)} %get-tuple-element.450.refs_0_), channel_id=1, source_target_pairs={{0,1},{1,0},{2,3},{3,2},{4,5},{5,4},{6,7},{7,6},{8,9},{9,8},{10,11... | collective-permute-start | bytes 4718600 | tf_op jit(solution)/shard_map/ppermute | solution.py:31
  567.4 249.7 %reduce-scatter.8.cloned.1.call-start = ((), (), s32[]{:S(2)}) async-start(), calls=%async_computation.7 | async-start | bytes 6488064 | tf_op jit(solution)/shard_map/reduce_scatter | solution.py:938
  604.6 36.3 %collective-permute-start.42 = (bf16[384,2048]{1,0:T(8,128)(2,1)S(1)}, bf16[384,2048]{1,0:T(8,128)(2,1)}, u32[]{:S(2)}, u32[]{:S(2)}) collective-permute-start(bf16[384,2048]{1,0:T(8,128)(2,1)S(1)} %copy-done.52), channel_id=1, source_target_pairs={{0,2},{1,3},{2,0},{3,1},{4,6},{5,7},{6,4},{7,5},{8,10},{9,11},{10,... | collective-permute-start | bytes 4718600 | tf_op jit(solution)/shard_map/ppermute | solution.py:31
  642.8 87.1 %collective-permute-start.46 = (bf16[384,2048]{1,0:T(8,128)(2,1)}, bf16[384,2048]{1,0:T(8,128)(2,1)S(1)}, u32[]{:S(2)}, u32[]{:S(2)}) collective-permute-start(bf16[384,2048]{1,0:T(8,128)(2,1)} %get-tuple-element.467), channel_id=1, source_target_pairs={{0,2},{1,3},{2,0},{3,1},{4,6},{5,7},{6,4},{7,5},{8,10},{9,11},{10,... | collective-permute-start | bytes 4718600 | tf_op jit(solution)/shard_map/ppermute | solution.py:31
  644.3 85.7 %collective-permute-start.47 = (bf16[384,2048]{1,0:T(8,128)(2,1)}, bf16[384,2048]{1,0:T(8,128)(2,1)S(1)}, u32[]{:S(2)}, u32[]{:S(2)}) collective-permute-start(bf16[384,2048]{1,0:T(8,128)(2,1)} %get-tuple-element.468), channel_id=1, source_target_pairs={{0,2},{1,3},{2,0},{3,1},{4,6},{5,7},{6,4},{7,5},{8,10},{9,11},{10,... | collective-permute-start | bytes 4718600 | tf_op jit(solution)/shard_map/ppermute | solution.py:31
  694.8 35.6 %collective-permute-start.45 = (bf16[4,256,512]{2,1,0:T(8,128)(2,1)}, bf16[4,256,512]{2,1,0:T(8,128)(2,1)S(1)}, u32[]{:S(2)}, u32[]{:S(2)}) collective-permute-start(bf16[4,256,512]{2,1,0:T(8,128)(2,1)} %get-tuple-element.461), channel_id=1, source_target_pairs={{0,4},{4,0},{8,12},{12,8},{16,20},{20,16},{24,28},{28,24},{1,5},{5... | collective-permute-start | bytes 3145736 | tf_op jit(solution)/shard_map/ppermute | solution.py:31
  730.4 39.1 %collective-permute-start.49 = (bf16[4,256,512]{2,1,0:T(8,128)(2,1)}, bf16[4,256,512]{2,1,0:T(8,128)(2,1)}, u32[]{:S(2)}, u32[]{:S(2)}) collective-permute-start(bf16[4,256,512]{2,1,0:T(8,128)(2,1)} %get-tuple-element.469), channel_id=1, source_target_pairs={{0,4},{4,0},{8,12},{12,8},{16,20},{20,16},{24,28},{28,24},{1,5},{5... | collective-permute-start | bytes 3145736 | tf_op jit(solution)/shard_map/ppermute | solution.py:31
  730.8 38.7 %collective-permute-start.48 = (bf16[768,2048]{1,0:T(8,128)(2,1)}, bf16[768,2048]{1,0:T(8,128)(2,1)}, u32[]{:S(2)}, u32[]{:S(2)}) collective-permute-start(bf16[768,2048]{1,0:T(8,128)(2,1)} %convolution_convert_fusion.2), channel_id=1, source_target_pairs={{0,1},{1,0},{2,3},{3,2},{4,5},{5,4},{6,7},{7,6},{8,9},{9,8},{10,11... | collective-permute-start | bytes 9437192 | tf_op jit(solution)/shard_map/ppermute | solution.py:31
  769.6 43.1 %collective-permute-start.53 = (bf16[4,256,512]{2,1,0:T(8,128)(2,1)S(1)}, bf16[4,256,512]{2,1,0:T(8,128)(2,1)}, u32[]{:S(2)}, u32[]{:S(2)}) collective-permute-start(bf16[4,256,512]{2,1,0:T(8,128)(2,1)S(1)} %copy-done.115), channel_id=1, source_target_pairs={{0,4},{4,0},{8,12},{12,8},{16,20},{20,16},{24,28},{28,24},{1,5},{5... | collective-permute-start | bytes 3145736 | tf_op jit(solution)/shard_map/ppermute | solution.py:31
  773.6 39.1 %collective-permute-start.54 = (bf16[2,256,512]{2,1,0:T(8,128)(2,1)S(1)}, bf16[2,256,512]{2,1,0:T(8,128)(2,1)S(1)}, u32[]{:S(2)}, u32[]{:S(2)}) collective-permute-start(bf16[2,256,512]{2,1,0:T(8,128)(2,1)S(1)} %get-tuple-element.628), channel_id=1, source_target_pairs={{0,8},{4,12},{8,0},{12,4},{16,24},{20,28},{24,16},{28,20},{1,9},{5... | collective-permute-start | bytes 1572872 | tf_op jit(solution)/shard_map/ppermute | solution.py:31
  817.1 39.4 %collective-permute-start.56 = (bf16[384,2048]{1,0:T(8,128)(2,1)}, bf16[384,2048]{1,0:T(8,128)(2,1)S(1)}, u32[]{:S(2)}, u32[]{:S(2)}) collective-permute-start(bf16[384,2048]{1,0:T(8,128)(2,1)} %get-tuple-element.501), channel_id=1, source_target_pairs={{0,2},{1,3},{2,0},{3,1},{4,6},{5,7},{6,4},{7,5},{8,10},{9,11},{10,... | collective-permute-start | bytes 4718600 | tf_op jit(solution)/shard_map/ppermute | solution.py:31
  (160 other events, 2189.4 us)
Sparse Core Ops, SparseCore 0:
  124.5 168.2 all-gather.2
  309.6 95.3 all-gather.4
  412.7 112.4 reduce-scatter.3
  567.5 112.4 reduce-scatter.5
  683.5 133.5 reduce-scatter.7
